TPU v7x, 32 devices: a whole 2x2x4 slice. The times are simulated.
32 devices in a mesh: dp: 4 (over y, x), ctx: 4 (over z), tensor: 2 (over core).
Axes of the slice: x: 2, y: 2, z: 4, core: 2. Of those that a mesh axis runs over, the one named last changes fastest.
Arguments:
- inputs: bfloat16 [2048, 2304], P(('dp', 'ctx')), may hold values from -6 to 6
- cotangent: bfloat16 [2048, 2304], P(('dp', 'ctx')), may hold values from -6 to 6
- lengths: int32 [4], replicated, may hold values from 256 to 512
- dealing: int32 [4], replicated, may hold values from 0 to 3, each once
- span_table: int32 [4, 8], replicated, may hold values from 0 to 7, as said below
- prenorm_gain: bfloat16 [2, 2304], P(None, ('dp', 'ctx')), may hold values from 0.5 to 1.5
- query_weight: bfloat16 [2, 2304, 2304], P(None, ('dp', 'ctx'), 'tensor'), may hold values from -0.125 to 0.125
- keys_weight: bfloat16 [2, 2304, 2304], P(None, ('dp', 'ctx'), 'tensor'), may hold values from -0.125 to 0.125
- values_weight: bfloat16 [2, 2304, 2304], P(None, ('dp', 'ctx'), 'tensor'), may hold values from -0.125 to 0.125
- project_weight: bfloat16 [2, 2304, 2304], P(None, 'tensor', ('dp', 'ctx')), may hold values from -2.5 to 2.5
- postnorm_gain: bfloat16 [2, 2304], P(None, ('dp', 'ctx')), may hold values from 0.5 to 1.5
- gating_weight: bfloat16 [2, 2304, 5760], P(None, ('dp', 'ctx'), 'tensor'), may hold values from -0.125 to 0.125
- upward_weight: bfloat16 [2, 2304, 5760], P(None, ('dp', 'ctx'), 'tensor'), may hold values from -0.125 to 0.125
- downward_weight: bfloat16 [2, 5760, 2304], P(None, 'tensor', ('dp', 'ctx')), may hold values from -0.5 to 0.5
Outputs:
- output: bfloat16 [2048, 2304], P(('dp', 'ctx'))
- grad_inputs: float32 [2048, 2304], P(('dp', 'ctx'))
- grad_prenorm: float32 [2, 2304], P(None, ('dp', 'ctx'))
- grad_query: float32 [2, 2304, 2304], P(None, ('dp', 'ctx'), 'tensor')
- grad_keys: float32 [2, 2304, 2304], P(None, ('dp', 'ctx'), 'tensor')
- grad_values: float32 [2, 2304, 2304], P(None, ('dp', 'ctx'), 'tensor')
- grad_project: float32 [2, 2304, 2304], P(None, 'tensor', ('dp', 'ctx'))
- grad_postnorm: float32 [2, 2304], P(None, ('dp', 'ctx'))
- grad_gating: float32 [2, 2304, 5760], P(None, ('dp', 'ctx'), 'tensor')
- grad_upward: float32 [2, 2304, 5760], P(None, ('dp', 'ctx'), 'tensor')
- grad_downward: float32 [2, 5760, 2304], P(None, 'tensor', ('dp', 'ctx'))
Inputs may be any that keep to these rules, and one draw needn't show every extreme that they name: For each group g and each index c of ctx, span_table[g, 2 c] and span_table[g, 2 c + 1] are some j and 7 - j, in either order; every j below 4 appears once in a group.
All inputs are finite; a program needn't handle non-finite values.
Results may differ from a plain program's by a relative error of at most 0.035.
Values may be sent and summed in bfloat16 or wider, within the bound.
A program may use at most 448 MiB of HBM per device.

v0:
```python
import math

import jax
import jax.numpy as jnp
from jax import lax
from jax.sharding import PartitionSpec as P

HEAD_DIM = 64
LAYERS = 2
BLOCK = 128


eps_norm = 1e-05
depth_scale = 1.4 / math.sqrt(40.0)
rope_base = 10000.0
masked_score = -1e30


def times_transposed(left, right):
    return lax.dot_general(
        left, right, (((1,), (1,)), ((), ())), preferred_element_type=jnp.float32
    )


def outer_rows(left, right):
    return lax.dot_general(
        left, right, (((0,), (0,)), ((), ())), preferred_element_type=jnp.float32
    )


def rms_parts(values):
    inverse = lax.rsqrt(jnp.mean(values * values, axis=-1, keepdims=True) + eps_norm)
    return (values * inverse, inverse)


def norm_backward(values, gain, grad_normed):
    scaled, inverse = rms_parts(values)
    gain_grad = jnp.sum(grad_normed * scaled, axis=0)
    grad_scaled = grad_normed * gain.astype(jnp.float32)
    return (
        gain_grad,
        inverse * (grad_scaled - scaled * jnp.mean(grad_scaled * scaled, axis=-1, keepdims=True)),
    )


def rope_tables(position, half_dim):
    inverse = rope_base ** (-jnp.arange(half_dim).astype(jnp.float32) / half_dim)
    angles = position.astype(jnp.float32)[:, None] * inverse[None, :]
    return (jnp.cos(angles)[:, None, :], jnp.sin(angles)[:, None, :])


def rotate(values, tables, direction):
    cosine, sine_table = tables
    half_dim = values.shape[-1] // 2
    front_half = values[..., :half_dim]
    back_half = values[..., half_dim:]
    return jnp.concatenate(
        [
            front_half * cosine - direction * back_half * sine_table,
            back_half * cosine + direction * front_half * sine_table,
        ],
        axis=-1,
    )


def group_layout(lengths, dealing, group_index, seq_count):
    chosen = lax.dynamic_slice_in_dim(dealing, group_index * seq_count, seq_count)
    matches = chosen[:, None] == jnp.arange(lengths.shape[0], dtype=jnp.int32)[None, :]
    seq_lens = jnp.sum(jnp.where(matches, lengths[None, :], 0), axis=1)
    padded = (seq_lens + BLOCK - 1) // BLOCK * BLOCK
    starts = jnp.cumsum(padded) - padded
    return (starts, seq_lens)


def slots_for(first_row, number, span_row, half_span):
    global_rows = first_row + jnp.arange(number, dtype=jnp.int32)
    matches = (global_rows // half_span)[:, None] == jnp.arange(span_row.shape[0], dtype=jnp.int32)[
        None, :
    ]
    span_of = jnp.sum(jnp.where(matches, span_row[None, :], 0), axis=1)
    return span_of * half_span + global_rows % half_span


def slot_facts(slots, starts, seq_lens):
    member = jnp.sum((slots[:, None] >= starts[None, :]).astype(jnp.int32), axis=1) - 1
    matches = member[:, None] == jnp.arange(starts.shape[0], dtype=jnp.int32)[None, :]
    anchor = jnp.sum(jnp.where(matches, starts[None, :], 0), axis=1)
    extent = jnp.sum(jnp.where(matches, seq_lens[None, :], 0), axis=1)
    position = slots - anchor
    return (slots, member, position, (position < extent).astype(jnp.int32))


def allowed(query_facts, key_facts):
    query_slot, query_member, query_position, query_valid = query_facts
    key_slot, key_member, key_position, key_valid = key_facts
    same_slot = query_slot[:, None] == key_slot[None, :]
    both_valid = (query_valid[:, None] == 1) & (key_valid[None, :] == 1)
    causal = (query_member[:, None] == key_member[None, :]) & (
        key_position[None, :] <= query_position[:, None]
    )
    return same_slot | both_valid & causal


def key_facts_for(first_row, number, context):
    span_row, half_span, starts, seq_lens, own_facts = context
    return slot_facts(slots_for(first_row, number, span_row, half_span), starts, seq_lens)


def block_scores(query_rot, key_block, query_facts, key_facts):
    score_scale = 1.0 / math.sqrt(query_rot.shape[-1])
    scores = (
        jnp.einsum("qhd,khd->hqk", query_rot, key_block, preferred_element_type=jnp.float32)
        * score_scale
    )
    allowed_pairs = allowed(query_facts, key_facts)
    return (jnp.where(allowed_pairs[None], scores, masked_score), allowed_pairs)


def branch_total(partial_sum):
    return lax.psum(partial_sum.astype(jnp.bfloat16), "tensor").astype(jnp.float32)


def input_total(partial_sum):
    return lax.psum(partial_sum.astype(jnp.bfloat16), "tensor").astype(jnp.float32)


def cycle_attention(query_rot, key_flat, value_flat, context):
    own_facts = context[4]
    count_rows, head_count, head_dim = query_rot.shape
    initial = (
        jnp.full((head_count, count_rows), masked_score, jnp.float32),
        jnp.zeros((head_count, count_rows), jnp.float32),
        jnp.zeros((count_rows, head_count, head_dim), jnp.float32),
    )
    key_piece = lax.all_gather(key_flat, "ctx", axis=0, tiled=True)
    value_piece = lax.all_gather(value_flat, "ctx", axis=0, tiled=True)
    number = key_piece.shape[0]
    block_size = 512
    keys_all = key_piece.reshape(number // block_size, block_size, head_count, head_dim)
    values_all = value_piece.reshape(number // block_size, block_size, head_count, head_dim)

    def fold_key_step(running, members):
        running_max, running_sum, accumulated = running
        key_block, value_block, offset = members
        key_facts = key_facts_for(offset, block_size, context)
        scores, allowed_pairs = block_scores(query_rot, key_block, own_facts, key_facts)
        updated_max = jnp.maximum(running_max, jnp.max(scores, axis=-1))
        factor = jnp.exp(running_max - updated_max)
        softmax_terms = jnp.exp(scores - updated_max[..., None])
        running_sum = running_sum * factor + jnp.sum(softmax_terms, axis=-1)
        accumulated = accumulated * factor.T[:, :, None] + jnp.einsum(
            "hqk,khd->qhd",
            softmax_terms.astype(jnp.bfloat16),
            value_block,
            preferred_element_type=jnp.float32,
        )
        return ((updated_max, running_sum, accumulated), None)

    offsets = jnp.arange(number // block_size, dtype=jnp.int32) * block_size
    running_max, running_sum, accumulated = lax.scan(
        fold_key_step, initial, (keys_all, values_all, offsets)
    )[0]
    attended = accumulated / running_sum.T[:, :, None]
    return (attended, running_max + jnp.log(running_sum))


def attention_backward(query_rot, key_flat, value_flat, attended, log_total, grad_out, context):
    own_facts = context[4]
    count_rows, head_count, head_dim = query_rot.shape
    key_whole, value_whole = (
        lax.all_gather(key_flat, "ctx", axis=0, tiled=True),
        lax.all_gather(value_flat, "ctx", axis=0, tiled=True),
    )
    number = key_whole.shape[0]
    block_size = 512
    score_scale = 1.0 / math.sqrt(head_dim)
    delta = jnp.einsum("qhd,qhd->hq", grad_out.astype(jnp.float32), attended)

    def attention_key_step(grad_query, members):
        key_block, value_block, offset = members
        key_facts = key_facts_for(offset, block_size, context)
        scores, allowed_pairs = block_scores(query_rot, key_block, own_facts, key_facts)
        softmax_terms = jnp.where(allowed_pairs[None], jnp.exp(scores - log_total[..., None]), 0.0)
        grad_terms = jnp.einsum(
            "qhd,khd->hqk", grad_out, value_block, preferred_element_type=jnp.float32
        )
        grad_scores = (softmax_terms * (grad_terms - delta[..., None]) * score_scale).astype(
            jnp.bfloat16
        )
        grad_query = grad_query + jnp.einsum(
            "hqk,khd->qhd", grad_scores, key_block, preferred_element_type=jnp.float32
        )
        grad_keys = jnp.einsum(
            "hqk,qhd->khd", grad_scores, query_rot, preferred_element_type=jnp.float32
        )
        grad_values = jnp.einsum(
            "hqk,qhd->khd",
            softmax_terms.astype(jnp.bfloat16),
            grad_out,
            preferred_element_type=jnp.float32,
        )
        return (
            grad_query,
            (grad_keys.reshape(block_size, -1), grad_values.reshape(block_size, -1)),
        )

    keys_all = key_whole.reshape(number // block_size, block_size, head_count, head_dim)
    values_all = value_whole.reshape(number // block_size, block_size, head_count, head_dim)
    offsets = jnp.arange(number // block_size, dtype=jnp.int32) * block_size
    zeros = jnp.zeros((count_rows, head_count, head_dim), jnp.float32)
    grad_query, (key_terms, value_terms) = lax.scan(
        attention_key_step, zeros, (keys_all, values_all, offsets)
    )
    own_keys, own_values = (
        lax.psum_scatter(
            key_terms.reshape(number, -1).astype(jnp.bfloat16),
            "ctx",
            scatter_dimension=0,
            tiled=True,
        ).astype(jnp.float32),
        lax.psum_scatter(
            value_terms.reshape(number, -1).astype(jnp.bfloat16),
            "ctx",
            scatter_dimension=0,
            tiled=True,
        ).astype(jnp.float32),
    )
    return (grad_query, own_keys, own_values)


def forward_layer(residual, full_weights, context, tables):
    (
        gain_front,
        query_full,
        keys_full,
        values_full,
        project_full,
        gain_back,
        gating_full,
        upward_full,
        downward_full,
    ) = full_weights
    count_rows = residual.shape[0]
    head_count = query_full.shape[1] // HEAD_DIM
    head_shape = (count_rows, head_count, HEAD_DIM)
    scaled = rms_parts(residual)[0]
    normed = (scaled * gain_front.astype(jnp.float32)).astype(jnp.bfloat16)
    query_rot = rotate(
        jnp.dot(normed, query_full, preferred_element_type=jnp.float32).reshape(head_shape),
        tables,
        1.0,
    ).astype(jnp.bfloat16)
    key_rot = rotate(
        jnp.dot(normed, keys_full, preferred_element_type=jnp.float32).reshape(head_shape),
        tables,
        1.0,
    ).astype(jnp.bfloat16)
    key_flat = key_rot.reshape(count_rows, -1)
    value_flat = jnp.dot(normed, values_full, preferred_element_type=jnp.float32).astype(
        jnp.bfloat16
    )
    attended, log_total = cycle_attention(query_rot, key_flat, value_flat, context)
    mixed_heads = attended.reshape(count_rows, -1).astype(jnp.bfloat16)
    hidden = residual + depth_scale * branch_total(
        jnp.dot(mixed_heads, project_full, preferred_element_type=jnp.float32)
    )
    scaled_two = rms_parts(hidden)[0]
    normed_two = (scaled_two * gain_back.astype(jnp.float32)).astype(jnp.bfloat16)
    gating = jnp.dot(normed_two, gating_full, preferred_element_type=jnp.float32)
    upward = jnp.dot(normed_two, upward_full, preferred_element_type=jnp.float32)
    activated = (jax.nn.silu(gating) * upward).astype(jnp.bfloat16)
    result = hidden + depth_scale * branch_total(
        jnp.dot(activated, downward_full, preferred_element_type=jnp.float32)
    )
    record = (
        residual,
        normed,
        query_rot,
        key_flat,
        value_flat,
        attended,
        log_total,
        mixed_heads,
        hidden,
        normed_two,
        gating,
        upward,
        activated,
    )
    return (result, record)


def backward_layer(grad_rows, full_weights, record, context, tables):
    (
        gain_front,
        query_full,
        keys_full,
        values_full,
        project_full,
        gain_back,
        gating_full,
        upward_full,
        downward_full,
    ) = full_weights
    (
        residual,
        normed,
        query_rot,
        key_flat,
        value_flat,
        attended,
        log_total,
        mixed_heads,
        hidden,
        normed_two,
        gating,
        upward,
        activated,
    ) = record
    count_rows = grad_rows.shape[0]
    head_shape = query_rot.shape
    down_grad = (depth_scale * grad_rows).astype(jnp.bfloat16)
    grad_act = times_transposed(down_grad, downward_full)
    sigmoid_gate = jax.nn.sigmoid(gating)
    grad_gating = (grad_act * upward * sigmoid_gate * (1.0 + gating * (1.0 - sigmoid_gate))).astype(
        jnp.bfloat16
    )
    grad_upward = (grad_act * gating * sigmoid_gate).astype(jnp.bfloat16)
    grad_normed_two = input_total(
        times_transposed(grad_gating, gating_full) + times_transposed(grad_upward, upward_full)
    )
    gain_back_grad, grad_from_norm = norm_backward(hidden, gain_back, grad_normed_two)
    grad_hidden = grad_rows + grad_from_norm
    mlp_part = (
        lax.psum_scatter(gain_back_grad, ("dp", "ctx"), scatter_dimension=0, tiled=True),
        lax.psum_scatter(
            outer_rows(normed_two, grad_gating), ("dp", "ctx"), scatter_dimension=0, tiled=True
        ),
        lax.psum_scatter(
            outer_rows(normed_two, grad_upward), ("dp", "ctx"), scatter_dimension=0, tiled=True
        ),
        lax.psum_scatter(
            outer_rows(down_grad, activated), ("dp", "ctx"), scatter_dimension=0, tiled=True
        ),
    )
    branch_grad = (depth_scale * grad_hidden).astype(jnp.bfloat16)
    grad_mixed = (
        times_transposed(branch_grad, project_full).astype(jnp.bfloat16).reshape(head_shape)
    )
    grad_query, own_keys, own_values = attention_backward(
        query_rot, key_flat, value_flat, attended, log_total, grad_mixed, context
    )
    query_grad = rotate(grad_query, tables, -1.0).reshape(count_rows, -1).astype(jnp.bfloat16)
    keys_grad = (
        rotate(own_keys.reshape(head_shape), tables, -1.0)
        .reshape(count_rows, -1)
        .astype(jnp.bfloat16)
    )
    values_grad = own_values.astype(jnp.bfloat16)
    grad_normed = input_total(
        times_transposed(query_grad, query_full)
        + times_transposed(keys_grad, keys_full)
        + times_transposed(values_grad, values_full)
    )
    gain_front_grad, grad_input_norm = norm_backward(residual, gain_front, grad_normed)
    attention_part = (
        lax.psum_scatter(gain_front_grad, ("dp", "ctx"), scatter_dimension=0, tiled=True),
        lax.psum_scatter(
            outer_rows(normed, query_grad), ("dp", "ctx"), scatter_dimension=0, tiled=True
        ),
        lax.psum_scatter(
            outer_rows(normed, keys_grad), ("dp", "ctx"), scatter_dimension=0, tiled=True
        ),
        lax.psum_scatter(
            outer_rows(normed, values_grad), ("dp", "ctx"), scatter_dimension=0, tiled=True
        ),
        lax.psum_scatter(
            outer_rows(branch_grad, mixed_heads), ("dp", "ctx"), scatter_dimension=0, tiled=True
        ),
    )
    attention_list = (
        attention_part[0],
        attention_part[1],
        attention_part[2],
        attention_part[3],
        attention_part[4].T,
    )
    mlp_list = (mlp_part[0], mlp_part[1], mlp_part[2], mlp_part[3].T)
    return (grad_hidden + grad_input_norm, attention_list + mlp_list)


def body(
    inputs,
    cotangent,
    lengths,
    dealing,
    span_table,
    prenorm_gain,
    query_weight,
    keys_weight,
    values_weight,
    project_weight,
    postnorm_gain,
    gating_weight,
    upward_weight,
    downward_weight,
):
    stacked = (
        prenorm_gain,
        query_weight,
        keys_weight,
        values_weight,
        project_weight,
        postnorm_gain,
        gating_weight,
        upward_weight,
        downward_weight,
    )
    count_rows = inputs.shape[0]
    half_span = count_rows // 2
    group_index = lax.axis_index("dp")
    ctx_index = lax.axis_index("ctx")
    seq_count = lengths.shape[0] // lax.axis_size("dp")
    starts, seq_lens = group_layout(lengths, dealing, group_index, seq_count)
    span_row = lax.dynamic_index_in_dim(span_table, group_index, 0, keepdims=False)
    own_facts = slot_facts(
        slots_for(ctx_index * count_rows, count_rows, span_row, half_span), starts, seq_lens
    )
    tables = rope_tables(own_facts[2], HEAD_DIM // 2)
    context = (span_row, half_span, starts, seq_lens, own_facts)
    residual = inputs.astype(jnp.float32)
    records = []
    gathered = []
    for layer_index in range(LAYERS):
        local_parts = tuple((weight[layer_index] for weight in stacked))
        full_weights = (
            lax.all_gather(local_parts[0], ("dp", "ctx"), axis=0, tiled=True),
            lax.all_gather(local_parts[1], ("dp", "ctx"), axis=0, tiled=True),
            lax.all_gather(local_parts[2], ("dp", "ctx"), axis=0, tiled=True),
            lax.all_gather(local_parts[3], ("dp", "ctx"), axis=0, tiled=True),
            lax.all_gather(local_parts[4], ("dp", "ctx"), axis=1, tiled=True),
            lax.all_gather(local_parts[5], ("dp", "ctx"), axis=0, tiled=True),
            lax.all_gather(local_parts[6], ("dp", "ctx"), axis=0, tiled=True),
            lax.all_gather(local_parts[7], ("dp", "ctx"), axis=0, tiled=True),
            lax.all_gather(local_parts[8], ("dp", "ctx"), axis=1, tiled=True),
        )
        gathered.append(full_weights)
        residual, record = forward_layer(residual, full_weights, context, tables)
        records.append(record)
    grad_rows = cotangent.astype(jnp.float32)
    layer_grads = [None] * LAYERS
    for layer_index in reversed(range(LAYERS)):
        local_parts = tuple((weight[layer_index] for weight in stacked))
        full_weights = (
            lax.all_gather(local_parts[0], ("dp", "ctx"), axis=0, tiled=True),
            lax.all_gather(local_parts[1], ("dp", "ctx"), axis=0, tiled=True),
            lax.all_gather(local_parts[2], ("dp", "ctx"), axis=0, tiled=True),
            lax.all_gather(local_parts[3], ("dp", "ctx"), axis=0, tiled=True),
            lax.all_gather(local_parts[4], ("dp", "ctx"), axis=1, tiled=True),
            lax.all_gather(local_parts[5], ("dp", "ctx"), axis=0, tiled=True),
            lax.all_gather(local_parts[6], ("dp", "ctx"), axis=0, tiled=True),
            lax.all_gather(local_parts[7], ("dp", "ctx"), axis=0, tiled=True),
            lax.all_gather(local_parts[8], ("dp", "ctx"), axis=1, tiled=True),
        )
        grad_rows, layer_grads[layer_index] = backward_layer(
            grad_rows, full_weights, records[layer_index], context, tables
        )
    grads = tuple(
        (jnp.stack([parts[member_index] for parts in layer_grads]) for member_index in range(9))
    )
    return (residual.astype(jnp.bfloat16), grad_rows) + grads


def solution(mesh):
    placed = (
        P(("dp", "ctx"), None),
        P(("dp", "ctx"), None),
        P(),
        P(),
        P(),
        P(None, ("dp", "ctx")),
        P(None, ("dp", "ctx"), "tensor"),
        P(None, ("dp", "ctx"), "tensor"),
        P(None, ("dp", "ctx"), "tensor"),
        P(None, "tensor", ("dp", "ctx")),
        P(None, ("dp", "ctx")),
        P(None, ("dp", "ctx"), "tensor"),
        P(None, ("dp", "ctx"), "tensor"),
        P(None, "tensor", ("dp", "ctx")),
    )
    return jax.shard_map(
        body,
        mesh=mesh,
        in_specs=placed,
        out_specs=(
            P(("dp", "ctx"), None),
            P(("dp", "ctx"), None),
            P(None, ("dp", "ctx")),
            P(None, ("dp", "ctx"), "tensor"),
            P(None, ("dp", "ctx"), "tensor"),
            P(None, ("dp", "ctx"), "tensor"),
            P(None, "tensor", ("dp", "ctx")),
            P(None, ("dp", "ctx")),
            P(None, ("dp", "ctx"), "tensor"),
            P(None, ("dp", "ctx"), "tensor"),
            P(None, "tensor", ("dp", "ctx")),
        ),
        check_vma=False,
    )
```

profile of v0, /device:TPU:0, one launch (start us, length us, event | category | flops | bytes accessed | tf_op | source)
XLA Modules:
  0.0 6063.0 jit_solution(2649568263841352777)
XLA Ops:
  13.7 79.9 %all-reduce.9 = (bf16[2304]{0:T(1024)(128)(2,1)S(1)}, bf16[2304]{0:T(1024)(128)(2,1)S(1)}, bf16[2304]{0:T(1024)(128)(2,1)S(1)}, bf16[2304]{0:T(1024)(128)(2,1)S(1)}) all-reduce(bf16[2304]{0:T(1024)(128)(2,1)S(1)} %dynamic-update-slice.1, ...), channel_id=7, replica_groups=mesh['dp'=4,'ctx'=4,'tensor'=2] {'dp','ctx'}, use_global_device_ids=true, to_apply=%add.1 | all-reduce | flops 9216 | bytes 36864
  106.1 82.2 %all-gather.45.cloned.1.call-done = bf16[1,2304,1152]{2,1,0:T(8,128)(2,1)} async-done(((bf16[1,144,1152]{2,1,0:T(8,128)(2,1)}), bf16[1,2304,1152]{2,1,0:T(8,128)(2,1)}) %all-gather.45.cloned.1.call-update) | async-done | bytes 5308432 | tf_op jit(solution)/shard_map/all_gather | solution.py:438
  193.1 82.8 %all-gather.47.cloned.1.call-done = bf16[1,2304,1152]{2,1,0:T(8,128)(2,1)} async-done(((bf16[1,144,1152]{2,1,0:T(8,128)(2,1)}), bf16[1,2304,1152]{2,1,0:T(8,128)(2,1)}) %all-gather.47.cloned.1.call-update) | async-done | bytes 5308432 | tf_op jit(solution)/shard_map/all_gather | solution.py:439
  283.8 23.0 all-gather.39.cloned.1.call-done
  308.4 31.4 all-gather.37.cloned.1.call-done
  346.5 80.5 %all-gather.51.cloned.1.call-done = bf16[1,1152,2304]{1,2,0:T(8,128)(2,1)} async-done(((bf16[1,1152,144]{1,2,0:T(8,128)(2,1)}), bf16[1,1152,2304]{1,2,0:T(8,128)(2,1)}) %all-gather.51.cloned.1.call-update) | async-done | bytes 5308432 | tf_op jit(solution)/shard_map/all_gather | solution.py:441
  451.4 164.5 %all-gather.53.cloned.1.call-done = bf16[1,2304,2880]{2,1,0:T(8,128)(2,1)} async-done(((bf16[1,144,2880]{2,1,0:T(8,128)(2,1)}), bf16[1,2304,2880]{2,1,0:T(8,128)(2,1)}) %all-gather.53.cloned.1.call-update) | async-done | bytes 13271056 | tf_op jit(solution)/shard_map/all_gather | solution.py:443
  625.1 153.9 %all-gather.55.cloned.1.call-done = bf16[1,2304,2880]{2,1,0:T(8,128)(2,1)} async-done(((bf16[1,144,2880]{2,1,0:T(8,128)(2,1)}), bf16[1,2304,2880]{2,1,0:T(8,128)(2,1)}) %all-gather.55.cloned.1.call-update) | async-done | bytes 13271056 | tf_op jit(solution)/shard_map/all_gather | solution.py:444
  790.8 151.4 %all-gather.57.cloned.1.call-done = bf16[1,2880,2304]{1,2,0:T(8,128)(2,1)} async-done(((bf16[1,2880,144]{1,2,0:T(8,128)(2,1)}), bf16[1,2880,2304]{1,2,0:T(8,128)(2,1)}) %all-gather.57.cloned.1.call-update) | async-done | bytes 13271056 | tf_op jit(solution)/shard_map/all_gather | solution.py:445
  970.5 87.8 %all-gather.63.cloned.1.call-done = bf16[1,2304,1152]{2,1,0:T(8,128)(2,1)} async-done(((bf16[1,144,1152]{2,1,0:T(8,128)(2,1)}), bf16[1,2304,1152]{2,1,0:T(8,128)(2,1)}) %all-gather.63.cloned.1.call-update) | async-done | bytes 5308432 | tf_op jit(solution)/shard_map/all_gather | solution.py:440
  1062.6 82.7 %all-gather.61.cloned.1.call-done = bf16[1,2304,1152]{2,1,0:T(8,128)(2,1)} async-done(((bf16[1,144,1152]{2,1,0:T(8,128)(2,1)}), bf16[1,2304,1152]{2,1,0:T(8,128)(2,1)}) %all-gather.61.cloned.1.call-update) | async-done | bytes 5308432 | tf_op jit(solution)/shard_map/all_gather | solution.py:439
  1150.1 82.2 %all-gather.59.cloned.1.call-done = bf16[1,2304,1152]{2,1,0:T(8,128)(2,1)} async-done(((bf16[1,144,1152]{2,1,0:T(8,128)(2,1)}), bf16[1,2304,1152]{2,1,0:T(8,128)(2,1)}) %all-gather.59.cloned.1.call-update) | async-done | bytes 5308432 | tf_op jit(solution)/shard_map/all_gather | solution.py:438
  1239.1 24.1 all-gather.43.cloned.1.call-done
  1265.6 30.5 all-gather.41.cloned.1.call-done
  1302.9 79.9 %all-gather.65.cloned.1.call-done = bf16[1,1152,2304]{1,2,0:T(8,128)(2,1)} async-done(((bf16[1,1152,144]{1,2,0:T(8,128)(2,1)}), bf16[1,1152,2304]{1,2,0:T(8,128)(2,1)}) %all-gather.65.cloned.1.call-update) | async-done | bytes 5308432 | tf_op jit(solution)/shard_map/all_gather | solution.py:441
  1389.1 156.7 %all-gather.71.cloned.1.call-done = bf16[1,2880,2304]{1,2,0:T(8,128)(2,1)} async-done(((bf16[1,2880,144]{1,2,0:T(8,128)(2,1)}), bf16[1,2880,2304]{1,2,0:T(8,128)(2,1)}) %all-gather.71.cloned.1.call-update) | async-done | bytes 13271056 | tf_op jit(solution)/shard_map/all_gather | solution.py:445
  1568.3 163.5 %all-gather.69.cloned.1.call-done = bf16[1,2304,2880]{2,1,0:T(8,128)(2,1)} async-done(((bf16[1,144,2880]{2,1,0:T(8,128)(2,1)}), bf16[1,2304,2880]{2,1,0:T(8,128)(2,1)}) %all-gather.69.cloned.1.call-update) | async-done | bytes 13271056 | tf_op jit(solution)/shard_map/all_gather | solution.py:444
  1743.4 151.7 %all-gather.67.cloned.1.call-done = bf16[1,2304,2880]{2,1,0:T(8,128)(2,1)} async-done(((bf16[1,144,2880]{2,1,0:T(8,128)(2,1)}), bf16[1,2304,2880]{2,1,0:T(8,128)(2,1)}) %all-gather.67.cloned.1.call-update) | async-done | bytes 13271056 | tf_op jit(solution)/shard_map/all_gather | solution.py:443
  2317.6 79.4 %all-reduce.8 = (f32[2304]{0:T(1024)}, f32[2304]{0:T(1024)}, f32[2304]{0:T(1024)}, f32[2304]{0:T(1024)}) all-reduce(f32[2304]{0:T(1024)} %get-tuple-element.150, f32[2304]{0:T(1024)} %get-tuple-element.152, f32[2304]{0:T(1024)} %get-tuple-element.148, ...), channel_id=25, replica_groups=mesh['dp'=4,'ctx'=4,'tensor'=2] {'dp','ctx'}, use_global_device_ids=true, to_apply=%region_30.31.clone | all-reduce | flops 9216 | bytes 73728
  2405.3 176.7 %reduce-scatter.39.cloned.1.call-done = f32[144,1152]{1,0:T(8,128)} async-done(((f32[2304,1152]{1,0:T(8,128)}), f32[144,1152]{1,0:T(8,128)}) %reduce-scatter.39.cloned.1.call-update) | async-done | bytes 663568 | tf_op jit(solution)/shard_map/reduce_scatter | solution.py:377
  2584.5 185.8 %reduce-scatter.37.cloned.1.call-done = f32[144,1152]{1,0:T(8,128)} async-done(((f32[2304,1152]{1,0:T(8,128)}), f32[144,1152]{1,0:T(8,128)}) %reduce-scatter.37.cloned.1.call-update) | async-done | bytes 663568 | tf_op jit(solution)/shard_map/reduce_scatter | solution.py:374
  2770.3 187.2 %reduce-scatter.35.cloned.1.call-done = f32[144,1152]{1,0:T(8,128)} async-done(((f32[2304,1152]{1,0:T(8,128)}), f32[144,1152]{1,0:T(8,128)}) %reduce-scatter.35.cloned.1.call-update) | async-done | bytes 663568 | tf_op jit(solution)/shard_map/reduce_scatter | solution.py:374
  2959.9 186.0 %reduce-scatter.29.cloned.1.call-done = f32[144,1152]{1,0:T(8,128)} async-done(((f32[2304,1152]{1,0:T(8,128)}), f32[144,1152]{1,0:T(8,128)}) %reduce-scatter.29.cloned.1.call-update) | async-done | bytes 663568 | tf_op jit(solution)/shard_map/reduce_scatter | solution.py:368
  3145.9 187.3 %reduce-scatter.27.cloned.1.call-done = f32[144,1152]{1,0:T(8,128)} async-done(((f32[2304,1152]{1,0:T(8,128)}), f32[144,1152]{1,0:T(8,128)}) %reduce-scatter.27.cloned.1.call-update) | async-done | bytes 663568 | tf_op jit(solution)/shard_map/reduce_scatter | solution.py:368
  3335.6 185.7 %reduce-scatter.33.cloned.1.call-done = f32[144,1152]{1,0:T(8,128)} async-done(((f32[2304,1152]{1,0:T(8,128)}), f32[144,1152]{1,0:T(8,128)}) %reduce-scatter.33.cloned.1.call-update) | async-done | bytes 663568 | tf_op jit(solution)/shard_map/reduce_scatter | solution.py:371
  3521.3 187.2 %reduce-scatter.31.cloned.1.call-done = f32[144,1152]{1,0:T(8,128)} async-done(((f32[2304,1152]{1,0:T(8,128)}), f32[144,1152]{1,0:T(8,128)}) %reduce-scatter.31.cloned.1.call-update) | async-done | bytes 663568 | tf_op jit(solution)/shard_map/reduce_scatter | solution.py:371
  3710.9 388.4 %reduce-scatter.53.cloned.1.call-done = f32[144,2880]{1,0:T(8,128)} async-done(((f32[2304,2880]{1,0:T(8,128)}), f32[144,2880]{1,0:T(8,128)}) %reduce-scatter.53.cloned.1.call-update) | async-done | bytes 1658896 | tf_op jit(solution)/shard_map/reduce_scatter | solution.py:342
  4099.3 390.5 %reduce-scatter.51.cloned.1.call-done = f32[144,2880]{1,0:T(8,128)} async-done(((f32[2304,2880]{1,0:T(8,128)}), f32[144,2880]{1,0:T(8,128)}) %reduce-scatter.51.cloned.1.call-update) | async-done | bytes 1658896 | tf_op jit(solution)/shard_map/reduce_scatter | solution.py:342
  4493.7 386.7 %reduce-scatter.45.cloned.1.call-done = f32[144,2880]{1,0:T(8,128)} async-done(((f32[2304,2880]{1,0:T(8,128)}), f32[144,2880]{1,0:T(8,128)}) %reduce-scatter.45.cloned.1.call-update) | async-done | bytes 1658896 | tf_op jit(solution)/shard_map/reduce_scatter | solution.py:336
  4880.4 390.6 %reduce-scatter.43.cloned.1.call-done = f32[144,2880]{1,0:T(8,128)} async-done(((f32[2304,2880]{1,0:T(8,128)}), f32[144,2880]{1,0:T(8,128)}) %reduce-scatter.43.cloned.1.call-update) | async-done | bytes 1658896 | tf_op jit(solution)/shard_map/reduce_scatter | solution.py:336
  5274.9 386.6 %reduce-scatter.49.cloned.1.call-done = f32[144,2880]{1,0:T(8,128)} async-done(((f32[2304,2880]{1,0:T(8,128)}), f32[144,2880]{1,0:T(8,128)}) %reduce-scatter.49.cloned.1.call-update) | async-done | bytes 1658896 | tf_op jit(solution)/shard_map/reduce_scatter | solution.py:339
  5661.6 390.4 %reduce-scatter.47.cloned.1.call-done = f32[144,2880]{1,0:T(8,128)} async-done(((f32[2304,2880]{1,0:T(8,128)}), f32[144,2880]{1,0:T(8,128)}) %reduce-scatter.47.cloned.1.call-update) | async-done | bytes 1658896 | tf_op jit(solution)/shard_map/reduce_scatter | solution.py:339
  (439 shorter events, 628.4 us)
Async XLA Ops:
  9.4 178.9 %all-gather.45.cloned.1.call-start = ((), (), s32[]{:S(2)}) async-start(), calls=%async_computation.42 | async-start | bytes 5640192 | tf_op jit(solution)/shard_map/all_gather | solution.py:438
  10.4 265.5 %all-gather.47.cloned.1.call-start = ((), (), s32[]{:S(2)}) async-start(), calls=%async_computation.43 | async-start | bytes 5640192 | tf_op jit(solution)/shard_map/all_gather | solution.py:439
  11.4 295.4 %all-gather.39.cloned.1.call-start = ((), (), s32[]{:S(2)}) async-start(), calls=%async_computation.19 | async-start | bytes 1474560 | tf_op jit(solution)/shard_map/all_gather | solution.py:136
  104.6 235.2 %all-gather.37.cloned.1.call-start = ((), (), s32[]{:S(2)}) async-start(), calls=%async_computation.18 | async-start | bytes 1474560 | tf_op jit(solution)/shard_map/all_gather | solution.py:135
  432.1 183.7 %all-gather.53.cloned.1.call-start = ((), (), s32[]{:S(2)}) async-start(), calls=%async_computation.46 | async-start | bytes 14413824 | tf_op jit(solution)/shard_map/all_gather | solution.py:443
  433.5 345.6 %all-gather.55.cloned.1.call-start = ((), (), s32[]{:S(2)}) async-start(), calls=%async_computation.47 | async-start | bytes 14413824 | tf_op jit(solution)/shard_map/all_gather | solution.py:444
  436.4 505.7 %all-gather.57.cloned.1.call-start = ((), (), s32[]{:S(2)}) async-start(), calls=%async_computation.48 | async-start | bytes 14413824 | tf_op jit(solution)/shard_map/all_gather | solution.py:445
  437.8 531.0 %all-reduce.21.cloned.1.call-start = ((), (), s32[]{:S(2)}) async-start(), calls=%async_computation.21 | async-start | bytes 1179648 | tf_op jit(solution)/shard_map/psum | solution.py:120
  952.2 193.2 %all-gather.61.cloned.1.call-start = ((), (), s32[]{:S(2)}) async-start(), calls=%async_computation.50 | async-start | bytes 5640192 | tf_op jit(solution)/shard_map/all_gather | solution.py:439
  953.0 279.3 %all-gather.59.cloned.1.call-start = ((), (), s32[]{:S(2)}) async-start(), calls=%async_computation.49 | async-start | bytes 5640192 | tf_op jit(solution)/shard_map/all_gather | solution.py:438
  953.5 309.7 %all-gather.43.cloned.1.call-start = ((), (), s32[]{:S(2)}) async-start(), calls=%async_computation.23 | async-start | bytes 1474560 | tf_op jit(solution)/shard_map/all_gather | solution.py:136
  1062.6 233.5 %all-gather.41.cloned.1.call-start = ((), (), s32[]{:S(2)}) async-start(), calls=%async_computation.22 | async-start | bytes 1474560 | tf_op jit(solution)/shard_map/all_gather | solution.py:135
  1238.5 307.3 %all-gather.71.cloned.1.call-start = ((), (), s32[]{:S(2)}) async-start(), calls=%async_computation.55 | async-start | bytes 14413824 | tf_op jit(solution)/shard_map/all_gather | solution.py:445
  1239.1 326.7 %all-reduce.23.cloned.1.call-start = ((), (), s32[]{:S(2)}) async-start(), calls=%async_computation.24 | async-start | bytes 1179648 | tf_op jit(solution)/shard_map/psum | solution.py:120
  1387.7 344.1 %all-gather.69.cloned.1.call-start = ((), (), s32[]{:S(2)}) async-start(), calls=%async_computation.54 | async-start | bytes 14413824 | tf_op jit(solution)/shard_map/all_gather | solution.py:444
  1388.3 506.8 %all-gather.67.cloned.1.call-start = ((), (), s32[]{:S(2)}) async-start(), calls=%async_computation.53 | async-start | bytes 14413824 | tf_op jit(solution)/shard_map/all_gather | solution.py:443
  1389.1 554.5 %all-reduce.25.cloned.1.call-start = ((), (), s32[]{:S(2)}) async-start(), calls=%async_computation.25 | async-start | bytes 1179648 | tf_op jit(solution)/shard_map/psum | solution.py:124
  2124.9 190.5 %all-reduce.31.cloned.1.call-start = ((), (), s32[]{:S(2)}) async-start(), calls=%async_computation.60 | async-start | bytes 2359296 | tf_op jit(solution)/shard_map/psum | solution.py:120
  2184.3 221.0 %reduce-scatter.41.cloned.1.call-start = ((), (), s32[]{:S(2)}) async-start(), calls=%async_computation.35 | async-start | bytes 11280384 | tf_op jit(solution)/shard_map/reduce_scatter | solution.py:377
  2190.9 391.1 %reduce-scatter.39.cloned.1.call-start = ((), (), s32[]{:S(2)}) async-start(), calls=%async_computation.34 | async-start | bytes 11280384 | tf_op jit(solution)/shard_map/reduce_scatter | solution.py:377
  2197.4 572.9 %reduce-scatter.37.cloned.1.call-start = ((), (), s32[]{:S(2)}) async-start(), calls=%async_computation.33 | async-start | bytes 11280384 | tf_op jit(solution)/shard_map/reduce_scatter | solution.py:374
  2203.9 753.5 %reduce-scatter.35.cloned.1.call-start = ((), (), s32[]{:S(2)}) async-start(), calls=%async_computation.32 | async-start | bytes 11280384 | tf_op jit(solution)/shard_map/reduce_scatter | solution.py:374
  2210.6 935.3 %reduce-scatter.29.cloned.1.call-start = ((), (), s32[]{:S(2)}) async-start(), calls=%async_computation.29 | async-start | bytes 11280384 | tf_op jit(solution)/shard_map/reduce_scatter | solution.py:368
  2217.0 1116.2 %reduce-scatter.27.cloned.1.call-start = ((), (), s32[]{:S(2)}) async-start(), calls=%async_computation.28 | async-start | bytes 11280384 | tf_op jit(solution)/shard_map/reduce_scatter | solution.py:368
  2223.7 1297.7 %reduce-scatter.33.cloned.1.call-start = ((), (), s32[]{:S(2)}) async-start(), calls=%async_computation.31 | async-start | bytes 11280384 | tf_op jit(solution)/shard_map/reduce_scatter | solution.py:371
  2230.1 1478.4 %reduce-scatter.31.cloned.1.call-start = ((), (), s32[]{:S(2)}) async-start(), calls=%async_computation.30 | async-start | bytes 11280384 | tf_op jit(solution)/shard_map/reduce_scatter | solution.py:371
  2236.7 1862.6 %reduce-scatter.53.cloned.1.call-start = ((), (), s32[]{:S(2)}) async-start(), calls=%async_computation.41 | async-start | bytes 28827648 | tf_op jit(solution)/shard_map/reduce_scatter | solution.py:342
  2249.4 2240.4 %reduce-scatter.51.cloned.1.call-start = ((), (), s32[]{:S(2)}) async-start(), calls=%async_computation.40 | async-start | bytes 28827648 | tf_op jit(solution)/shard_map/reduce_scatter | solution.py:342
  2263.0 2617.4 %reduce-scatter.45.cloned.1.call-start = ((), (), s32[]{:S(2)}) async-start(), calls=%async_computation.37 | async-start | bytes 28827648 | tf_op jit(solution)/shard_map/reduce_scatter | solution.py:336
  2276.5 2994.5 %reduce-scatter.43.cloned.1.call-start = ((), (), s32[]{:S(2)}) async-start(), calls=%async_computation.36 | async-start | bytes 28827648 | tf_op jit(solution)/shard_map/reduce_scatter | solution.py:336
  2289.7 3371.8 %reduce-scatter.49.cloned.1.call-start = ((), (), s32[]{:S(2)}) async-start(), calls=%async_computation.39 | async-start | bytes 28827648 | tf_op jit(solution)/shard_map/reduce_scatter | solution.py:339
  2302.2 3749.8 %reduce-scatter.47.cloned.1.call-start = ((), (), s32[]{:S(2)}) async-start(), calls=%async_computation.38 | async-start | bytes 28827648 | tf_op jit(solution)/shard_map/reduce_scatter | solution.py:339
  (102 other events, 6289.1 us)
Sparse Core Ops, SparseCore 0:
  11.4 88.9 all-gather.48
  103.7 84.5 all-gather.44
  191.6 84.2 all-gather.46
  308.8 30.9 all-gather.36
  342.9 84.0 all-gather.50
  453.3 162.4 all-gather.52
  619.5 159.4 all-gather.54
  782.6 159.4 all-gather.56
  971.4 86.8 all-gather.62
  1061.1 84.2 all-gather.60
  1148.0 84.2 all-gather.58
  1265.2 30.8 all-gather.40
  1298.7 84.0 all-gather.64
  1386.0 159.7 all-gather.70
  1569.4 162.4 all-gather.68
  1735.6 159.4 all-gather.66
  1960.1 30.3 reduce-scatter.54
  2117.7 30.3 reduce-scatter.58
  2209.7 184.9 reduce-scatter.40
  2400.5 181.5 reduce-scatter.38
  2588.9 181.3 reduce-scatter.36
  2776.0 181.4 reduce-scatter.34
  2964.3 181.5 reduce-scatter.28
  3151.7 181.4 reduce-scatter.26
  3339.9 181.4 reduce-scatter.32
  3527.0 181.4 reduce-scatter.30
  3715.4 383.8 reduce-scatter.52
  4106.1 383.5 reduce-scatter.50
  4496.8 383.5 reduce-scatter.44
  4887.4 383.5 reduce-scatter.42
  5278.0 383.5 reduce-scatter.48
  5668.4 383.5 reduce-scatter.46
  (11 shorter events, 237.5 us)
where the time goes:
time: 6070 us; the launch traced here: 6060 us
  waiting for transfers between devices  5430 us (89%)
  matrix products  349 us (6%)
  blocking collectives  159 us (3%)
    reduce_scatter x2, waiting for transfers between devices, backward_layer(): lax.psum_scatter(outer_rows(down_grad, activated), ('dp', 'ctx'), scatter...  779 us
    reduce_scatter x2, waiting for transfers between devices, backward_layer(): lax.psum_scatter(outer_rows(normed_two, grad_gating), ('dp', 'ctx'), scat...  777 us
    reduce_scatter x2, waiting for transfers between devices, backward_layer(): lax.psum_scatter(outer_rows(normed_two, grad_upward), ('dp', 'ctx'), scat...  777 us
    reduce_scatter x2, waiting for transfers between devices, backward_layer(): lax.psum_scatter(outer_rows(normed, query_grad), ('dp', 'ctx'), scatter_d...  373 us
    reduce_scatter x2, waiting for transfers between devices, backward_layer(): lax.psum_scatter(outer_rows(normed, values_grad), ('dp', 'ctx'), scatter_...  373 us
    reduce_scatter x2, waiting for transfers between devices, backward_layer(): lax.psum_scatter(outer_rows(normed, keys_grad), ('dp', 'ctx'), scatter_di...  373 us
    all_gather x2, waiting for transfers between devices, body(): lax.all_gather(local_parts[7], ('dp', 'ctx'), axis=0, tiled=True)  317 us
    all_gather x2, waiting for transfers between devices, body(): lax.all_gather(local_parts[6], ('dp', 'ctx'), axis=0, tiled=True)  316 us
  transfers between devices with their start and end apart: 43, of which 41 were waited for; matrix products, arithmetic and copies ran while one was open for 5% of the time, Pallas kernels for 0%

commit v1 on v0

v1 whole, which is shorter than its diff:
```python
import math

import functools

import jax
import jax.numpy as jnp
from jax import lax
from jax.experimental import pallas as pl
from jax.experimental.pallas import tpu as pltpu
from jax.sharding import PartitionSpec as P

MESH = pl.DeviceIdType.MESH

HEAD_DIM = 64
LAYERS = 2
BLOCK = 128
LANES = 128

eps_norm = 1e-05
depth_scale = 1.4 / math.sqrt(40.0)
rope_base = 10000.0
masked_score = -1e30
score_scale = 1.0 / math.sqrt(HEAD_DIM)


def times(left, right):
    return jnp.dot(left, right, preferred_element_type=jnp.float32)


def times_transposed(left, right):
    return lax.dot_general(
        left, right, (((1,), (1,)), ((), ())), preferred_element_type=jnp.float32
    )


def outer_rows(left, right):
    return lax.dot_general(
        left, right, (((0,), (0,)), ((), ())), preferred_element_type=jnp.float32
    )


def rms_parts(values):
    inverse = lax.rsqrt(jnp.mean(values * values, axis=-1, keepdims=True) + eps_norm)
    return (values * inverse, inverse)


def norm_backward(values, gain, grad_normed):
    scaled, inverse = rms_parts(values)
    gain_grad = jnp.sum(grad_normed * scaled, axis=0, keepdims=True)
    grad_scaled = grad_normed * gain
    return (
        gain_grad,
        inverse * (grad_scaled - scaled * jnp.mean(grad_scaled * scaled, axis=-1, keepdims=True)),
    )


def rope_tables(position, half_dim):
    inverse = rope_base ** (-jnp.arange(half_dim).astype(jnp.float32) / half_dim)
    angles = position.astype(jnp.float32)[:, None] * inverse[None, :]
    return (jnp.cos(angles)[:, None, :], jnp.sin(angles)[:, None, :])


def rotate(values, tables, direction):
    cosine, sine_table = tables
    half_dim = values.shape[-1] // 2
    front_half = values[..., :half_dim]
    back_half = values[..., half_dim:]
    return jnp.concatenate(
        [
            front_half * cosine - direction * back_half * sine_table,
            back_half * cosine + direction * front_half * sine_table,
        ],
        axis=-1,
    )


def group_layout(lengths, dealing, group_index, seq_count):
    chosen = lax.dynamic_slice_in_dim(dealing, group_index * seq_count, seq_count)
    matches = chosen[:, None] == jnp.arange(lengths.shape[0], dtype=jnp.int32)[None, :]
    seq_lens = jnp.sum(jnp.where(matches, lengths[None, :], 0), axis=1)
    padded = (seq_lens + BLOCK - 1) // BLOCK * BLOCK
    starts = jnp.cumsum(padded) - padded
    return (starts, seq_lens)


def slots_for(number, span_row, half_span):
    rows = jnp.arange(number, dtype=jnp.int32)
    matches = (rows // half_span)[:, None] == jnp.arange(span_row.shape[0], dtype=jnp.int32)[None, :]
    span_of = jnp.sum(jnp.where(matches, span_row[None, :], 0), axis=1)
    return span_of * half_span + rows % half_span


def slot_facts(slots, starts, seq_lens):
    member = jnp.sum((slots[:, None] >= starts[None, :]).astype(jnp.int32), axis=1) - 1
    matches = member[:, None] == jnp.arange(starts.shape[0], dtype=jnp.int32)[None, :]
    anchor = jnp.sum(jnp.where(matches, starts[None, :], 0), axis=1)
    extent = jnp.sum(jnp.where(matches, seq_lens[None, :], 0), axis=1)
    position = slots - anchor
    return (slots, member, position, (position < extent).astype(jnp.int32))


def allowed(query_facts, key_facts):
    query_slot, query_member, query_position, query_valid = query_facts
    key_slot, key_member, key_position, key_valid = key_facts
    same_slot = query_slot[:, None] == key_slot[None, :]
    both_valid = (query_valid[:, None] == 1) & (key_valid[None, :] == 1)
    causal = (query_member[:, None] == key_member[None, :]) & (
        key_position[None, :] <= query_position[:, None]
    )
    return same_slot | both_valid & causal


class Plan:
    def __init__(self, n_dp, n_ctx, columns, hidden):
        self.n_dp, self.n_ctx = n_dp, n_ctx
        heads = columns // HEAD_DIM
        self.head_cuts = [i * heads // n_ctx for i in range(n_ctx + 1)]
        self.head_count = max(b - a for a, b in zip(self.head_cuts, self.head_cuts[1:]))
        self.head_width = self.head_count * HEAD_DIM
        self.unit_cuts = [i * hidden // n_ctx for i in range(n_ctx + 1)]
        units = max(b - a for a, b in zip(self.unit_cuts, self.unit_cuts[1:]))
        self.unit_width = (units + LANES - 1) // LANES * LANES


def cut_windows(weight, cuts, width):
    pieces = []
    for first, last in zip(cuts, cuts[1:]):
        pieces.append(jnp.pad(weight[:, first:last], ((0, 0), (0, width - (last - first)))))
    return jnp.stack(pieces)


def join_windows(windows, cuts):
    return jnp.concatenate(
        [windows[i, :, : last - first] for i, (first, last) in enumerate(zip(cuts, cuts[1:]))], axis=1
    )


def spread_weights(blocks):
    return lax.all_gather(blocks.reshape(-1, blocks.shape[-1]), "dp", axis=0, tiled=True)


def reduce_grads(full, n_ctx):
    own = lax.psum_scatter(full, "dp", scatter_dimension=0, tiled=True)
    return own.reshape(n_ctx, -1, own.shape[-1])


def gather_rows(piece):
    return lax.all_gather(piece, ("ctx", "tensor"), axis=0, tiled=True)


def scatter_rows(partial_sum):
    return lax.psum_scatter(
        partial_sum.astype(jnp.bfloat16), ("ctx", "tensor"), scatter_dimension=0, tiled=True
    ).astype(jnp.float32)


SLOT = 16
SKEW = 3


def place():
    return lax.axis_index("dp"), lax.axis_index("ctx"), lax.axis_index("tensor")


def slot_rows(base, index):
    return pl.ds(pl.multiple_of(base + index * SLOT, SLOT), SLOT)


def send(src, dst, send_sem, recv_sem, target):
    return pltpu.make_async_remote_copy(
        src_ref=src, dst_ref=dst, send_sem=send_sem, recv_sem=recv_sem, device_id=target, device_id_type=MESH
    )


def greet(d, c, t):
    barrier = pltpu.get_barrier_semaphore()
    for other in ((d, c, 1 - t), (d, c ^ 1, t), (d, c ^ 2, t), (d, c ^ 3, t)):
        pl.semaphore_signal(barrier, inc=1, device_id=other, device_id_type=MESH)
    pl.semaphore_wait(barrier, 4)


class Exchange:
    semaphores = 7

    @staticmethod
    def result(source):
        return jax.ShapeDtypeStruct(source.shape, source.dtype)

    def __init__(self, source, result, sems):
        d, c, t = place()
        self.own = pltpu.make_async_copy(source.at[c], result.at[c], sems.at[6])
        self.copies = [
            send(source.at[c ^ k], result.at[c], sems.at[k - 1], sems.at[k + 2], (d, c ^ k, t)) for k in (3, 2, 1)
        ]

    def start(self):
        for copy in self.copies:
            copy.start()
        self.own.start()

    def finish(self):
        for copy in self.copies:
            copy.wait()
        self.own.wait()


class Collect:
    semaphores = 13

    @staticmethod
    def result(source):
        return jax.ShapeDtypeStruct((4 * source.shape[0], source.shape[1]), source.dtype)

    def __init__(self, source, result, sems):
        d, c, t = place()
        block = source.shape[0]
        half = block // 2

        def piece(chip, core):
            return pl.ds(pl.multiple_of(chip * block + core * half, half), half)

        self.own = pltpu.make_async_copy(source, result.at[pl.ds(pl.multiple_of(c * block, block), block)], sems.at[12])
        mine = source.at[pl.ds(pl.multiple_of(t * half, half), half)]
        self.copies, self.onward = [], []
        for k in (3, 2, 1):
            self.copies.append(
                send(mine, result.at[piece(c, t)], sems.at[k - 1], sems.at[k + 2], (d, c ^ k, t))
            )
            there = result.at[piece(c ^ k, t)]
            self.onward.append(send(there, there, sems.at[k + 5], sems.at[k + 8], (d, c, 1 - t)))

    def start(self):
        for copy in self.copies:
            copy.start()
        self.own.start()

    def finish(self):
        for copy, onward in zip(self.copies, self.onward):
            copy.wait_recv()
            onward.start()
        for copy, onward in zip(self.copies, self.onward):
            copy.wait_send()
            onward.wait()
        self.own.wait()


def make_jobs(kinds, sources, results, sem_refs):
    return [kind(*refs) for kind, *refs in zip(kinds, sources, results, sem_refs)]


def jobs_kernel(kinds, *refs):
    n = len(kinds)
    greet(*place())
    jobs = make_jobs(kinds, refs[:n], refs[n : 2 * n], refs[2 * n :])
    for job in jobs:
        job.start()
    for job in jobs:
        job.finish()


def jobs_call(number, jobs):
    hbm = pl.BlockSpec(memory_space=pl.ANY)
    kinds = [kind for kind, _ in jobs]
    return pl.pallas_call(
        functools.partial(jobs_kernel, kinds),
        name="moves",
        out_shape=tuple(kind.result(source) for kind, source in jobs),
        in_specs=[hbm] * len(jobs),
        out_specs=tuple([hbm] * len(jobs)),
        scratch_shapes=[pltpu.SemaphoreType.DMA((kind.semaphores,)) for kind in kinds],
        compiler_params=pltpu.CompilerParams(collective_id=number, has_side_effects=True),
        cost_estimate=pl.CostEstimate(flops=10**9, bytes_accessed=100 * 10**6, transcendentals=0),
    )(*[source for _, source in jobs])


def line_kernel(settle, with_gather, n_settle_in, n_settle_out, kinds, *refs):
    n_jobs = len(kinds)
    partial_ref, refs = refs[0], refs[1:]
    settle_in, refs = refs[:n_settle_in], refs[n_settle_in:]
    job_sources, refs = refs[:n_jobs], refs[n_jobs:]
    settle_out, refs = refs[:n_settle_out], refs[n_settle_out:]
    if with_gather:
        whole_ref, refs = refs[0], refs[1:]
    job_results, refs = refs[:n_jobs], refs[n_jobs:]
    acc_up, acc_down, in_up, in_down, sib, stage, send_sems, sib_sems, up_sems, down_sems, back_up, back_down = refs[:12]
    whole_sems = refs[12]
    d, c, t = place()
    block = acc_up.shape[0]
    slots = block // SLOT
    sibling, above, below = (d, c, 1 - t), (d, c + 1, t), (d, c - 1, t)
    down_base, up_base = t * block, (2 + t) * block
    low, high = c > 0, c < 3

    greet(d, c, t)
    half = block // 2
    for part in range(2):
        for which, base in ((0, (1 - t) * block), (1, (3 - t) * block)):
            rows = pl.ds(pl.multiple_of(base + part * half, half), half)
            copy = send(
                partial_ref.at[rows],
                sib.at[which, pl.ds(part * half, half)],
                send_sems.at[0],
                sib_sems.at[which, part],
                sibling,
            )
            copy.start()
    middle = low & high
    jobs = make_jobs(kinds, job_sources, job_results, refs[13:])
    for job in jobs:
        job.start()

    @pl.when(middle)
    def _():
        for ref in settle_out:
            ref[...] = jnp.zeros(ref.shape, ref.dtype)

    def own_term(which, base, index):
        @pl.when(index % (slots // 2) == 0)
        def _():
            pltpu.make_async_copy(
                sib.at[which, pl.ds(0, half)], sib.at[which, pl.ds(0, half)], sib_sems.at[which, index // (slots // 2)]
            ).wait()

    def chain(index, which, base, first, last, into, acc, recv_sems, send_sem, target, back_target, back_sems):
        rows = slot_rows(0, index)
        own = slot_rows(base, index)

        @pl.when((index >= 0) & (index < slots))
        def _():
            own_term(which, base, index)

            def term():
                return partial_ref[own].astype(jnp.float32) + sib[which, rows].astype(jnp.float32)

            def pass_on(total):
                acc[rows] = total.astype(jnp.bfloat16)
                send(acc.at[rows], into.at[rows], send_sem, recv_sems.at[index], target).start()

            @pl.when(first)
            def _():
                pass_on(term())

            @pl.when(jnp.logical_not(first))
            def _():
                pltpu.make_async_copy(into.at[rows], into.at[rows], recv_sems.at[index]).wait()

            @pl.when(middle)
            def _():
                pass_on(term() + into[rows].astype(jnp.float32))

            @pl.when(last)
            def _():
                total = term() + into[rows].astype(jnp.float32)
                value = settle(total, rows, settle_in, settle_out)
                if with_gather:
                    stage[rows] = value
                    whole_ref[own] = value
                    send(stage.at[rows], whole_ref.at[own], send_sems.at[3], back_sems.at[index], back_target).start()
                    send(stage.at[rows], whole_ref.at[own], send_sems.at[5], whole_sems.at[which], sibling).start()

    def back(index, which, base, reached, more, back_sems, target):
        own = slot_rows(base, index)

        @pl.when((index >= 0) & (index < slots) & reached)
        def _():
            pltpu.make_async_copy(whole_ref.at[own], whole_ref.at[own], back_sems.at[index]).wait()

            @pl.when(more)
            def _():
                send(whole_ref.at[own], whole_ref.at[own], send_sems.at[4], back_sems.at[index], target).start()

            send(whole_ref.at[own], whole_ref.at[own], send_sems.at[5], whole_sems.at[which], sibling).start()

    def step(j, carry):
        chain(j - SKEW * c, 1, up_base, c == 0, c == 3, in_up, acc_up, up_sems, send_sems.at[1], above, below, back_down)
        chain(j - SKEW * (3 - c), 0, down_base, c == 3, c == 0, in_down, acc_down, down_sems, send_sems.at[2], below, above, back_up)
        if with_gather:
            back(j - SKEW * (6 - c), 1, up_base, high, low, back_down, below)
            back(j - SKEW * (3 + c), 0, down_base, low, high, back_up, above)
        return carry

    lax.fori_loop(0, slots + SKEW * (6 if with_gather else 3), step, 0)

    def drain(ref, sem):
        pltpu.make_async_copy(ref, ref, sem).wait()

    drain(sib, send_sems.at[0])

    @pl.when(high)
    def _():
        drain(acc_up, send_sems.at[1])

    @pl.when(low)
    def _():
        drain(acc_down, send_sems.at[2])

    if with_gather:
        up_rows = pl.ds(pl.multiple_of(up_base, block), block)
        down_rows = pl.ds(pl.multiple_of(down_base, block), block)
        other_up = pl.ds(pl.multiple_of((3 - t) * block, block), block)
        other_down = pl.ds(pl.multiple_of((1 - t) * block, block), block)

        @pl.when(jnp.logical_not(middle))
        def _():
            drain(stage, send_sems.at[3])

        @pl.when(middle)
        def _():
            drain(whole_ref.at[up_rows], send_sems.at[4])
            drain(whole_ref.at[down_rows], send_sems.at[4])

        drain(whole_ref.at[up_rows], send_sems.at[5])
        drain(whole_ref.at[down_rows], send_sems.at[5])
        drain(whole_ref.at[other_up], whole_sems.at[1])
        drain(whole_ref.at[other_down], whole_sems.at[0])

    for job in jobs:
        job.finish()


def line_call(name, number, settle, partial_sum, settle_in, settle_out, with_gather, jobs):
    rows, width = partial_sum.shape
    block = rows // 4
    outs = list(settle_out)
    if with_gather:
        outs.append(jax.ShapeDtypeStruct((rows, width), jnp.bfloat16))
    vmem = pl.BlockSpec(memory_space=pltpu.VMEM)
    hbm = pl.BlockSpec(memory_space=pl.ANY)
    kinds = [kind for kind, _ in jobs]
    piece = pltpu.VMEM((block, width), jnp.bfloat16)
    dma = pltpu.SemaphoreType.DMA
    slots = block // SLOT
    return pl.pallas_call(
        functools.partial(line_kernel, settle, with_gather, len(settle_in), len(settle_out), kinds),
        name=name,
        out_shape=tuple(outs) + tuple(kind.result(source) for kind, source in jobs),
        in_specs=[vmem] * (1 + len(settle_in)) + [hbm] * len(jobs),
        out_specs=tuple([vmem] * len(outs) + [hbm] * len(jobs)),
        scratch_shapes=[
            piece,
            piece,
            piece,
            piece,
            pltpu.VMEM((2, block, width), jnp.bfloat16),
            piece,
            dma((6,)),
            dma((2, 2)),
            dma((slots,)),
            dma((slots,)),
            dma((slots,)),
            dma((slots,)),
            dma((2,)),
        ]
        + [dma((kind.semaphores,)) for kind in kinds],
        compiler_params=pltpu.CompilerParams(
            collective_id=number, has_side_effects=True, vmem_limit_bytes=40 * 2**20
        ),
        cost_estimate=pl.CostEstimate(flops=10**9, bytes_accessed=100 * 10**6, transcendentals=0),
    )(partial_sum, *settle_in, *[source for _, source in jobs])


def settle_forward(total, rows, ins, outs):
    residual_ref, gain_ref = ins
    value = residual_ref[rows] + depth_scale * total
    outs[0][rows] = value
    inverse = lax.rsqrt(jnp.mean(value * value, axis=-1, keepdims=True) + eps_norm)
    return (value * inverse * gain_ref[...]).astype(jnp.bfloat16)


def settle_last(total, rows, ins, outs):
    outs[0][rows] = ins[0][rows] + depth_scale * total
    return None


def settle_backward(total, rows, ins, outs):
    values_ref, grad_ref, gain_ref = ins
    grad_out, gain_grad = outs
    value = values_ref[rows]
    inverse = lax.rsqrt(jnp.mean(value * value, axis=-1, keepdims=True) + eps_norm)
    scaled = value * inverse
    contribution = jnp.sum(total * scaled, axis=0, keepdims=True)

    first = rows.start == 0

    @pl.when(first)
    def _():
        gain_grad[...] = contribution

    @pl.when(jnp.logical_not(first))
    def _():
        gain_grad[...] += contribution

    grad_scaled = total * gain_ref[...]
    grad = grad_ref[rows] + inverse * (
        grad_scaled - scaled * jnp.mean(grad_scaled * scaled, axis=-1, keepdims=True)
    )
    grad_out[rows] = grad
    return (depth_scale * grad).astype(jnp.bfloat16)


class LineComm:
    def __init__(self):
        self.number = 0

    def next_number(self):
        self.number += 1
        return self.number

    def moves(self, *jobs):
        return jobs_call(self.next_number(), jobs)

    def own_rows(self, whole):
        block = whole.shape[0] // 4
        _, c, t = place()
        return lax.dynamic_slice_in_dim(whole, (jnp.where(c >= 2, 2, 0) + t) * block, block, 0)

    def forward(self, partial_sum, residual, gain, jobs):
        value, normed, *moved = line_call(
            "forward_line",
            self.next_number(),
            settle_forward,
            partial_sum,
            [residual, gain],
            [jax.ShapeDtypeStruct(residual.shape, jnp.float32)],
            True,
            jobs,
        )
        return value, normed, moved

    def last(self, partial_sum, residual, jobs):
        value, *moved = line_call(
            "last_line",
            self.next_number(),
            settle_last,
            partial_sum,
            [residual],
            [jax.ShapeDtypeStruct(residual.shape, jnp.float32)],
            False,
            jobs,
        )
        return value, moved

    def backward(self, partial_sum, values, grad_rows, gain, with_gather, jobs):
        outs = line_call(
            "backward_line",
            self.next_number(),
            settle_backward,
            partial_sum,
            [values, grad_rows, gain],
            [jax.ShapeDtypeStruct(values.shape, jnp.float32), jax.ShapeDtypeStruct(gain.shape, jnp.float32)],
            with_gather,
            jobs,
        )
        grad, gain_grad = outs[:2]
        return grad, gain_grad, outs[2] if with_gather else None, outs[3 if with_gather else 2 :]

    def deliver(self, rows):
        block = rows.shape[0]
        _, c, t = place()
        moved = lax.ppermute(rows, "ctx", [(0, 1), (3, 2)])
        mine = jnp.where((c == 0) | (c == 3), rows, moved)
        pair = lax.all_gather(mine, "tensor", axis=0, tiled=False)
        pick = jnp.where((c == 0) | (c == 2), 0, 1)
        return lax.dynamic_index_in_dim(pair, pick, 0, keepdims=False)


class PlainComm:
    def moves(self, *jobs):
        return tuple(
            lax.all_to_all(source, "ctx", 0, 0, tiled=False)
            if kind is Exchange
            else lax.all_gather(source, "ctx", axis=0, tiled=True)
            for kind, source in jobs
        )

    def own_rows(self, whole):
        _, c, t = place()
        share = whole.shape[0] // (lax.axis_size("ctx") * lax.axis_size("tensor"))
        return lax.dynamic_slice_in_dim(whole, (c * lax.axis_size("tensor") + t) * share, share, 0)

    def forward(self, partial_sum, residual, gain, jobs):
        value = residual + depth_scale * scatter_rows(partial_sum)
        return value, gather_rows((rms_parts(value)[0] * gain).astype(jnp.bfloat16)), self.moves(*jobs)

    def last(self, partial_sum, residual, jobs):
        return residual + depth_scale * scatter_rows(partial_sum), self.moves(*jobs)

    def backward(self, partial_sum, values, grad_rows, gain, with_gather, jobs):
        gain_grad, from_norm = norm_backward(values, gain, scatter_rows(partial_sum))
        grad = grad_rows + from_norm
        gathered = gather_rows((depth_scale * grad).astype(jnp.bfloat16)) if with_gather else None
        return grad, gain_grad, gathered, self.moves(*jobs)

    def deliver(self, rows):
        return lax.all_gather(rows, "tensor", axis=0, tiled=True)


def outer_kernel(*refs):
    out_ref, first = refs[-1], 0
    for left, right in zip(refs[:-1:2], refs[1:-1:2]):
        last = first + right.shape[1]
        out_ref[:, first:last] = outer_rows(left[...], right[...]).astype(out_ref.dtype)
        first = last


def outer_sums(*pairs):
    rows, width = pairs[0][0].shape
    columns = sum(right.shape[1] for _, right in pairs)
    tile = 256
    specs, operands = [], []
    for left, right in pairs:
        specs += [
            pl.BlockSpec((rows, tile), lambda i: (0, i)),
            pl.BlockSpec(right.shape, lambda i: (0, 0)),
        ]
        operands += [left, right]
    return pl.pallas_call(
        outer_kernel,
        name="outer_sums",
        grid=(width // tile,),
        out_shape=jax.ShapeDtypeStruct((width, columns), jnp.bfloat16),
        in_specs=specs,
        out_specs=pl.BlockSpec((tile, columns), lambda i: (i, 0)),
        compiler_params=pltpu.CompilerParams(vmem_limit_bytes=40 * 2**20),
        cost_estimate=pl.CostEstimate(
            flops=2 * rows * width * columns, bytes_accessed=2 * (rows + width) * columns, transcendentals=0
        ),
    )(*operands)


def attention_forward(query, key, value, bias):
    scores = jnp.einsum("qhd,khd->hqk", query, key, preferred_element_type=jnp.float32) * score_scale
    scores = scores + bias[None]
    top = jnp.max(scores, axis=-1, keepdims=True)
    terms = jnp.exp(scores - top)
    probs = terms / jnp.sum(terms, axis=-1, keepdims=True)
    attended = jnp.einsum(
        "hqk,khd->qhd", probs.astype(jnp.bfloat16), value, preferred_element_type=jnp.float32
    )
    return attended, probs


def attention_backward(query, key, value, probs, grad_out):
    grad_probs = jnp.einsum("qhd,khd->hqk", grad_out, value, preferred_element_type=jnp.float32)
    delta = jnp.sum(probs * grad_probs, axis=-1, keepdims=True)
    grad_scores = (probs * (grad_probs - delta) * score_scale).astype(jnp.bfloat16)
    grad_query = jnp.einsum("hqk,khd->qhd", grad_scores, key, preferred_element_type=jnp.float32)
    grad_key = jnp.einsum("hqk,qhd->khd", grad_scores, query, preferred_element_type=jnp.float32)
    grad_value = jnp.einsum(
        "hqk,qhd->khd", probs.astype(jnp.bfloat16), grad_out, preferred_element_type=jnp.float32
    )
    return grad_query, grad_key, grad_value


def forward_attention(normed, weight, plan, bias, tables):
    width = plan.head_width
    rows = normed.shape[0]
    head_shape = (rows, plan.head_count, HEAD_DIM)
    mixed = times(normed, weight[:, : 3 * width])
    query = rotate(mixed[:, :width].reshape(head_shape), tables, 1.0).astype(jnp.bfloat16)
    key = rotate(mixed[:, width : 2 * width].reshape(head_shape), tables, 1.0).astype(jnp.bfloat16)
    value = mixed[:, 2 * width :].reshape(head_shape).astype(jnp.bfloat16)
    attended, probs = attention_forward(query, key, value, bias)
    attended = attended.reshape(rows, width).astype(jnp.bfloat16)
    partial_sum = times_transposed(attended, weight[:, 3 * width :]).astype(jnp.bfloat16)
    return partial_sum, (normed, query, key, value, probs, attended)


def forward_feed(normed, weight, plan):
    units = plan.unit_width
    both = times(normed, weight[:, : 2 * units])
    gating, upward = both[:, :units], both[:, units:]
    activated = (jax.nn.silu(gating) * upward).astype(jnp.bfloat16)
    partial_sum = times_transposed(activated, weight[:, 2 * units :]).astype(jnp.bfloat16)
    return partial_sum, (normed, gating, upward, activated)


def backward_feed(down_grad, weight, record, plan):
    normed, gating, upward, activated = record
    units = plan.unit_width
    grad_act = times(down_grad, weight[:, 2 * units :])
    sigmoid_gate = jax.nn.sigmoid(gating)
    grad_gating = grad_act * upward * sigmoid_gate * (1.0 + gating * (1.0 - sigmoid_gate))
    grad_upward = grad_act * gating * sigmoid_gate
    grad_both = jnp.concatenate([grad_gating, grad_upward], axis=1).astype(jnp.bfloat16)
    partial_sum = times_transposed(grad_both, weight[:, : 2 * units]).astype(jnp.bfloat16)
    return partial_sum, ((normed, grad_both), (down_grad, activated))


def backward_attention(branch_grad, weight, record, plan, tables):
    normed, query, key, value, probs, attended = record
    width = plan.head_width
    rows = normed.shape[0]
    grad_mixed = times(branch_grad, weight[:, 3 * width :]).astype(jnp.bfloat16)
    grad_query, grad_key, grad_value = attention_backward(
        query, key, value, probs, grad_mixed.reshape(query.shape)
    )
    grad_all = jnp.concatenate(
        [
            rotate(grad_query, tables, -1.0).reshape(rows, width),
            rotate(grad_key, tables, -1.0).reshape(rows, width),
            grad_value.reshape(rows, width),
        ],
        axis=1,
    ).astype(jnp.bfloat16)
    partial_sum = times_transposed(grad_all, weight[:, : 3 * width]).astype(jnp.bfloat16)
    return partial_sum, ((normed, grad_all), (branch_grad, attended))


def body(
    inputs,
    cotangent,
    lengths,
    dealing,
    span_table,
    prenorm_gain,
    query_weight,
    keys_weight,
    values_weight,
    project_weight,
    postnorm_gain,
    gating_weight,
    upward_weight,
    downward_weight,
):
    n_dp, n_ctx, n_ten = lax.axis_size("dp"), lax.axis_size("ctx"), lax.axis_size("tensor")
    plan = Plan(n_dp, n_ctx, query_weight.shape[2], gating_weight.shape[2])
    own_rows = inputs.shape[0]
    half_span = own_rows // 2
    share = own_rows // n_ten
    group_index = lax.axis_index("dp")
    core = lax.axis_index("tensor")
    seq_count = lengths.shape[0] // n_dp
    starts, seq_lens = group_layout(lengths, dealing, group_index, seq_count)
    span_row = lax.dynamic_index_in_dim(span_table, group_index, 0, keepdims=False)
    facts = slot_facts(slots_for(own_rows * n_ctx, span_row, half_span), starts, seq_lens)
    tables = rope_tables(facts[2], HEAD_DIM // 2)
    bias = jnp.where(allowed(facts, facts), 0.0, masked_score)

    gains = lax.all_gather(
        jnp.concatenate([prenorm_gain, postnorm_gain], axis=0), ("dp", "ctx"), axis=1, tiled=True
    ).astype(jnp.float32)
    comm = LineComm() if (n_dp, n_ctx, n_ten) == (4, 4, 2) else PlainComm()
    head_cuts = [cut * HEAD_DIM for cut in plan.head_cuts]

    def attention_windows(layer):
        weights = (query_weight[layer], keys_weight[layer], values_weight[layer], project_weight[layer].T)
        return jnp.concatenate([cut_windows(weight, head_cuts, plan.head_width) for weight in weights], axis=2)

    def feed_windows(layer):
        weights = (gating_weight[layer], upward_weight[layer], downward_weight[layer].T)
        return jnp.concatenate([cut_windows(weight, plan.unit_cuts, plan.unit_width) for weight in weights], axis=2)

    front = [gains[layer : layer + 1] for layer in range(LAYERS)]
    behind = [gains[LAYERS + layer : LAYERS + layer + 1] for layer in range(LAYERS)]
    attention_weights, feed_weights = [None] * LAYERS, [None] * LAYERS
    attention_records, feed_records, middles = [None] * LAYERS, [None] * LAYERS, [None] * LAYERS
    starts_of = [None] * LAYERS

    blocks, inputs_whole = comm.moves((Exchange, attention_windows(0)), (Collect, inputs))
    attention_weights[0] = spread_weights(blocks)
    residual = comm.own_rows(inputs_whole).astype(jnp.float32)
    normed = (rms_parts(inputs_whole.astype(jnp.float32))[0] * front[0]).astype(jnp.bfloat16)
    windows, normed = lax.optimization_barrier((feed_windows(0), normed))
    (blocks,) = comm.moves((Exchange, windows))
    feed_weights[0] = spread_weights(blocks)
    for layer in range(LAYERS):
        starts_of[layer] = residual
        more = layer + 1 < LAYERS
        partial_sum, attention_records[layer] = forward_attention(
            normed, attention_weights[layer], plan, bias, tables
        )
        jobs = [(Exchange, attention_windows(layer + 1))] if more else [(Collect, cotangent)]
        hidden, normed, moved = comm.forward(partial_sum, residual, behind[layer], jobs)
        if more:
            attention_weights[layer + 1] = spread_weights(moved[0])
        else:
            cotangent_whole = moved[0]
        middles[layer] = hidden
        partial_sum, feed_records[layer] = forward_feed(normed, feed_weights[layer], plan)
        if more:
            jobs = [(Exchange, feed_windows(layer + 1))]
            residual, normed, moved = comm.forward(partial_sum, hidden, front[layer + 1], jobs)
            feed_weights[layer + 1] = spread_weights(moved[0])
        else:
            residual, _ = comm.last(partial_sum, hidden, [])
    output = comm.deliver(residual.astype(jnp.bfloat16))

    grad_rows = comm.own_rows(cotangent_whole).astype(jnp.float32)
    down_grad = (depth_scale * cotangent_whole.astype(jnp.float32)).astype(jnp.bfloat16)
    gain_grads, attention_parts, feed_parts = [None] * LAYERS, [None] * LAYERS, [None] * LAYERS
    for layer in reversed(range(LAYERS)):
        more = layer > 0
        partial_sum, pairs = backward_feed(down_grad, feed_weights[layer], feed_records[layer], plan)
        feed_sums = reduce_grads(outer_sums(*pairs), n_ctx)
        jobs = [] if layer + 1 == LAYERS else [(Exchange, feed_parts[layer + 1])]
        grad_rows, gain_back, branch_grad, moved = comm.backward(
            partial_sum, middles[layer], grad_rows, behind[layer], True, jobs
        )
        if moved:
            feed_parts[layer + 1] = moved[0]
        feed_parts[layer] = feed_sums
        partial_sum, pairs = backward_attention(
            branch_grad, attention_weights[layer], attention_records[layer], plan, tables
        )
        attention_sums = reduce_grads(outer_sums(*pairs), n_ctx)
        jobs = [] if layer + 1 == LAYERS else [(Exchange, attention_parts[layer + 1])]
        grad_rows, gain_front, down_grad, moved = comm.backward(
            partial_sum, starts_of[layer], grad_rows, front[layer], more, jobs
        )
        if moved:
            attention_parts[layer + 1] = moved[0]
        attention_parts[layer] = attention_sums
        gain_grads[layer] = (gain_front, gain_back)
    (feed_parts[0],) = comm.moves((Exchange, feed_parts[0]))
    (attention_parts[0],) = comm.moves((Exchange, attention_parts[0]))
    grad_inputs = comm.deliver(grad_rows.astype(jnp.bfloat16)).astype(jnp.float32)
    gain_sums = jnp.concatenate([pair[which] for which in range(2) for pair in gain_grads], axis=0)
    gain_sums = lax.psum_scatter(
        lax.psum(gain_sums, "tensor"), ("dp", "ctx"), scatter_dimension=1, tiled=True
    )

    def spread(parts, index, width, cuts, flip):
        out = []
        for part in parts:
            whole = join_windows(part[:, :, index * width : (index + 1) * width], cuts)
            out.append((whole.T if flip else whole).astype(jnp.float32))
        return jnp.stack(out)

    attention_out = [
        spread(attention_parts, i, plan.head_width, head_cuts, i == 3) for i in range(4)
    ]
    feed_out = [spread(feed_parts, i, plan.unit_width, plan.unit_cuts, i == 2) for i in range(3)]
    return (
        output,
        grad_inputs,
        gain_sums[:LAYERS],
        *attention_out,
        gain_sums[LAYERS:],
        *feed_out,
    )


def solution(mesh):
    rows = P(("dp", "ctx"), None)
    gain = P(None, ("dp", "ctx"))
    wide = P(None, ("dp", "ctx"), "tensor")
    tall = P(None, "tensor", ("dp", "ctx"))
    weights = (gain, wide, wide, wide, tall, gain, wide, wide, tall)
    return jax.shard_map(
        body,
        mesh=mesh,
        in_specs=(rows, rows, P(), P(), P()) + weights,
        out_specs=(rows, rows) + weights,
        check_vma=False,
    )
```

time: 6070 us -> 1220 us (0.20)
  waiting for transfers between devices: 5430 us -> 132 us
  Pallas kernels: 0 us -> 727 us
  matrix products: 349 us -> 149 us
  blocking collectives: 159 us -> 42.8 us
    reduce_scatter x14 -> x4, waiting for transfers between devices: 3630 us -> 69 us  [reduce_grads(): own = lax.psum_scatter(full, 'dp', scatter_dimension=0, tiled=True)]
    all_gather x18 -> x6, waiting for transfers between devices: 1630 us -> 25 us  [the longest x4 18.7 us: spread_weights(): lax.all_gather(blocks.reshape(-1, blocks.shape[-1]), 'dp', axis=0, tiled=...]
    pallas_call x0 -> x16, Pallas kernels: none -> 727 us  [the longest x8 475 us: line_call(): pl.pallas_call(functools.partial(line_kernel, settle, with_gather, len(se...]
    unnamed x2 -> x0, blocking collectives: 159 us -> none
    dot_general x40 -> x18, matrix products: 255 us -> 96.8 us  [the longest x8 44.4 us: times(): return jnp.dot(left, right, preferred_element_type=jnp.float32)]
    psum x7 -> x0, waiting for transfers between devices: 91.4 us -> none  [the longest x3 54.3 us: input_total(): lax.psum(partial_sum.astype(jnp.bfloat16), 'tensor').astype(jnp.float32)]
  transfers between devices with their start and end apart: 43 -> 13, of which waited for: 41 -> 5; matrix products, arithmetic and copies ran while one was open for 5% -> 19% of each run, Pallas kernels for 0% -> 51%
where the time goes in v1:
time: 1220 us; the launch traced here: 1210 us
  Pallas kernels  727 us (60%)
  matrix products  149 us (12%)
  waiting for transfers between devices  132 us (11%)
  local copies, waits for them, and re-layouts  99.1 us (8%)
  other arithmetic  43.8 us (4%)
  blocking collectives  42.8 us (4%)
  between operations  16.5 us (1%)
    pallas_call x8, Pallas kernels, line_call(): pl.pallas_call(functools.partial(line_kernel, settle, with_gather, len(se...  475 us
    pallas_call x4, Pallas kernels, jobs_call(): pl.pallas_call(functools.partial(jobs_kernel, kinds), name='moves', out_s...  220 us
    reduce_scatter x4, waiting for transfers between devices, reduce_grads(): own = lax.psum_scatter(full, 'dp', scatter_dimension=0, tiled=True)  69 us
    dot_general x8, matrix products, times(): return jnp.dot(left, right, preferred_element_type=jnp.float32)  44.4 us
    unnamed x266, local copies, waits for them, and re-layouts  43.5 us
    dot_general x8, matrix products, times_transposed(): lax.dot_general(left, right, (((1,), (1,)), ((), ())), preferred_element_...  43.4 us
    all_gather x1, blocking collectives, body(): lax.all_gather(jnp.concatenate([prenorm_gain, postnorm_gain], axis=0), ('...  40.4 us
    pallas_call x4, Pallas kernels, outer_sums(): pl.pallas_call(outer_kernel, name='outer_sums', grid=(width // tile,), ou...  32 us
  transfers between devices with their start and end apart: 13, of which 5 were waited for; matrix products, arithmetic and copies ran while one was open for 19% of the time, Pallas kernels for 51%

profile of v1, /device:TPU:0, one launch (start us, length us, event | category | flops | bytes accessed | tf_op | source)
XLA Modules:
  0.0 1214.5 jit_solution(3814018682057460532)
XLA Ops:
  14.0 65.4 %moves.4 = (bf16[4,144,1280]{2,1,0:T(8,128)(2,1)}, bf16[512,2304]{1,0:T(8,128)(2,1)}) custom-call(bf16[4,144,1280]{2,1,0:T(8,128)(2,1)} %concatenate.179.refs_0_, bf16[128,2304]{1,0:T(8,128)(2,1)} %refs_1_.1), custom_call_target="tpu_custom_call" | custom-call | flops 1000000000 | bytes 100000000 | tf_op jit(solution)/shard_map/moves/pallas_call | solution.py:264
  79.5 40.4 %all-gather.2 = bf16[16,144,4]{1,2,0:T(4,128)(2,1)S(1)} all-gather(bf16[1,144,4]{1,2,0:T(4,128)(2,1)S(1)} %maximum_bitcast_fusion), channel_id=1, replica_groups=mesh['dp'=4,'ctx'=4,'tensor'=2] {'dp','ctx'}, dimensions={0}, use_global_device_ids=true | all-gather | bytes 19584 | tf_op jit(solution)/shard_map/all_gather | solution.py:740
  130.0 55.4 %moves.5 = bf16[4,144,2304]{2,1,0:T(8,128)(2,1)} custom-call(bf16[4,144,2304]{2,1,0:T(8,128)(2,1)} %maximum_maximum_fusion.refs_0_), custom_call_target="tpu_custom_call" | custom-call | flops 1000000000 | bytes 100000000 | tf_op jit(solution)/shard_map/moves/pallas_call | solution.py:264
  222.1 65.4 %forward_line.3 = (f32[128,2304]{1,0:T(8,128)S(1)}, bf16[512,2304]{1,0:T(8,128)(2,1)S(1)}, bf16[4,144,1280]{2,1,0:T(8,128)(2,1)}) custom-call(bf16[512,2304]{1,0:T(8,128)(2,1)S(1)} %convolution_convert_fusion.5.refs_0_, f32[128,2304]{1,0:T(8,128)S(1)} %dynamic-slice_convert_fusion.1.refs_1_, f32[1,2304]{1,0:T(1,128)S(1)} %get-tuple-element.214.refs_2_.refs_3_, ...), custom_call_target="tpu_custom_call" | custom-call | flops 1000000000 | bytes 100000000 | tf_op jit(solution)/shard_map/forward_line/pallas_call | solution.py:433
  293.8 6.8 fusion.10
  306.8 90.8 %forward_line.4 = (f32[128,2304]{1,0:T(8,128)S(1)}, bf16[512,2304]{1,0:T(8,128)(2,1)S(1)}, bf16[4,144,2304]{2,1,0:T(8,128)(2,1)S(1)}) custom-call(bf16[512,2304]{1,0:T(8,128)(2,1)S(1)} %convolution_convert_fusion.4.refs_0_, f32[128,2304]{1,0:T(8,128)S(1)} %copy-done.10, f32[1,2304]{1,0:T(1,128)S(1)} %copy-done.42, ...), custom_call_target="tpu_custom_call" | custom-call | flops 1000000000 | bytes 100000000 | tf_op jit(solution)/shard_map/forward_line/pallas_call | solution.py:433
  420.0 62.6 %forward_line.5 = (f32[128,2304]{1,0:T(8,128)S(1)}, bf16[512,2304]{1,0:T(8,128)(2,1)S(1)}, bf16[512,2304]{1,0:T(8,128)(2,1)S(1)}) custom-call(bf16[512,2304]{1,0:T(8,128)(2,1)S(1)} %convolution_convert_fusion.3.refs_0_, f32[128,2304]{1,0:T(8,128)S(1)} %copy-done.13, f32[1,2304]{1,0:T(1,128)S(1)} %copy-done.43, bf16[128,2304]{1,0:T(8,128)(2,1)S(1)} %copy-done.41), custom_call_target="tpu_custom_call" | custom-call | flops 1000000000 | bytes 100000000 | tf_op jit(solution)/shard_map/forward_line/pallas_call | solution.py:433
  487.3 18.7 %all-gather.16.cloned.1.call-done = bf16[2304,2304]{1,0:T(8,128)(2,1)} async-done(((bf16[576,2304]{1,0:T(8,128)(2,1)}), bf16[2304,2304]{1,0:T(8,128)(2,1)}) %all-gather.16.cloned.1.call-update) | async-done | bytes 10616848 | tf_op jit(solution)/shard_map/all_gather | solution.py:139
  506.0 6.9 fusion.6
  520.1 9.4 outer_sums.4
  532.9 7.3 fusion.20.refs_0_
  540.2 42.2 %backward_line.4 = (f32[128,2304]{1,0:T(8,128)S(1)}, f32[1,2304]{1,0:T(1,128)S(1)}, bf16[512,2304]{1,0:T(8,128)(2,1)S(1)}) custom-call(bf16[512,2304]{1,0:T(8,128)(2,1)S(1)} %fusion.20.refs_0_, f32[128,2304]{1,0:T(8,128)S(1)} %get-tuple-element.48.refs_1_, f32[128,2304]{1,0:T(8,128)S(1)} %dynamic-slice_convert_fusion.refs_2_, f32[1,2304]{1,0:T(1,128)S(1)} %copy-done.43), custom_call_target="tpu_custom_call" | custom-call | flops 1000000000 | bytes 100000000 | tf_op jit(solution)/shard_map/backward_line/pallas_call | solution.py:433
  592.1 10.4 fusion.81
  602.5 8.9 fusion.84
  620.9 6.5 outer_sums.5
  634.4 27.2 %last_line.1 = f32[128,2304]{1,0:T(8,128)S(1)} custom-call(bf16[512,2304]{1,0:T(8,128)(2,1)S(1)} %convolution_convert_fusion.2.refs_0_, f32[128,2304]{1,0:T(8,128)S(1)} %get-tuple-element.48.refs_1_), custom_call_target="tpu_custom_call" | custom-call | flops 1000000000 | bytes 100000000 | tf_op jit(solution)/shard_map/last_line/pallas_call | solution.py:433
  668.7 43.5 %backward_line.5 = (f32[128,2304]{1,0:T(8,128)S(1)}, f32[1,2304]{1,0:T(1,128)S(1)}, bf16[512,2304]{1,0:T(8,128)(2,1)S(1)}) custom-call(bf16[512,2304]{1,0:T(8,128)(2,1)S(1)} %convolution_convert_fusion.1.refs_0_, f32[128,2304]{1,0:T(8,128)S(1)} %copy-done.13, f32[128,2304]{1,0:T(8,128)S(1)} %copy-done.36, f32[1,2304]{1,0:T(1,128)S(1)} %copy-done.42), custom_call_target="tpu_custom_call" | custom-call | flops 1000000000 | bytes 100000000 | tf_op jit(solution)/shard_map/backward_line/pallas_call | solution.py:433
  715.6 6.1 multiply_convert_fusion.4
  724.2 9.5 outer_sums.7
  733.8 7.4 fusion.17.refs_0_
  744.2 91.0 %backward_line.6 = (f32[128,2304]{1,0:T(8,128)S(1)}, f32[1,2304]{1,0:T(1,128)S(1)}, bf16[512,2304]{1,0:T(8,128)(2,1)S(1)}, bf16[4,144,2304]{2,1,0:T(8,128)(2,1)S(1)}) custom-call(bf16[512,2304]{1,0:T(8,128)(2,1)S(1)} %fusion.17.refs_0_, f32[128,2304]{1,0:T(8,128)S(1)} %copy-done.11, f32[128,2304]{1,0:T(8,128)S(1)} %copy-done.38, ...), custom_call_target="tpu_custom_call" | custom-call | flops 1000000000 | bytes 100000000 | tf_op jit(solution)/shard_map/backward_line/pallas_call | solution.py:433
  847.0 8.1 fusion.75
  855.1 8.1 fusion.78
  864.3 6.4 convolution_convert_fusion.refs_0_
  874.7 52.2 %backward_line.7 = (f32[128,2304]{1,0:T(8,128)S(1)}, f32[1,2304]{1,0:T(1,128)S(1)}, bf16[4,144,1280]{2,1,0:T(8,128)(2,1)S(1)}) custom-call(bf16[512,2304]{1,0:T(8,128)(2,1)S(1)} %copy-done.23, f32[128,2304]{1,0:T(8,128)S(1)} %copy-done.5, f32[128,2304]{1,0:T(8,128)S(1)} %copy-done.34, f32[1,2304]{1,0:T(1,128)S(1)} %copy-done.44, ...), custom_call_target="tpu_custom_call" | custom-call | flops 1000000000 | bytes 100000000 | tf_op jit(solution)/shard_map/backward_line/pallas_call | solution.py:433
  934.2 9.3 collective-permute-done.1
  948.8 6.5 outer_sums.6
  973.8 62.7 %moves.7 = bf16[4,144,2304]{2,1,0:T(8,128)(2,1)} custom-call(bf16[4,144,2304]{2,1,0:T(8,128)(2,1)} %bitcast.279), custom_call_target="tpu_custom_call" | custom-call | flops 1000000000 | bytes 100000000 | tf_op jit(solution)/shard_map/moves/pallas_call | solution.py:264
  1053.2 28.3 %reduce-scatter.16.cloned.1.call-done = f32[144,4]{1,0:T(8,128)} async-done(((f32[2304,4]{1,0:T(8,128)}), f32[144,4]{1,0:T(8,128)}) %reduce-scatter.16.cloned.1.call-update) | async-done | bytes 2320
  1085.5 6.2 all-gather.20.cloned.1.call-done
  1093.9 69.0 %reduce-scatter.12.cloned.1.call-done = bf16[576,1280]{1,0:T(8,128)(2,1)} async-done(((bf16[2304,1280]{1,0:T(8,128)(2,1)}), bf16[576,1280]{1,0:T(8,128)(2,1)}) %reduce-scatter.12.cloned.1.call-update) | async-done | bytes 1474576 | tf_op jit(solution)/shard_map/reduce_scatter | solution.py:143
  1162.9 36.3 %moves.6 = bf16[4,144,1280]{2,1,0:T(8,128)(2,1)} custom-call(bf16[4,144,1280]{2,1,0:T(8,128)(2,1)} %bitcast.309), custom_call_target="tpu_custom_call" | custom-call | flops 1000000000 | bytes 100000000 | tf_op jit(solution)/shard_map/moves/pallas_call | solution.py:264
  (457 shorter events, 223.1 us)
Async XLA Ops:
  7.2 191.7 %copy-start = (s32[4,8]{1,0:T(4,128)S(1)}, s32[4,8]{1,0:T(4,128)}, u32[]{:S(2)}) copy-start(s32[4,8]{1,0:T(4,128)} %param.18) | copy-start | bytes 388
  7.2 197.3 %all-gather.10.cloned.1.call-start = ((), (), s32[]{:S(2)}) async-start(), calls=%async_computation.5 | async-start | bytes 7372800 | tf_op jit(solution)/shard_map/all_gather | solution.py:139
  14.0 65.5 %copy-start.125 = (bf16[2,144]{1,0:T(2,128)(2,1)S(1)}, bf16[2,144]{1,0:T(2,128)(2,1)}, u32[]{:S(2)}) copy-start(bf16[2,144]{1,0:T(2,128)(2,1)} %param.24) | copy-start | bytes 1732
  14.0 65.5 %copy-start.126 = (bf16[2,144]{1,0:T(2,128)(2,1)S(1)}, bf16[2,144]{1,0:T(2,128)(2,1)}, u32[]{:S(2)}) copy-start(bf16[2,144]{1,0:T(2,128)(2,1)} %param.19) | copy-start | bytes 1732
  14.0 106.0 %copy-start.62 = (bf16[2,2880,144]{1,2,0:T(8,128)(2,1)S(1)}, bf16[2,2880,144]{1,2,0:T(8,128)(2,1)}, u32[]{:S(2)}) copy-start(bf16[2,2880,144]{1,2,0:T(8,128)(2,1)} %param.27) | copy-start | bytes 4976644
  79.4 214.4 %all-gather.12.cloned.1.call-start = ((), (), s32[]{:S(2)}) async-start(), calls=%async_computation.6 | async-start | bytes 13271040 | tf_op jit(solution)/shard_map/all_gather | solution.py:139
  127.7 76.8 %copy-start.6 = (bf16[512,2304]{1,0:T(8,128)(2,1)}, bf16[512,2304]{1,0:T(8,128)(2,1)S(1)}, u32[]{:S(2)}) copy-start(bf16[512,2304]{1,0:T(8,128)(2,1)S(1)} %fusion.16.refs_0_) | copy-start | bytes 7077892
  185.4 216.3 %all-gather.14.cloned.1.call-start = ((), (), s32[]{:S(2)}) async-start(), calls=%async_computation.7 | async-start | bytes 7372800 | tf_op jit(solution)/shard_map/all_gather | solution.py:139
  204.5 17.6 %copy-start.4 = (f32[128,2304]{1,0:T(8,128)}, f32[128,2304]{1,0:T(8,128)S(1)}, u32[]{:S(2)}) copy-start(f32[128,2304]{1,0:T(8,128)S(1)} %dynamic-slice_convert_fusion.1.refs_1_) | copy-start | bytes 3538948
  222.1 68.2 %copy-start.81 = (bf16[144,720]{1,0:T(8,128)(2,1)S(1)}, bf16[144,720]{1,0:T(8,128)(2,1)}, u32[]{:S(2)}) copy-start(bf16[144,720]{1,0:T(8,128)(2,1)} %get-tuple-element.143) | copy-start | bytes 622084
  222.1 68.2 %copy-start.80 = (bf16[144,720]{1,0:T(8,128)(2,1)S(1)}, bf16[144,720]{1,0:T(8,128)(2,1)}, u32[]{:S(2)}) copy-start(bf16[144,720]{1,0:T(8,128)(2,1)} %get-tuple-element.144) | copy-start | bytes 622084
  222.1 68.3 %copy-start.79 = (bf16[144,720]{1,0:T(8,128)(2,1)S(1)}, bf16[144,720]{1,0:T(8,128)(2,1)}, u32[]{:S(2)}) copy-start(bf16[144,720]{1,0:T(8,128)(2,1)} %get-tuple-element.142) | copy-start | bytes 622084
  222.1 68.3 %copy-start.84 = (bf16[144,720]{1,0:T(8,128)(2,1)S(1)}, bf16[144,720]{1,0:T(8,128)(2,1)}, u32[]{:S(2)}) copy-start(bf16[144,720]{1,0:T(8,128)(2,1)} %get-tuple-element.140) | copy-start | bytes 622084
  222.1 68.3 %copy-start.83 = (bf16[144,720]{1,0:T(8,128)(2,1)S(1)}, bf16[144,720]{1,0:T(8,128)(2,1)}, u32[]{:S(2)}) copy-start(bf16[144,720]{1,0:T(8,128)(2,1)} %get-tuple-element.141) | copy-start | bytes 622084
  222.1 68.4 %copy-start.82 = (bf16[144,720]{1,0:T(8,128)(2,1)S(1)}, bf16[144,720]{1,0:T(8,128)(2,1)}, u32[]{:S(2)}) copy-start(bf16[144,720]{1,0:T(8,128)(2,1)} %get-tuple-element.139) | copy-start | bytes 622084
  290.0 216.0 %all-gather.16.cloned.1.call-start = ((), (), s32[]{:S(2)}) async-start(), calls=%async_computation.8 | async-start | bytes 13271040 | tf_op jit(solution)/shard_map/all_gather | solution.py:139
  401.6 339.6 %reduce-scatter.8.cloned.1.call-start = ((), (), s32[]{:S(2)}) async-start(), calls=%async_computation.9 | async-start | bytes 13271040 | tf_op jit(solution)/shard_map/reduce_scatter | solution.py:143
  529.6 342.1 %reduce-scatter.10.cloned.1.call-start = ((), (), s32[]{:S(2)}) async-start(), calls=%async_computation.10 | async-start | bytes 7372800 | tf_op jit(solution)/shard_map/reduce_scatter | solution.py:143
  531.6 55.4 %slice-start = ((s8[5242880]{0:T(1024)(128)(4,1)}), s8[4194304]{0:T(1024)(128)(4,1)S(1)}, s32[]{:S(2)}) async-start(s8[5242880]{0:T(1024)(128)(4,1)} %bitcast.310), calls=%async_computation.16 | async-start | bytes 8388608
  532.9 54.2 %slice-start.1 = ((s8[5242880]{0:T(1024)(128)(4,1)}), s8[1048576]{0:T(1024)(128)(4,1)S(1)}, s32[]{:S(2)}) async-start(s8[5242880]{0:T(1024)(128)(4,1)} %bitcast.310), calls=%async_computation.17 | async-start | bytes 2097152
  630.0 327.9 %all-gather.18.cloned.1.call-start = ((), (), s32[]{:S(2)}) async-start(), calls=%async_computation.13 | async-start | bytes 1769472 | tf_op jit(solution)/shard_map/all_gather | solution.py:562
  661.7 52.9 %collective-permute-start = (bf16[128,2304]{1,0:T(8,128)(2,1)S(1)}, bf16[128,2304]{1,0:T(8,128)(2,1)S(1)}, u32[]{:S(2)}, u32[]{:S(2)}) collective-permute-start(bf16[128,2304]{1,0:T(8,128)(2,1)S(1)} %convert_element_type.335), channel_id=1, source_target_pairs={{0,2},{6,4},{1,3},{7,5},{8,10},{14,12},{9,11},{15,13},{16,18},{22,... | collective-permute-start | bytes 1769480 | tf_op jit(solution)/shard_map/ppermute | solution.py:560
  715.6 258.2 %reduce-scatter.14.cloned.1.call-start = ((), (), s32[]{:S(2)}) async-start(), calls=%async_computation.12 | async-start | bytes 13271040 | tf_op jit(solution)/shard_map/reduce_scatter | solution.py:143
  733.7 347.8 %reduce-scatter.16.cloned.1.call-start = ((), (), s32[]{:S(2)}) async-start(), calls=%async_computation.15 | async-start | bytes 1253376
  874.7 56.5 %copy-start.46 = (f32[1,2304]{1,0:T(1,128)S(1)}, f32[1,2304]{1,0:T(1,128)}, u32[]{:S(2)}) copy-start(f32[1,2304]{1,0:T(1,128)} %copy-done.45) | copy-start | bytes 27652
  874.7 56.5 %copy-start.48 = (f32[1,2304]{1,0:T(1,128)S(1)}, f32[1,2304]{1,0:T(1,128)}, u32[]{:S(2)}) copy-start(f32[1,2304]{1,0:T(1,128)} %copy-done.47) | copy-start | bytes 27652
  874.7 56.5 %copy-start.50 = (f32[1,2304]{1,0:T(1,128)S(1)}, f32[1,2304]{1,0:T(1,128)}, u32[]{:S(2)}) copy-start(f32[1,2304]{1,0:T(1,128)} %copy-done.49) | copy-start | bytes 27652
  929.0 16.9 %copy-start.7 = (bf16[512,2304]{1,0:T(8,128)(2,1)S(1)}, bf16[512,2304]{1,0:T(8,128)(2,1)}, u32[]{:S(2)}) copy-start(bf16[512,2304]{1,0:T(8,128)(2,1)} %copy-done.6) | copy-start | bytes 7077892
  929.0 14.5 %collective-permute-start.1 = (bf16[128,2304]{1,0:T(8,128)(2,1)}, bf16[128,2304]{1,0:T(8,128)(2,1)}, u32[]{:S(2)}, u32[]{:S(2)}) collective-permute-start(bf16[128,2304]{1,0:T(8,128)(2,1)} %convert_element_type.347), channel_id=1, source_target_pairs={{0,2},{6,4},{1,3},{7,5},{8,10},{14,12},{9,11},{15,13},{16,18},{22,... | collective-permute-start | bytes 1769480 | tf_op jit(solution)/shard_map/ppermute | solution.py:560
  934.1 157.7 %all-gather.20.cloned.1.call-start = ((), (), s32[]{:S(2)}) async-start(), calls=%async_computation.14 | async-start | bytes 1769472 | tf_op jit(solution)/shard_map/all_gather | solution.py:562
  944.4 218.5 %reduce-scatter.12.cloned.1.call-start = ((), (), s32[]{:S(2)}) async-start(), calls=%async_computation.11 | async-start | bytes 7372800 | tf_op jit(solution)/shard_map/reduce_scatter | solution.py:143
  1162.9 39.4 %copy-start.72 = (bf16[1,144,1152]{2,1,0:T(8,128)(2,1)S(1)}, bf16[1,144,1152]{2,1,0:T(8,128)(2,1)}, u32[]{:S(2)}) copy-start(bf16[1,144,1152]{2,1,0:T(8,128)(2,1)} %concatenate.197) | copy-start | bytes 995332
  (113 other events, 437.0 us)
Sparse Core Ops, SparseCore 0:
  79.5 67.0 all-gather.9
  185.5 106.2 all-gather.11
  293.6 66.8 all-gather.13
  401.8 104.1 all-gather.15
  529.7 104.6 reduce-scatter.7
  637.2 66.8 reduce-scatter.9
  715.7 7.6 all-gather.17
  733.8 103.2 reduce-scatter.13
  934.2 147.2 reduce-scatter.15
  1083.5 8.2 all-gather.19
  1094.8 68.0 reduce-scatter.11

commit v2 on v1

v2 whole, which is shorter than its diff:
```python
import math

import functools

import jax
import jax.numpy as jnp
from jax import lax
from jax.experimental import pallas as pl
from jax.experimental.pallas import tpu as pltpu
from jax.sharding import PartitionSpec as P

MESH = pl.DeviceIdType.MESH

HEAD_DIM = 64
LAYERS = 2
BLOCK = 128
LANES = 128

eps_norm = 1e-05
depth_scale = 1.4 / math.sqrt(40.0)
rope_base = 10000.0
masked_score = -1e30
score_scale = 1.0 / math.sqrt(HEAD_DIM)


def times(left, right):
    return jnp.dot(left, right, preferred_element_type=jnp.float32)


def times_transposed(left, right):
    return lax.dot_general(
        left, right, (((1,), (1,)), ((), ())), preferred_element_type=jnp.float32
    )


def outer_rows(left, right):
    return lax.dot_general(
        left, right, (((0,), (0,)), ((), ())), preferred_element_type=jnp.float32
    )


def rms_parts(values):
    inverse = lax.rsqrt(jnp.mean(values * values, axis=-1, keepdims=True) + eps_norm)
    return (values * inverse, inverse)


def norm_backward(values, gain, grad_normed):
    scaled, inverse = rms_parts(values)
    gain_grad = jnp.sum(grad_normed * scaled, axis=0, keepdims=True)
    grad_scaled = grad_normed * gain
    return (
        gain_grad,
        inverse * (grad_scaled - scaled * jnp.mean(grad_scaled * scaled, axis=-1, keepdims=True)),
    )


def rope_tables(position, half_dim):
    inverse = rope_base ** (-jnp.arange(half_dim).astype(jnp.float32) / half_dim)
    angles = position.astype(jnp.float32)[:, None] * inverse[None, :]
    return (jnp.cos(angles)[:, None, :], jnp.sin(angles)[:, None, :])


def rotate(values, tables, direction):
    cosine, sine_table = tables
    half_dim = values.shape[-1] // 2
    front_half = values[..., :half_dim]
    back_half = values[..., half_dim:]
    return jnp.concatenate(
        [
            front_half * cosine - direction * back_half * sine_table,
            back_half * cosine + direction * front_half * sine_table,
        ],
        axis=-1,
    )


def group_layout(lengths, dealing, group_index, seq_count):
    chosen = lax.dynamic_slice_in_dim(dealing, group_index * seq_count, seq_count)
    matches = chosen[:, None] == jnp.arange(lengths.shape[0], dtype=jnp.int32)[None, :]
    seq_lens = jnp.sum(jnp.where(matches, lengths[None, :], 0), axis=1)
    padded = (seq_lens + BLOCK - 1) // BLOCK * BLOCK
    starts = jnp.cumsum(padded) - padded
    return (starts, seq_lens)


def slots_for(number, span_row, half_span):
    rows = jnp.arange(number, dtype=jnp.int32)
    matches = (rows // half_span)[:, None] == jnp.arange(span_row.shape[0], dtype=jnp.int32)[None, :]
    span_of = jnp.sum(jnp.where(matches, span_row[None, :], 0), axis=1)
    return span_of * half_span + rows % half_span


def slot_facts(slots, starts, seq_lens):
    member = jnp.sum((slots[:, None] >= starts[None, :]).astype(jnp.int32), axis=1) - 1
    matches = member[:, None] == jnp.arange(starts.shape[0], dtype=jnp.int32)[None, :]
    anchor = jnp.sum(jnp.where(matches, starts[None, :], 0), axis=1)
    extent = jnp.sum(jnp.where(matches, seq_lens[None, :], 0), axis=1)
    position = slots - anchor
    return (slots, member, position, (position < extent).astype(jnp.int32))


def allowed(query_facts, key_facts):
    query_slot, query_member, query_position, query_valid = query_facts
    key_slot, key_member, key_position, key_valid = key_facts
    same_slot = query_slot[:, None] == key_slot[None, :]
    both_valid = (query_valid[:, None] == 1) & (key_valid[None, :] == 1)
    causal = (query_member[:, None] == key_member[None, :]) & (
        key_position[None, :] <= query_position[:, None]
    )
    return same_slot | both_valid & causal


class Plan:
    def __init__(self, n_dp, n_ctx, columns, hidden):
        self.n_dp, self.n_ctx = n_dp, n_ctx
        heads = columns // HEAD_DIM
        self.head_cuts = [i * heads // n_ctx for i in range(n_ctx + 1)]
        self.head_count = max(b - a for a, b in zip(self.head_cuts, self.head_cuts[1:]))
        self.head_width = self.head_count * HEAD_DIM
        self.unit_cuts = [i * hidden // n_ctx for i in range(n_ctx + 1)]
        units = max(b - a for a, b in zip(self.unit_cuts, self.unit_cuts[1:]))
        self.unit_width = (units + LANES - 1) // LANES * LANES


def cut_windows(weight, cuts, width):
    pieces = []
    for first, last in zip(cuts, cuts[1:]):
        pieces.append(jnp.pad(weight[:, first:last], ((0, 0), (0, width - (last - first)))))
    return jnp.stack(pieces)


def join_windows(windows, cuts):
    return jnp.concatenate(
        [windows[i, :, : last - first] for i, (first, last) in enumerate(zip(cuts, cuts[1:]))], axis=1
    )


def cut_kernel(plan, *refs):
    attention, feed, outs = refs[:4], refs[4:7], refs[7:]
    for i, ref in enumerate(attention):
        for j, (first, last) in enumerate(zip(plan.head_cuts, plan.head_cuts[1:])):
            start, count = i * plan.head_width, (last - first) * HEAD_DIM
            outs[0][j, :, start : start + count] = ref[0, :, first * HEAD_DIM : last * HEAD_DIM]
            if count < plan.head_width:
                outs[0][j, :, start + count : start + plan.head_width] = jnp.zeros(
                    (ref.shape[1], plan.head_width - count), ref.dtype
                )
    for ref, out in zip(feed, outs[1:]):
        for j, (first, last) in enumerate(zip(plan.unit_cuts, plan.unit_cuts[1:])):
            out[j, :, : last - first] = ref[0, :, first:last]
            out[j, :, last - first :] = jnp.zeros((ref.shape[1], plan.unit_width - (last - first)), ref.dtype)


def cut_layer(plan, layer, attention, feed):
    specs = [
        pl.BlockSpec((1,) + weight.shape[1:], lambda i, layer=layer: (layer, 0, 0)) for weight in attention + feed
    ]
    rows = attention[0].shape[1]
    outs = [
        jax.ShapeDtypeStruct((plan.n_ctx, rows, width), jnp.bfloat16)
        for width in [4 * plan.head_width] + [plan.unit_width] * 3
    ]
    return pl.pallas_call(
        functools.partial(cut_kernel, plan),
        name="cut_layer",
        grid=(1,),
        out_shape=tuple(outs),
        in_specs=specs,
        out_specs=tuple(pl.BlockSpec(out.shape, lambda i: (0, 0, 0)) for out in outs),
        compiler_params=pltpu.CompilerParams(vmem_limit_bytes=40 * 2**20),
        cost_estimate=pl.CostEstimate(flops=0, bytes_accessed=8 * 10**6, transcendentals=0),
    )(*attention, *feed)


def join_kernel(plan, places, count, *refs):
    sources, outs = refs[:count], refs[count:]
    for layer in range(LAYERS):
        for i, out in enumerate(outs):
            cuts = [cut * HEAD_DIM for cut in plan.head_cuts] if i < 4 else plan.unit_cuts
            which, start = places[layer][i]
            for j, (first, last) in enumerate(zip(cuts, cuts[1:])):
                out[layer, :, first:last] = sources[which][j, :, start : start + last - first].astype(jnp.float32)


def join_layers(plan, parts):
    widths = [plan.head_width] * 4 + [plan.unit_width] * 3
    sources, places = [], []
    for arrays in parts:
        spots, queue = [], list(widths)
        for array in arrays:
            start = 0
            while start < array.shape[2]:
                spots.append((len(sources), start))
                start += queue.pop(0)
            sources.append(array)
        places.append(spots)
    rows = sources[0].shape[1]
    outs = [
        jax.ShapeDtypeStruct((LAYERS, rows, width), jnp.float32)
        for width in [plan.head_cuts[-1] * HEAD_DIM] * 4 + [plan.unit_cuts[-1]] * 3
    ]
    return local_call(functools.partial(join_kernel, plan, places, len(sources)), "join_layers", sources, outs, [], 0)


def reduce_grads(full, n_ctx):
    own = lax.psum_scatter(full, "dp", scatter_dimension=0, tiled=True)
    return own.reshape(n_ctx, -1, own.shape[-1])


def gather_rows(piece):
    return lax.all_gather(piece, ("ctx", "tensor"), axis=0, tiled=True)


def scatter_rows(partial_sum):
    return lax.psum_scatter(
        partial_sum.astype(jnp.bfloat16), ("ctx", "tensor"), scatter_dimension=0, tiled=True
    ).astype(jnp.float32)


SLOT = 16
PARTS = 1
SKEW = 3


def place():
    return lax.axis_index("dp"), lax.axis_index("ctx"), lax.axis_index("tensor")


def slot_rows(base, index):
    return pl.ds(pl.multiple_of(base + index * SLOT, SLOT), SLOT)


def send(src, dst, send_sem, recv_sem, target):
    return pltpu.make_async_remote_copy(
        src_ref=src, dst_ref=dst, send_sem=send_sem, recv_sem=recv_sem, device_id=target, device_id_type=MESH
    )


def greet(d, c, t, everyone=False):
    barrier = pltpu.get_barrier_semaphore()
    others = [(d, c, 1 - t), (d, c ^ 1, t), (d, c ^ 2, t), (d, c ^ 3, t), (d ^ 1, c, t), (d ^ 2, c, t)]
    if everyone:
        others = others[:1] + [(d ^ (k // 4), c ^ (k % 4), t) for k in range(1, 16)]
    for other in others:
        pl.semaphore_signal(barrier, inc=1, device_id=other, device_id_type=MESH)
    pl.semaphore_wait(barrier, len(others))


class Job:
    everyone = False
    near = False
    late = False

    @staticmethod
    def scratch(source):
        return []

    def steps(self):
        return []


class Exchange(Job):
    semaphores = 7

    @staticmethod
    def result(source):
        return jax.ShapeDtypeStruct(source.shape, source.dtype)

    def __init__(self, source, result, sems):
        d, c, t = place()
        self.own = pltpu.make_async_copy(source.at[c], result.at[c], sems.at[6])
        self.copies = [
            send(source.at[c ^ k], result.at[c], sems.at[k - 1], sems.at[k + 2], (d, c ^ k, t)) for k in (3, 2, 1)
        ]

    def start(self):
        for copy in self.copies:
            copy.start()
        self.own.start()

    def finish(self):
        for copy in self.copies:
            copy.wait()
        self.own.wait()


class Collect(Job):
    semaphores = 25

    @staticmethod
    def result(source):
        return jax.ShapeDtypeStruct((4 * source.shape[0], source.shape[1]), source.dtype)

    def __init__(self, source, result, sems):
        d, c, t = place()
        block = source.shape[0]
        half = block // 2

        def piece(chip):
            return result.at[pl.ds(pl.multiple_of(chip * block + t * half, half), half)]

        self.own = pltpu.make_async_copy(source, result.at[pl.ds(pl.multiple_of(c * block, block), block)], sems.at[24])
        mine = source.at[pl.ds(pl.multiple_of(t * half, half), half)]
        self.hops, self.onward = {}, {}
        for way, more, target in ((0, c < 3, (d, c + 1, t)), (1, c > 0, (d, c - 1, t))):
            for hop in range(4):
                chip = c - hop if way == 0 else c + hop
                held = (chip >= 0) if way == 0 else (chip <= 3)
                if hop < 3:
                    self.hops[way, hop] = (
                        more & held,
                        send(
                            piece(chip) if hop else mine,
                            piece(chip),
                            sems.at[way * 12 + hop],
                            sems.at[way * 12 + 3 + hop],
                            target,
                        ),
                    )
                if hop:
                    self.onward[way, hop] = (
                        held,
                        send(
                            piece(chip),
                            piece(chip),
                            sems.at[way * 12 + 5 + hop],
                            sems.at[way * 12 + 8 + hop],
                            (d, c, 1 - t),
                        ),
                    )

    def start(self):
        for way in range(2):
            go, copy = self.hops[way, 0]
            pl.when(go)(copy.start)
        self.own.start()

    def steps(self):
        return [functools.partial(self.pass_on, hop) for hop in range(1, 4)]

    def pass_on(self, hop):
        for way in range(2):
            held, onward = self.onward[way, hop]
            arrived = self.hops[way, hop - 1][1]

            @pl.when(held)
            def _():
                arrived.wait_recv()
                onward.start()

            if hop < 3:
                go, copy = self.hops[way, hop]
                pl.when(go)(copy.start)

    def finish(self):
        for go, copy in self.hops.values():
            pl.when(go)(copy.wait_send)
        for held, onward in self.onward.values():
            pl.when(held)(onward.wait)
        self.own.wait()


class GainScatter(Job):
    semaphores = 31
    everyone = True
    near = True
    late = True

    @staticmethod
    def blocks(source):
        return (16, 8, (source.shape[1] // 16 + LANES - 1) // LANES * LANES)

    @staticmethod
    def result(source):
        return jax.ShapeDtypeStruct(GainScatter.blocks(source), source.dtype)

    @staticmethod
    def scratch(source):
        return [pltpu.VMEM(GainScatter.blocks(source), source.dtype)]

    def __init__(self, source, result, sems, cut):
        d, c, t = place()
        mine = d * 4 + c
        self.source, self.cut = source, cut
        self.own = pltpu.make_async_copy(cut.at[mine], result.at[mine], sems.at[0])
        self.copies = []
        for k in range(1, 16):
            g, i = d ^ (k // 4), c ^ (k % 4)
            self.copies.append(send(cut.at[g * 4 + i], result.at[mine], sems.at[k], sems.at[k + 15], (g, i, t)))

    def start(self, made):
        self.cut[...] = jnp.zeros(self.cut.shape, self.cut.dtype)
        part = made.shape[1] // 16
        for i in range(16):
            self.cut[i, 0:1, :part] = made[:, i * part : (i + 1) * part]
            rows = self.source.shape[0]
            self.cut[i, 1 : 1 + rows, :part] = self.source[:, i * part : (i + 1) * part]
        for copy in self.copies:
            copy.start()
        self.own.start()

    def finish(self):
        for copy in self.copies:
            copy.wait()
        self.own.wait()


class Return(Job):
    semaphores = 31
    near = True
    order = (0, 2, 1, 3)

    @staticmethod
    def result(source):
        return jax.ShapeDtypeStruct((4,) + source.shape[1:], source.dtype)

    @staticmethod
    def scratch(source):
        four = pltpu.VMEM((4,) + source.shape[1:], source.dtype)
        return [four] * 5

    def __init__(self, source, result, sems, corner_in, x_in, y_in, passed, total):
        d, c, t = place()
        self.corner_in, self.sides_in, self.passed, self.total = corner_in, (x_in, y_in), passed, total
        self.terms, self.corners, self.sides, self.line = [], [], [], [None]
        for k in range(4):
            i = c ^ k
            way = k // 2
            self.terms.append([source.at[(d ^ flip) * 4 + i] for flip in (0, 1, 2)])
            self.corners.append(
                send(source.at[(d ^ 3) * 4 + i], corner_in.at[k], sems.at[k], sems.at[4 + k], (d ^ (1 + way), c, t))
            )
            self.sides.append(
                [
                    send(
                        passed.at[k] if side != way else source.at[(d ^ (1 + side)) * 4 + i],
                        self.sides_in[side].at[k],
                        sems.at[8 + 2 * k + side],
                        sems.at[16 + 2 * k + side],
                        (d ^ (1 + side), c, t),
                    )
                    for side in range(2)
                ]
            )
            if k:
                self.line.append(send(total.at[k], result.at[c], sems.at[23 + k], sems.at[26 + k], (d, i, t)))
        self.own = pltpu.make_async_copy(total.at[0], result.at[c], sems.at[30])

    def start(self):
        for k in self.order:
            self.corners[k].start()
        for k in self.order:
            self.sides[k][k // 2].start()

    def steps(self):
        return [functools.partial(self.pass_term, k) for k in self.order] + [
            functools.partial(self.add_up, k) for k in (3, 2, 1, 0)
        ]

    def pass_term(self, k):
        side = 1 - k // 2
        self.corners[k].wait_recv()
        self.passed[k] = (self.terms[k][1 + side][...].astype(jnp.float32) + self.corner_in[k].astype(jnp.float32)).astype(
            self.passed.dtype
        )
        self.sides[k][side].start()

    def add_up(self, k):
        for side in range(2):
            self.sides[k][side].wait_recv()
        self.total[k] = (
            self.terms[k][0][...].astype(jnp.float32)
            + self.sides_in[0][k].astype(jnp.float32)
            + self.sides_in[1][k].astype(jnp.float32)
        ).astype(self.total.dtype)
        if k:
            self.line[k].start()
        else:
            self.own.start()

    def finish(self):
        for k in range(4):
            self.corners[k].wait_send()
            for copy in self.sides[k]:
                copy.wait_send()
            if k:
                self.line[k].wait()
        self.own.wait()


class Fetch(Job):
    semaphores = 31

    @staticmethod
    def result(source):
        return jax.ShapeDtypeStruct((16,) + source.shape[1:], source.dtype)

    order = (0, 2, 1, 3)

    def __init__(self, source, result, sems):
        d, c, t = place()
        self.own = pltpu.make_async_copy(source.at[c], result.at[d * 4 + c], sems.at[0])
        self.line = [None]
        for k in range(1, 4):
            self.line.append(
                send(source.at[c ^ k], result.at[d * 4 + c], sems.at[k], sems.at[k + 3], (d, c ^ k, t))
            )
        self.link(source, result, sems)

    def link(self, source, result, sems):
        d, c, t = place()
        self.side, self.corners = [], []
        for k in range(4):
            held = result.at[d * 4 + (c ^ k)]
            ready = held if self.line[k] is not None else source.at[c ^ k]
            self.side.append(
                [
                    send(ready, held, sems.at[7 + 2 * k + way], sems.at[15 + 2 * k + way], (d ^ (1 + way), c, t))
                    for way in range(2)
                ]
            )
            way = k // 2
            passed = result.at[(d ^ (1 + way)) * 4 + (c ^ k)]
            self.corners.append(
                send(passed, passed, sems.at[23 + k], sems.at[27 + k], (d ^ (2 - way), c, t))
            )

    def start(self):
        self.own.start()
        for k in (3, 2, 1):
            self.line[k].start()
        for copy in self.side[0]:
            copy.start()

    def steps(self):
        return [functools.partial(self.pass_sides, k) for k in (1, 2, 3)] + self.corner_steps()

    def corner_steps(self):
        return [functools.partial(self.pass_corner, k) for k in self.order]

    def pass_sides(self, k):
        self.line[k].wait_recv()
        for copy in self.side[k]:
            copy.start()

    def pass_corner(self, k):
        self.side[k][k // 2].wait_recv()
        self.corners[k].start()

    def finish(self):
        for k in range(4):
            self.side[k][1 - k // 2].wait_recv()
        for k in range(4):
            self.corners[k].wait()
            for copy in self.side[k]:
                copy.wait_send()
            if self.line[k] is not None:
                self.line[k].wait_send()
        self.own.wait()


class Spread(Fetch):
    @staticmethod
    def result(source):
        return jax.ShapeDtypeStruct((16,) + source.shape[1:], source.dtype)

    def __init__(self, source, result, sems):
        d, c, t = place()
        self.own = pltpu.make_async_copy(source, result.at[pl.ds(d * 4, 4)], sems.at[0])
        self.line = [None] * 4
        self.link(source, result, sems)

    def start(self):
        for k in self.order:
            for copy in self.side[k]:
                copy.start()
        self.own.start()

    def steps(self):
        return self.corner_steps()


def take(refs, count):
    return refs[:count], refs[count:]


def make_jobs(kinds, scratch_counts, sources, results, refs):
    jobs = []
    for kind, count, source, result in zip(kinds, scratch_counts, sources, results):
        (sems, *scratch), refs = take(refs, 1 + count)
        jobs.append(kind(source, result, sems, *scratch))
    return jobs


def job_specs(jobs):
    vmem, hbm = pl.BlockSpec(memory_space=pltpu.VMEM), pl.BlockSpec(memory_space=pl.ANY)
    sources = [job[1] for job in jobs]
    in_specs = [vmem if job[0].near else hbm for job in jobs]
    out_shapes = [job[0].result(job[1]) for job in jobs]
    scratch, counts = [], []
    for kind, source, *_ in jobs:
        extra = kind.scratch(source)
        scratch += [pltpu.SemaphoreType.DMA((kind.semaphores,))] + extra
        counts.append(len(extra))
    return sources, in_specs, out_shapes, [hbm] * len(jobs), scratch, counts


def jobs_kernel(kinds, counts, urgent, *refs):
    n = len(kinds)
    greet(*place(), any(kind.everyone for kind in kinds))
    jobs = make_jobs(kinds, counts, refs[:n], refs[n : 2 * n], refs[2 * n :])
    first, later = jobs[:urgent], jobs[urgent:]
    for job in first:
        job.start()
    rest = []
    for job in first:
        todo = job.steps()
        for act in todo[:3]:
            act()
        rest += todo[3:]
    for job in later:
        job.start()
    for act in rest:
        act()
    for job in later:
        for act in job.steps():
            act()
    for job in jobs:
        job.finish()


def jobs_call(number, jobs, urgent):
    sources, in_specs, out_shapes, out_specs, scratch, counts = job_specs(jobs)
    return pl.pallas_call(
        functools.partial(jobs_kernel, [job[0] for job in jobs], counts, urgent),
        name="moves",
        out_shape=tuple(out_shapes),
        in_specs=in_specs,
        out_specs=tuple(out_specs),
        scratch_shapes=scratch,
        compiler_params=pltpu.CompilerParams(
            collective_id=number, has_side_effects=True, vmem_limit_bytes=48 * 2**20
        ),
        cost_estimate=pl.CostEstimate(flops=10**9, bytes_accessed=100 * 10**6, transcendentals=0),
    )(*sources)


def drain(ref, sem):
    pltpu.make_async_copy(ref, ref, sem).wait()


class Line:
    scratch_count = 14

    @staticmethod
    def scratch(block, width):
        pieces = block // SLOT * PARTS
        piece = pltpu.VMEM((block, width), jnp.bfloat16)
        dma = pltpu.SemaphoreType.DMA
        return (
            [piece] * 4
            + [pltpu.VMEM((2, block, width), jnp.bfloat16), piece, dma((6,)), dma((2, 2))]
            + [dma((pieces,))] * 4
            + [dma((2,)), pltpu.VMEM((SLOT, width), jnp.float32)]
        )

    def __init__(self, settle, gather, partial_ref, settle_in, settle_out, whole_ref, scratch):
        self.settle, self.gather = settle, gather
        self.partial_ref, self.settle_in, self.settle_out, self.whole_ref = partial_ref, settle_in, settle_out, whole_ref
        (
            self.acc_up,
            self.acc_down,
            self.in_up,
            self.in_down,
            self.sib,
            self.stage,
            self.send_sems,
            self.sib_sems,
            self.up_sems,
            self.down_sems,
            self.back_up,
            self.back_down,
            self.whole_sems,
            self.sum_ref,
        ) = scratch
        d, c, t = place()
        self.block = self.acc_up.shape[0]
        self.pieces = self.block // SLOT * PARTS
        self.columns = self.acc_up.shape[1] // PARTS
        self.turns = self.pieces + SKEW * (6 if gather else 3)
        self.sibling, self.above, self.below = (d, c, 1 - t), (d, c + 1, t), (d, c - 1, t)
        self.down_base, self.up_base = t * self.block, (2 + t) * self.block
        self.low, self.high = c > 0, c < 3
        self.middle = self.low & self.high

    def begin(self):
        _, _, t = place()
        half = self.block // 2
        for part in range(2):
            for which, base in ((0, (1 - t) * self.block), (1, (3 - t) * self.block)):
                rows = pl.ds(pl.multiple_of(base + part * half, half), half)
                send(
                    self.partial_ref.at[rows],
                    self.sib.at[which, pl.ds(part * half, half)],
                    self.send_sems.at[0],
                    self.sib_sems.at[which, part],
                    self.sibling,
                ).start()

        @pl.when(self.middle)
        def _():
            for ref in self.settle_out:
                ref[...] = jnp.zeros(ref.shape, ref.dtype)

    def piece(self, base, index, part):
        return (slot_rows(base, index // PARTS), pl.ds(part * self.columns, self.columns))

    def chain(self, index, which, base, first, last, into, acc, recv_sems, send_sem, target, back_target, back_sems):
        half = self.block // 2
        pieces = self.pieces

        @pl.when((index >= 0) & (index < pieces) & (index % (pieces // 2) == 0))
        def _():
            drain(self.sib.at[which, pl.ds(0, half)], self.sib_sems.at[which, index // (pieces // 2)])

        for part in range(PARTS):
            here = self.piece(0, index, part)
            own = self.piece(base, index, part)

            @pl.when((index >= 0) & (index < pieces) & (index % PARTS == part))
            def _():
                def term():
                    return self.partial_ref[own].astype(jnp.float32) + self.sib[(which, *here)].astype(jnp.float32)

                def pass_on(total):
                    acc[here] = total.astype(jnp.bfloat16)
                    send(acc.at[here], into.at[here], send_sem, recv_sems.at[index], target).start()

                @pl.when(first)
                def _():
                    pass_on(term())

                @pl.when(jnp.logical_not(first))
                def _():
                    drain(into.at[here], recv_sems.at[index])

                @pl.when(self.middle)
                def _():
                    pass_on(term() + into[here].astype(jnp.float32))

                @pl.when(last)
                def _():
                    self.sum_ref[:, here[1]] = term() + into[here].astype(jnp.float32)
                    if part == PARTS - 1:
                        self.settled(index, which, here[0], own[0], back_target, back_sems)

    def settled(self, index, which, rows, own_rows, back_target, back_sems):
        value = self.settle(self.sum_ref[...], rows, self.settle_in, self.settle_out)
        self.stage[rows] = value
        if self.gather:
            whole, sems = self.whole_ref, self.send_sems
            whole[own_rows] = value
            for part in range(PARTS):
                columns = pl.ds(part * self.columns, self.columns)
                send(
                    self.stage.at[rows, columns],
                    whole.at[own_rows, columns],
                    sems.at[3],
                    back_sems.at[index - (PARTS - 1) + part],
                    back_target,
                ).start()
            send(self.stage.at[rows], whole.at[own_rows], sems.at[5], self.whole_sems.at[which], self.sibling).start()

    def back(self, index, which, base, reached, more, back_sems, target):
        for part in range(PARTS):
            own = self.piece(base, index, part)
            held = self.whole_ref.at[own]

            @pl.when((index >= 0) & (index < self.pieces) & reached & (index % PARTS == part))
            def _():
                drain(held, back_sems.at[index])

                @pl.when(more)
                def _():
                    send(held, held, self.send_sems.at[4], back_sems.at[index], target).start()

                if part == PARTS - 1:
                    rows = self.whole_ref.at[own[0]]
                    send(rows, rows, self.send_sems.at[5], self.whole_sems.at[which], self.sibling).start()

    def step(self, j):
        _, c, _ = place()
        sems = self.send_sems
        self.chain(
            j - SKEW * c, 1, self.up_base, c == 0, c == 3, self.in_up, self.acc_up, self.up_sems, sems.at[1],
            self.above, self.below, self.back_down,
        )
        self.chain(
            j - SKEW * (3 - c), 0, self.down_base, c == 3, c == 0, self.in_down, self.acc_down, self.down_sems,
            sems.at[2], self.below, self.above, self.back_up,
        )
        if self.gather:
            self.back(j - SKEW * (6 - c), 1, self.up_base, self.high, self.low, self.back_down, self.below)
            self.back(j - SKEW * (3 + c), 0, self.down_base, self.low, self.high, self.back_up, self.above)

    def end(self):
        d, c, t = place()
        sems, whole, stage = self.send_sems, self.whole_ref, self.stage
        drain(self.sib, sems.at[0])

        @pl.when(self.high)
        def _():
            drain(self.acc_up, sems.at[1])

        @pl.when(self.low)
        def _():
            drain(self.acc_down, sems.at[2])

        if self.gather:
            block = self.block
            up_rows, down_rows, other_up, other_down = [
                pl.ds(pl.multiple_of(base, block), block)
                for base in (self.up_base, self.down_base, (3 - t) * block, (1 - t) * block)
            ]

            @pl.when(jnp.logical_not(self.middle))
            def _():
                drain(stage, sems.at[3])

            @pl.when(self.middle)
            def _():
                drain(whole.at[up_rows], sems.at[4])
                drain(whole.at[down_rows], sems.at[4])

            drain(whole.at[up_rows], sems.at[5])
            drain(whole.at[down_rows], sems.at[5])
            drain(whole.at[other_up], self.whole_sems.at[1])
            drain(whole.at[other_down], self.whole_sems.at[0])
            return
        keeps = ((c == 0) & (t == 0)) | ((c == 3) & (t == 1))
        gives = ((c == 0) & (t == 1)) | ((c == 3) & (t == 0))
        takes = ((c == 1) & (t == 1)) | ((c == 2) & (t == 0))
        inner = (d, jnp.where(c == 0, 1, 2), t)
        away = send(stage, whole, sems.at[3], self.whole_sems.at[0], inner)
        across = send(stage, whole, sems.at[5], self.whole_sems.at[1], self.sibling)
        hand_on = send(whole, whole, sems.at[5], self.whole_sems.at[1], self.sibling)

        @pl.when(keeps)
        def _():
            across.start()
            whole[...] = stage[...]
            across.wait_send()

        @pl.when(gives)
        def _():
            away.start()
            away.wait_send()

        @pl.when(takes)
        def _():
            away.wait_recv()
            hand_on.start()
            hand_on.wait_send()

        @pl.when(jnp.logical_not(keeps | takes))
        def _():
            across.wait_recv()


def line_kernel(prelude, lines, kinds, counts, paces, *refs):
    n_jobs = len(kinds)
    line_in = []
    if prelude:
        prelude_in, refs = take(refs, prelude[1])
    for i, (_, _, n_in, _) in enumerate(lines):
        partial_refs, refs = take(refs, 0 if prelude and i == 0 else 1)
        ins, refs = take(refs, n_in)
        line_in.append((partial_refs, ins))
    job_sources, refs = take(refs, n_jobs)
    if prelude:
        prelude_out, refs = take(refs, prelude[2])
    line_out = []
    for _, _, _, n_out in lines:
        outs, refs = take(refs, n_out)
        (whole_ref,), refs = take(refs, 1)
        line_out.append((outs, whole_ref))
    job_results, refs = take(refs, n_jobs)
    if prelude:
        made, refs = take(refs, 1)
        prelude_scratch, refs = take(refs, prelude[3])
    built = []
    for i, (settle, gather, _, _) in enumerate(lines):
        scratch, refs = take(refs, Line.scratch_count)
        partial_refs, ins = line_in[i]
        outs, whole_ref = line_out[i]
        partial_ref = partial_refs[0] if partial_refs else made[0]
        built.append(Line(settle, gather, partial_ref, ins, outs, whole_ref, scratch))
    greet(*place(), any(kind.everyone for kind in kinds))
    jobs = make_jobs(kinds, counts, job_sources, job_results, refs)
    if not prelude:
        built[0].begin()
    for line in built[1:]:
        line.begin()
    for job in jobs:
        if not job.late:
            job.start()
    if prelude:
        prelude[0](*prelude_in, made[0], *prelude_out, *prelude_scratch)
        built[0].begin()

    turns = max(line.turns for line in built)
    timed, rest = {}, []
    for job, (first_turn, gap) in zip(jobs, paces):
        for i, act in enumerate(job.steps()):
            turn = first_turn + i * gap
            if turn < turns:
                timed.setdefault(turn, []).append(act)
            else:
                rest.append(act)

    def step(j, carry):
        for turn, acts in timed.items():

            @pl.when(j == turn)
            def _():
                for act in acts:
                    act()

        for line in built:
            line.step(j)
        return carry

    lax.fori_loop(0, turns, step, 0)
    for job in jobs:
        if job.late:
            job.start(built[0].settle_out[0])
    for act in rest:
        act()
    for line in built:
        line.end()
    for job in jobs:
        job.finish()


def line_call(name, number, lines, jobs, prelude=None):
    vmem = pl.BlockSpec(memory_space=pltpu.VMEM)
    operands, shapes, scratch, facts = [], [], [], []
    if prelude:
        kernel, prelude_in, prelude_out, prelude_scratch, made = prelude
        operands += prelude_in
        shapes += prelude_out
        scratch += [pltpu.VMEM(made, jnp.bfloat16)] + prelude_scratch
    for settle, gather, partial_sum, settle_in, settle_out in lines:
        rows, width = made if partial_sum is None else partial_sum.shape
        block = rows // 4
        operands += ([] if partial_sum is None else [partial_sum]) + settle_in
        shapes += settle_out + [jax.ShapeDtypeStruct((rows if gather else block, width), jnp.bfloat16)]
        scratch += Line.scratch(block, width)
        facts.append((settle, gather, len(settle_in), len(settle_out)))
    sources, in_specs, out_shapes, out_specs, job_scratch, counts = job_specs(jobs)
    paces = [(tuple(job) + (0, 1))[2:4] for job in jobs]
    return pl.pallas_call(
        functools.partial(
            line_kernel,
            (kernel, len(prelude_in), len(prelude_out), len(prelude_scratch)) if prelude else None,
            facts,
            [job[0] for job in jobs],
            counts,
            paces,
        ),
        name=name,
        out_shape=tuple(shapes + out_shapes),
        in_specs=[vmem] * len(operands) + in_specs,
        out_specs=tuple([vmem] * len(shapes) + out_specs),
        scratch_shapes=scratch + job_scratch,
        compiler_params=pltpu.CompilerParams(
            collective_id=number, has_side_effects=True, vmem_limit_bytes=(58 if any(job[0] is Return for job in jobs) else 40) * 2**20
        ),
        cost_estimate=pl.CostEstimate(flops=10**9, bytes_accessed=100 * 10**6, transcendentals=0),
    )(*operands, *sources)


def settle_forward(total, rows, ins, outs):
    residual_ref, gain_ref = ins
    value = residual_ref[rows] + depth_scale * total
    outs[0][rows] = value
    inverse = lax.rsqrt(jnp.mean(value * value, axis=-1, keepdims=True) + eps_norm)
    return (value * inverse * gain_ref[...]).astype(jnp.bfloat16)


def settle_last(total, rows, ins, outs):
    return (ins[0][rows] + depth_scale * total).astype(jnp.bfloat16)


def settle_backward(total, rows, ins, outs, more=True):
    values_ref, grad_ref, gain_ref = ins
    gain_grad = outs[0]
    value = values_ref[rows]
    inverse = lax.rsqrt(jnp.mean(value * value, axis=-1, keepdims=True) + eps_norm)
    scaled = value * inverse
    contribution = jnp.sum(total * scaled, axis=0, keepdims=True)

    first = rows.start == 0

    @pl.when(first)
    def _():
        gain_grad[...] = contribution

    @pl.when(jnp.logical_not(first))
    def _():
        gain_grad[...] += contribution

    grad_scaled = total * gain_ref[...]
    grad = grad_ref[rows] + inverse * (
        grad_scaled - scaled * jnp.mean(grad_scaled * scaled, axis=-1, keepdims=True)
    )
    if not more:
        return grad.astype(jnp.bfloat16)
    outs[1][rows] = grad
    return (depth_scale * grad).astype(jnp.bfloat16)


class LineComm:
    def __init__(self):
        self.number = 0

    def next_number(self):
        self.number += 1
        return self.number

    def moves(self, *jobs, urgent=0):
        return jobs_call(self.next_number(), jobs, urgent)

    def own_rows(self, whole):
        block = whole.shape[0] // 4
        _, c, t = place()
        return lax.dynamic_slice_in_dim(whole, (jnp.where(c >= 2, 2, 0) + t) * block, block, 0)

    def forward(self, partial_sum, residual, gain, jobs, prelude=None):
        outs = line_call(
            "forward_line",
            self.next_number(),
            [(settle_forward, True, partial_sum, [residual, gain], [jax.ShapeDtypeStruct(residual.shape, jnp.float32)])],
            jobs,
            prelude,
        )
        made, (value, normed, *moved) = take(outs, len(prelude[2]) if prelude else 0)
        return value, normed, moved, made

    def last(self, partial_sum, residual, jobs):
        output, *moved = line_call(
            "last_line", self.next_number(), [(settle_last, False, partial_sum, [residual], [])], jobs
        )
        return output, moved

    def backward(self, partial_sum, values, grad_rows, gain, jobs):
        lines = [
            (
                settle_backward,
                True,
                partial_sum,
                [values, grad_rows, gain],
                [jax.ShapeDtypeStruct(gain.shape, jnp.float32), jax.ShapeDtypeStruct(values.shape, jnp.float32)],
            )
        ]
        gain_grad, grad, gathered, *moved = line_call("backward_line", self.next_number(), lines, jobs)
        return grad, gain_grad, gathered, moved

    def backward_last(self, partial_sum, values, grad_rows, gain, jobs, gain_grads):
        gain_grad, own, *moved, gain_blocks = line_call(
            "backward_last_line",
            self.next_number(),
            [
                (
                    functools.partial(settle_backward, more=False),
                    False,
                    partial_sum,
                    [values, grad_rows, gain],
                    [jax.ShapeDtypeStruct(gain.shape, jnp.float32)],
                )
            ],
            jobs + [(GainScatter, gain_grads)],
        )
        return own, jnp.sum(gain_blocks, axis=0)[: 1 + gain_grads.shape[0], : gain.shape[1] // 16], moved

    def return_grads(self, full):
        return full.reshape(16, -1, full.shape[1])


class PlainComm:
    def moves(self, *jobs, urgent=0):
        moved = []
        for kind, source, *_ in jobs:
            if kind is Collect:
                moved.append(lax.all_gather(source, "ctx", axis=0, tiled=True))
                continue
            if kind is Return:
                source = reduce_grads(source, lax.axis_size("ctx"))
                moved.append(lax.all_to_all(source, "ctx", 0, 0, tiled=False))
                continue
            blocks = source if kind is Spread else lax.all_to_all(source, "ctx", 0, 0, tiled=False)
            moved.append(blocks if kind is Exchange else lax.all_gather(blocks, "dp", axis=0, tiled=True))
        return tuple(moved)

    def own_rows(self, whole):
        _, c, t = place()
        share = whole.shape[0] // (lax.axis_size("ctx") * lax.axis_size("tensor"))
        return lax.dynamic_slice_in_dim(whole, (c * lax.axis_size("tensor") + t) * share, share, 0)

    def forward(self, partial_sum, residual, gain, jobs, prelude=None):
        value = residual + depth_scale * scatter_rows(partial_sum)
        return value, gather_rows((rms_parts(value)[0] * gain).astype(jnp.bfloat16)), self.moves(*jobs), ()

    def deliver(self, rows):
        return lax.all_gather(rows.astype(jnp.bfloat16), "tensor", axis=0, tiled=True)

    def last(self, partial_sum, residual, jobs):
        return self.deliver(residual + depth_scale * scatter_rows(partial_sum)), self.moves(*jobs)

    def backward(self, partial_sum, values, grad_rows, gain, jobs):
        gain_grad, from_norm = norm_backward(values, gain, scatter_rows(partial_sum))
        grad = grad_rows + from_norm
        gathered = gather_rows((depth_scale * grad).astype(jnp.bfloat16))
        return grad, gain_grad, gathered, self.moves(*jobs)

    def backward_last(self, partial_sum, values, grad_rows, gain, jobs, gain_grads):
        gain_grad, from_norm = norm_backward(values, gain, scatter_rows(partial_sum))
        sums = jnp.concatenate([gain_grad, gain_grads], axis=0)
        sums = lax.psum_scatter(sums, ("dp", "ctx"), scatter_dimension=1, tiled=True)
        return self.deliver(grad_rows + from_norm), sums, self.moves(*jobs)

    def return_grads(self, full):
        return full


def swap_halves(values):
    lane = lax.broadcasted_iota(jnp.int32, values.shape, 1)
    half = HEAD_DIM // 2
    width = values.shape[1]
    return jnp.where(lane % HEAD_DIM < half, pltpu.roll(values, width - half, 1), pltpu.roll(values, half, 1))


def head_scores(query, key, bias):
    return times_transposed(query, key) * score_scale + bias


def attend_kernel(heads, normed_ref, weight_ref, cosine_ref, sine_ref, bias_ref, partial_ref, mixed_ref, attended_ref, total_ref, wide):
    width = heads * HEAD_DIM
    lead = wide.shape[1] - width
    cosine, sine = cosine_ref[...], sine_ref[...]
    columns = mixed_ref.shape[1]
    normed = normed_ref[...]
    for first in range(0, columns, 2 * LANES):
        block = times(normed, weight_ref[:, first : first + 2 * LANES])
        for part in range(2):
            start = first + part * LANES
            tile = block[:, part * LANES : (part + 1) * LANES]
            if start < 2 * width:
                tile = tile * cosine + swap_halves(tile) * sine
            mixed_ref[:, start : start + LANES] = tile.astype(jnp.bfloat16)
    wide[:, :lead] = jnp.zeros((wide.shape[0], lead), jnp.bfloat16)
    for head in range(heads):
        low = head * HEAD_DIM
        query = mixed_ref[:, low : low + HEAD_DIM]
        key = mixed_ref[:, width + low : width + low + HEAD_DIM]
        value = mixed_ref[:, 2 * width + low : 2 * width + low + HEAD_DIM]
        scores = head_scores(query, key, bias_ref[...])
        top = jnp.max(scores, axis=-1, keepdims=True)
        terms = jnp.exp(scores - top)
        total = jnp.sum(terms, axis=-1, keepdims=True)
        probs = (terms / total).astype(jnp.bfloat16)
        wide[:, lead + low : lead + low + HEAD_DIM] = times(probs, value).astype(jnp.bfloat16)
        total_ref[:, head : head + 1] = top + jnp.log(total)
    attended_ref[...] = wide[:, lead:]
    attended = wide[...]
    for first in range(0, partial_ref.shape[1], 3 * LANES):
        partial_ref[:, first : first + 3 * LANES] = times_transposed(
            attended, weight_ref[first : first + 3 * LANES, 3 * width - lead :]
        ).astype(jnp.bfloat16)


def attend_back_kernel(heads, grad_ref, weight_ref, mixed_ref, total_ref, cosine_ref, sine_ref, bias_ref, partial_ref, all_ref, wide, turned):
    width = heads * HEAD_DIM
    lead = wide.shape[1] - width
    wide[...] = times(grad_ref[...], weight_ref[:, 3 * width - lead :]).astype(jnp.bfloat16)
    all_ref[:, 3 * width :] = jnp.zeros((all_ref.shape[0], all_ref.shape[1] - 3 * width), jnp.bfloat16)
    for head in range(heads):
        low = head * HEAD_DIM
        query = mixed_ref[:, low : low + HEAD_DIM]
        key = mixed_ref[:, width + low : width + low + HEAD_DIM]
        value = mixed_ref[:, 2 * width + low : 2 * width + low + HEAD_DIM]
        grad_out = wide[:, lead + low : lead + low + HEAD_DIM]
        scores = head_scores(query, key, bias_ref[...])
        probs = jnp.exp(scores - total_ref[:, head : head + 1])
        grad_probs = times_transposed(grad_out, value)
        delta = jnp.sum(probs * grad_probs, axis=-1, keepdims=True)
        grad_scores = (probs * (grad_probs - delta) * score_scale).astype(jnp.bfloat16)
        turned[:, low : low + HEAD_DIM] = times(grad_scores, key)
        turned[:, width + low : width + low + HEAD_DIM] = outer_rows(grad_scores, query)
        all_ref[:, 2 * width + low : 2 * width + low + HEAD_DIM] = outer_rows(
            probs.astype(jnp.bfloat16), grad_out
        ).astype(jnp.bfloat16)
    cosine, sine = cosine_ref[...], sine_ref[...]
    for start in range(0, 2 * width, LANES):
        tile = turned[:, start : start + LANES]
        all_ref[:, start : start + LANES] = (tile * cosine - swap_halves(tile) * sine).astype(jnp.bfloat16)
    grad_all = all_ref[...]
    for first in range(0, partial_ref.shape[1], 3 * LANES):
        partial_ref[:, first : first + 3 * LANES] = times_transposed(
            grad_all, weight_ref[first : first + 3 * LANES, : grad_all.shape[1]]
        ).astype(jnp.bfloat16)


def local_call(kernel, name, operands, outs, scratch, flops):
    vmem = pl.BlockSpec(memory_space=pltpu.VMEM)
    return pl.pallas_call(
        kernel,
        name=name,
        out_shape=tuple(outs),
        in_specs=[vmem] * len(operands),
        out_specs=tuple([vmem] * len(outs)),
        scratch_shapes=scratch,
        compiler_params=pltpu.CompilerParams(vmem_limit_bytes=48 * 2**20),
        cost_estimate=pl.CostEstimate(flops=flops, bytes_accessed=20 * 10**6, transcendentals=0),
    )(*operands)


def outer_kernel(*refs):
    out_ref, first = refs[-1], 0
    for left, right in zip(refs[:-1:2], refs[1:-1:2]):
        last = first + right.shape[1]
        out_ref[:, first:last] = outer_rows(left[...], right[...]).astype(out_ref.dtype)
        first = last


def outer_sums(*pairs):
    rows, width = pairs[0][0].shape
    columns = sum(right.shape[1] for _, right in pairs)
    tile = 256
    specs, operands = [], []
    for left, right in pairs:
        specs += [
            pl.BlockSpec((rows, tile), lambda i: (0, i)),
            pl.BlockSpec(right.shape, lambda i: (0, 0)),
        ]
        operands += [left, right]
    return pl.pallas_call(
        outer_kernel,
        name="outer_sums",
        grid=(width // tile,),
        out_shape=jax.ShapeDtypeStruct((width, columns), jnp.bfloat16),
        in_specs=specs,
        out_specs=pl.BlockSpec((tile, columns), lambda i: (i, 0)),
        compiler_params=pltpu.CompilerParams(vmem_limit_bytes=40 * 2**20),
        cost_estimate=pl.CostEstimate(
            flops=2 * rows * width * columns, bytes_accessed=2 * (rows + width) * columns, transcendentals=0
        ),
    )(*operands)


def attention_forward(query, key, value, bias):
    scores = jnp.einsum("qhd,khd->hqk", query, key, preferred_element_type=jnp.float32) * score_scale
    scores = scores + bias[None]
    top = jnp.max(scores, axis=-1, keepdims=True)
    terms = jnp.exp(scores - top)
    probs = terms / jnp.sum(terms, axis=-1, keepdims=True)
    attended = jnp.einsum(
        "hqk,khd->qhd", probs.astype(jnp.bfloat16), value, preferred_element_type=jnp.float32
    )
    return attended, probs


def attention_backward(query, key, value, probs, grad_out):
    grad_probs = jnp.einsum("qhd,khd->hqk", grad_out, value, preferred_element_type=jnp.float32)
    delta = jnp.sum(probs * grad_probs, axis=-1, keepdims=True)
    grad_scores = (probs * (grad_probs - delta) * score_scale).astype(jnp.bfloat16)
    grad_query = jnp.einsum("hqk,khd->qhd", grad_scores, key, preferred_element_type=jnp.float32)
    grad_key = jnp.einsum("hqk,qhd->khd", grad_scores, query, preferred_element_type=jnp.float32)
    grad_value = jnp.einsum(
        "hqk,qhd->khd", probs.astype(jnp.bfloat16), grad_out, preferred_element_type=jnp.float32
    )
    return grad_query, grad_key, grad_value


def lane_tables(tables):
    cosine, sine_table = tables[0][:, 0], tables[1][:, 0]
    return (
        jnp.concatenate([cosine] * (LANES // cosine.shape[1]), axis=1),
        jnp.concatenate([-sine_table, sine_table] * (LANES // HEAD_DIM), axis=1),
    )


def forward_attention(normed, weight, plan, bias, tables, kernels):
    width = plan.head_width
    rows = normed.shape[0]
    if kernels:
        columns = (3 * width + LANES - 1) // LANES * LANES
        wide = (width + LANES - 1) // LANES * LANES
        sized = jax.ShapeDtypeStruct
        return (
            functools.partial(attend_kernel, plan.head_count),
            [normed, weight, *lane_tables(tables), bias],
            [
                sized((rows, columns), jnp.bfloat16),
                sized((rows, width), jnp.bfloat16),
                sized((rows, LANES), jnp.float32),
            ],
            [pltpu.VMEM((rows, wide), jnp.bfloat16)],
            (rows, weight.shape[0]),
        ), None
    head_shape = (rows, plan.head_count, HEAD_DIM)
    mixed = times(normed, weight[:, : 3 * width])
    query = rotate(mixed[:, :width].reshape(head_shape), tables, 1.0).astype(jnp.bfloat16)
    key = rotate(mixed[:, width : 2 * width].reshape(head_shape), tables, 1.0).astype(jnp.bfloat16)
    value = mixed[:, 2 * width :].reshape(head_shape).astype(jnp.bfloat16)
    attended, probs = attention_forward(query, key, value, bias)
    attended = attended.reshape(rows, width).astype(jnp.bfloat16)
    partial_sum = times_transposed(attended, weight[:, 3 * width :]).astype(jnp.bfloat16)
    return partial_sum, (normed, query, key, value, probs, attended)


def feed_kernel(normed_ref, gate_ref, up_ref, down_ref, partial_ref, gating_ref, upward_ref, activated_ref):
    normed = normed_ref[...]
    for first in range(0, gating_ref.shape[1], 2 * LANES):
        tile = slice(first, first + 2 * LANES)
        gating, upward = times(normed, gate_ref[:, tile]), times(normed, up_ref[:, tile])
        gating_ref[:, tile] = gating
        upward_ref[:, tile] = upward
        activated_ref[:, tile] = (jax.nn.silu(gating) * upward).astype(jnp.bfloat16)
    activated = activated_ref[...]
    for first in range(0, partial_ref.shape[1], 2 * LANES):
        tile = slice(first, first + 2 * LANES)
        partial_ref[:, tile] = times_transposed(activated, down_ref[tile, :]).astype(jnp.bfloat16)


def feed_prelude(normed, weights):
    rows, width = normed.shape
    units = weights[0].shape[1]
    sized = jax.ShapeDtypeStruct
    wide = sized((rows, units), jnp.float32)
    return (feed_kernel, [normed, *weights], [wide, wide, sized((rows, units), jnp.bfloat16)], [], (rows, width))


def forward_feed(normed, weights):
    gate_weight, up_weight, down_weight = weights
    gating, upward = times(normed, gate_weight), times(normed, up_weight)
    activated = (jax.nn.silu(gating) * upward).astype(jnp.bfloat16)
    partial_sum = times_transposed(activated, down_weight).astype(jnp.bfloat16)
    return partial_sum, (normed, gating, upward, activated)


def backward_feed(down_grad, weights, record):
    gate_weight, up_weight, down_weight = weights
    normed, gating, upward, activated = record
    grad_act = times(down_grad, down_weight)
    sigmoid_gate = jax.nn.sigmoid(gating)
    grad_gating = (grad_act * upward * sigmoid_gate * (1.0 + gating * (1.0 - sigmoid_gate))).astype(jnp.bfloat16)
    grad_upward = (grad_act * gating * sigmoid_gate).astype(jnp.bfloat16)
    partial_sum = (times_transposed(grad_gating, gate_weight) + times_transposed(grad_upward, up_weight)).astype(
        jnp.bfloat16
    )
    return partial_sum, ((normed, grad_gating), (normed, grad_upward), (down_grad, activated))


def backward_attention(branch_grad, weight, record, plan, bias, tables, kernels):
    width = plan.head_width
    rows = branch_grad.shape[0]
    if kernels:
        normed, mixed, attended, total = record
        wide = (width + LANES - 1) // LANES * LANES
        sized = jax.ShapeDtypeStruct
        partial_sum, grad_all = local_call(
            functools.partial(attend_back_kernel, plan.head_count),
            "attend_back",
            [branch_grad, weight, mixed, total, *lane_tables(tables), bias],
            [sized((rows, weight.shape[0]), jnp.bfloat16), sized(mixed.shape, jnp.bfloat16)],
            [pltpu.VMEM((rows, wide), jnp.bfloat16), pltpu.VMEM((rows, 2 * width), jnp.float32)],
            4 * rows * weight.shape[0] * weight.shape[1],
        )
        return partial_sum, ((normed, grad_all[:, : 3 * width]), (branch_grad, attended))
    normed, query, key, value, probs, attended = record
    grad_mixed = times(branch_grad, weight[:, 3 * width :]).astype(jnp.bfloat16)
    grad_query, grad_key, grad_value = attention_backward(
        query, key, value, probs, grad_mixed.reshape(query.shape)
    )
    grad_all = jnp.concatenate(
        [
            rotate(grad_query, tables, -1.0).reshape(rows, width),
            rotate(grad_key, tables, -1.0).reshape(rows, width),
            grad_value.reshape(rows, width),
        ],
        axis=1,
    ).astype(jnp.bfloat16)
    partial_sum = times_transposed(grad_all, weight[:, : 3 * width]).astype(jnp.bfloat16)
    return partial_sum, ((normed, grad_all), (branch_grad, attended))


def body(
    inputs,
    cotangent,
    lengths,
    dealing,
    span_table,
    prenorm_gain,
    query_weight,
    keys_weight,
    values_weight,
    project_weight,
    postnorm_gain,
    gating_weight,
    upward_weight,
    downward_weight,
):
    n_dp, n_ctx, n_ten = lax.axis_size("dp"), lax.axis_size("ctx"), lax.axis_size("tensor")
    plan = Plan(n_dp, n_ctx, query_weight.shape[2], gating_weight.shape[2])
    own_rows = inputs.shape[0]
    half_span = own_rows // 2
    share = own_rows // n_ten
    group_index = lax.axis_index("dp")
    core = lax.axis_index("tensor")
    seq_count = lengths.shape[0] // n_dp
    starts, seq_lens = group_layout(lengths, dealing, group_index, seq_count)
    span_row = lax.dynamic_index_in_dim(span_table, group_index, 0, keepdims=False)
    facts = slot_facts(slots_for(own_rows * n_ctx, span_row, half_span), starts, seq_lens)
    tables = rope_tables(facts[2], HEAD_DIM // 2)
    bias = jnp.where(allowed(facts, facts), 0.0, masked_score)

    kernels = (n_dp, n_ctx, n_ten) == (4, 4, 2)
    comm = LineComm() if kernels else PlainComm()
    head_cuts = [cut * HEAD_DIM for cut in plan.head_cuts]

    attention_stack = [query_weight, keys_weight, values_weight, project_weight.transpose(0, 2, 1)]
    feed_stack = [gating_weight, upward_weight, downward_weight.transpose(0, 2, 1)]

    def windows(layer):
        if kernels:
            return cut_layer(plan, layer, attention_stack, feed_stack)
        attention = [cut_windows(weight[layer], head_cuts, plan.head_width) for weight in attention_stack]
        feed = [cut_windows(weight[layer], plan.unit_cuts, plan.unit_width) for weight in feed_stack]
        return [jnp.concatenate(attention, axis=2)] + feed

    def joined(blocks):
        return blocks.reshape(-1, blocks.shape[-1])

    own_gains = jnp.pad(
        jnp.concatenate([prenorm_gain, postnorm_gain], axis=0).T, ((0, 0), (0, LANES - 2 * LAYERS))
    )
    own_gains = jnp.broadcast_to(own_gains[None], (n_ctx,) + own_gains.shape)
    attention_windows, gate, up, down = windows(0)
    attention_blocks, gain_blocks, inputs_whole, gate, up, down = comm.moves(
        (Fetch, attention_windows),
        (Fetch, own_gains),
        (Collect, inputs),
        (Fetch, gate),
        (Exchange, up),
        (Exchange, down),
        urgent=3,
    )
    gains = gain_blocks.reshape(-1, LANES)[:, : 2 * LAYERS].T.astype(jnp.float32)
    front = [gains[layer : layer + 1] for layer in range(LAYERS)]
    behind = [gains[LAYERS + layer : LAYERS + layer + 1] for layer in range(LAYERS)]
    attention_weights, feed_weights = [None] * LAYERS, [None] * LAYERS
    attention_records, feed_records, middles = [None] * LAYERS, [None] * LAYERS, [None] * LAYERS
    starts_of = [None] * LAYERS

    attention_weights[0] = joined(attention_blocks)
    residual = comm.own_rows(inputs_whole).astype(jnp.float32)
    normed = (rms_parts(inputs_whole.astype(jnp.float32))[0] * front[0]).astype(jnp.bfloat16)
    for layer in range(LAYERS):
        starts_of[layer] = residual
        more = layer + 1 < LAYERS
        partial_sum, attention_records[layer] = forward_attention(
            normed, attention_weights[layer], plan, bias, tables, kernels
        )
        prelude = partial_sum if kernels else None
        jobs = [(Spread, up, 6, 2), (Spread, down, 14, 2)]
        if more:
            next_windows = windows(layer + 1)
            jobs += [(Exchange, next_windows[0]), (Exchange, next_windows[1])]
        else:
            jobs += [(Collect, cotangent, 5, 4)]
        hidden, normed_two, (up, down, *moved), made = comm.forward(
            None if kernels else partial_sum, residual, behind[layer], jobs, prelude
        )
        if kernels:
            attention_records[layer] = (normed, *made)
        normed = normed_two
        feed_weights[layer] = [joined(blocks) for blocks in (gate, up, down)]
        middles[layer] = hidden
        if more:
            jobs = [
                (Spread, moved[0], 8, 3),
                (Spread, moved[1], 19, 2),
                (Exchange, next_windows[2]),
                (Exchange, next_windows[3]),
            ]
            prelude, partial_sum = None, None
            if kernels:
                prelude = feed_prelude(normed, feed_weights[layer])
            else:
                partial_sum, feed_records[layer] = forward_feed(normed, feed_weights[layer])
            residual, normed_next, moved, made = comm.forward(partial_sum, hidden, front[layer + 1], jobs, prelude)
            if kernels:
                feed_records[layer] = (normed, *made)
            normed = normed_next
            attention_weights[layer + 1] = joined(moved[0])
            gate, up, down = moved[1:]
        else:
            last_sum, feed_records[layer] = forward_feed(normed, feed_weights[layer])
            cotangent_whole = moved[0]

    grad_rows = comm.own_rows(cotangent_whole).astype(jnp.float32)
    down_grad = (depth_scale * cotangent_whole.astype(jnp.float32)).astype(jnp.bfloat16)
    gain_fronts, gain_backs, attention_parts, feed_parts = [[None] * LAYERS for _ in range(4)]
    for layer in reversed(range(LAYERS)):
        more, last_layer = layer > 0, layer + 1 == LAYERS
        partial_sum, pairs = backward_feed(down_grad, feed_weights[layer], feed_records[layer])
        sums = outer_sums(*pairs)
        partial_sum, sums = lax.optimization_barrier((partial_sum, sums))
        feed_parts[layer] = reduce_grads(sums, n_ctx)
        jobs = [] if last_layer else [(Exchange, feed_parts[layer + 1])]
        grad_rows, gain_backs[layer], branch_grad, moved = comm.backward(
            partial_sum, middles[layer], grad_rows, behind[layer], jobs
        )
        if not last_layer:
            feed_parts[layer + 1] = moved[0]
        partial_sum, pairs = backward_attention(
            branch_grad, attention_weights[layer], attention_records[layer], plan, bias, tables, kernels
        )
        sums = outer_sums(*pairs)
        partial_sum, sums = lax.optimization_barrier((partial_sum, sums))
        attention_parts[layer] = reduce_grads(sums, n_ctx)
        if more:
            grad_rows, gain_fronts[layer], down_grad, _ = comm.backward(
                partial_sum, starts_of[layer], grad_rows, front[layer], []
            )
        else:
            others = jnp.concatenate(gain_fronts[1:] + gain_backs, axis=0)
            jobs = [(Exchange, attention_parts[layer + 1])]
            grad_inputs, gain_sums, moved = comm.backward_last(
                partial_sum, starts_of[layer], grad_rows, front[layer], jobs, others
            )
            attention_parts[layer + 1] = moved[0]
    last_sum, grad_inputs = lax.optimization_barrier((last_sum, grad_inputs))
    output, moved = comm.last(last_sum, middles[LAYERS - 1], [(Exchange, feed_parts[0])])
    feed_parts[0] = moved[0]
    attention_parts[0], output = lax.optimization_barrier((attention_parts[0], output))
    (attention_parts[0],) = comm.moves((Exchange, attention_parts[0]))
    grad_inputs = grad_inputs.astype(jnp.float32)
    gain_sums = lax.psum(gain_sums, "tensor")

    if kernels:
        joins = join_layers(plan, list(zip(attention_parts, feed_parts)))
    else:

        def spread(parts, index, width, cuts):
            return jnp.stack(
                [join_windows(part[:, :, index * width : (index + 1) * width], cuts) for part in parts]
            ).astype(jnp.float32)

        joins = [spread(attention_parts, i, plan.head_width, head_cuts) for i in range(4)]
        joins += [spread(feed_parts, i, plan.unit_width, plan.unit_cuts) for i in range(3)]
    query_out, keys_out, values_out, project_out, gating_out, upward_out, downward_out = joins
    return (
        output,
        grad_inputs,
        gain_sums[:LAYERS],
        query_out,
        keys_out,
        values_out,
        project_out.transpose(0, 2, 1),
        gain_sums[LAYERS:],
        gating_out,
        upward_out,
        downward_out.transpose(0, 2, 1),
    )


def solution(mesh):
    rows = P(("dp", "ctx"), None)
    gain = P(None, ("dp", "ctx"))
    wide = P(None, ("dp", "ctx"), "tensor")
    tall = P(None, "tensor", ("dp", "ctx"))
    weights = (gain, wide, wide, wide, tall, gain, wide, wide, tall)
    return jax.shard_map(
        body,
        mesh=mesh,
        in_specs=(rows, rows, P(), P(), P()) + weights,
        out_specs=(rows, rows) + weights,
        check_vma=False,
    )
```

time: 1220 us -> 928 us (0.76)
  waiting for transfers between devices: 132 us -> 0.09 us
  matrix products: 149 us -> 32.5 us
  Pallas kernels: 727 us -> 785 us
  blocking collectives: 42.8 us -> 4.5 us
  local copies, waits for them, and re-layouts: 99.1 us -> 71.1 us
  other arithmetic: 43.8 us -> 16.7 us
    reduce_scatter x4, waiting for transfers between devices: 69 us -> 0.02 us  [reduce_grads(): own = lax.psum_scatter(full, 'dp', scatter_dimension=0, tiled=True)]
    pallas_call x12 -> x15, Pallas kernels: 695 us -> 753 us  [the longest x8 554 us: line_call(): pl.pallas_call(functools.partial(line_kernel, (kernel, len(prelude_in), l...]
    dot_general x10 -> x0, matrix products: 52.4 us -> none  [the longest x2 18.5 us: attention_backward(): jnp.einsum('hqk,khd->qhd', grad_scores, key, preferred_element_type=jnp.f...]
    all_gather x1 -> x0, blocking collectives: 40.4 us -> none  [body(): lax.all_gather(jnp.concatenate([prenorm_gain, postnorm_gain], axis=0), ('...]
    dot_general x8 -> x4, matrix products: 44.4 us -> 11.2 us  [times(): return jnp.dot(left, right, preferred_element_type=jnp.float32)]
    unnamed x12 -> x4, waiting for transfers between devices: 28.5 us -> 0.07 us
    unnamed x266 -> x217, local copies, waits for them, and re-layouts: 43.5 us -> 69.8 us
    all_gather x6 -> x0, waiting for transfers between devices: 25 us -> none  [the longest x4 18.7 us: spread_weights(): lax.all_gather(blocks.reshape(-1, blocks.shape[-1]), 'dp', axis=0, tiled=...]
  transfers between devices with their start and end apart: 13 -> 4, of which waited for: 5 -> 0; matrix products, arithmetic and copies ran while one was open for 19% -> 3% of each run, Pallas kernels for 51% -> 40%
where the time goes in v2:
time: 928 us; the launch traced here: 925 us
  Pallas kernels  785 us (85%)
  local copies, waits for them, and re-layouts  71.1 us (8%)
  matrix products  32.5 us (4%)
  other arithmetic  16.7 us (2%)
  between operations  14.9 us (2%)
    pallas_call x8, Pallas kernels, line_call(): pl.pallas_call(functools.partial(line_kernel, (kernel, len(prelude_in), l...  554 us
    pallas_call x2, Pallas kernels, jobs_call(): pl.pallas_call(functools.partial(jobs_kernel, [job[0] for job in jobs], c...  157 us
    unnamed x217, local copies, waits for them, and re-layouts  69.8 us
    pallas_call x3, Pallas kernels, local_call(): pl.pallas_call(kernel, name=name, out_shape=tuple(outs), in_specs=[vmem]...  38.8 us
    pallas_call x4, Pallas kernels, outer_sums(): pl.pallas_call(outer_kernel, name='outer_sums', grid=(width // tile,), ou...  32.1 us
    dot_general x5, matrix products, times_transposed(): lax.dot_general(left, right, (((1,), (1,)), ((), ())), preferred_element_...  21.3 us
  transfers between devices with their start and end apart: 4, of which 0 were waited for; matrix products, arithmetic and copies ran while one was open for 3% of the time, Pallas kernels for 40%

profile of v2, /device:TPU:0, one launch (start us, length us, event | category | flops | bytes accessed | tf_op | source)
XLA Modules:
  0.0 924.7 jit_solution(989921354755558834)
XLA Ops:
  28.0 113.5 %moves.2 = (bf16[16,144,1280]{2,1,0:T(8,128)(2,1)}, bf16[16,144,128]{2,1,0:T(8,128)(2,1)S(1)}, bf16[512,2304]{1,0:T(8,128)(2,1)}, bf16[16,144,768]{2,1,0:T(8,128...) custom-call(bf16[4,144,1280]{2,1,0:T(8,128)(2,1)} %copy-done.44, ...), custom_call_target="tpu_custom_call" | custom-call | flops 1000000000 | bytes 100000000 | tf_op jit(solution)/shard_map/moves/pallas_call | solution.py:634
  143.3 2.2 fusion
  148.6 3.8 fusion.2.refs_0_
  153.0 87.0 %forward_line.3 = (bf16[512,1024]{1,0:T(8,128)(2,1)S(1)}, bf16[512,320]{1,0:T(8,128)(2,1)S(1)}, f32[512,128]{1,0:T(8,128)S(1)}, f32[128,2304]{1,0:T(8,128)S(1)},...) custom-call(bf16[512,2304]{1,0:T(8,128)(2,1)} %fusion.2.refs_0_, ...), custom_call_target="tpu_custom_call" | custom-call | flops 1000000000 | bytes 100000000 | tf_op jit(solution)/shard_map/forward_line/pallas_call | solution.py:962
  243.9 85.9 %forward_line.4 = (f32[512,768]{1,0:T(8,128)S(1)}, f32[512,768]{1,0:T(8,128)S(1)}, bf16[512,768]{1,0:T(8,128)(2,1)S(1)}, f32[128,2304]{1,0:T(8,128)S(1)}, bf16[5...) custom-call(bf16[512,2304]{1,0:T(8,128)(2,1)} %copy-done.35, ...), custom_call_target="tpu_custom_call" | custom-call | flops 1000000000 | bytes 100000000 | tf_op jit(solution)/shard_map/forward_line/pallas_call | solution.py:962
  332.5 66.7 %forward_line.5 = (bf16[512,1024]{1,0:T(8,128)(2,1)S(1)}, bf16[512,320]{1,0:T(8,128)(2,1)S(1)}, f32[512,128]{1,0:T(8,128)S(1)}, f32[128,2304]{1,0:T(8,128)S(1)},...) custom-call(bf16[512,2304]{1,0:T(8,128)(2,1)} %copy-done.5, ...), custom_call_target="tpu_custom_call" | custom-call | flops 1000000000 | bytes 100000000 | tf_op jit(solution)/shard_map/forward_line/pallas_call | solution.py:962
  404.3 2.0 fusion.16
  406.3 2.0 fusion.20
  408.3 2.5 multiply_convert_fusion.3
  410.8 2.0 fusion.21
  412.9 3.6 fusion.3.refs_0_
  416.4 9.5 %outer_sums.4 = bf16[2304,2304]{1,0:T(8,128)(2,1)} custom-call(bf16[512,2304]{1,0:T(8,128)(2,1)S(1)} %get-tuple-element.116.refs_0_.refs_2_, bf16[512,768]{1,0:T(8,128)(2,1)S(1)} %get-tuple-element.172.refs_1_, bf16[512,2304]{1,0:T(8,128)(2,1)S(1)} %get-tuple-element.116.refs_0_.refs_2_, bf16[512,768]{1,0:T(8,128)(2,1)S(1)} %get-tuple-element.173.refs_3_, ...), custom_call_target="tpu_custom_call" | custom-call | flops 5435817984 | bytes 12976128 | tf_op jit(solution)/shard_map/outer_sums/pallas_call | solution.py:1247
  429.1 40.0 %backward_line.3 = (f32[1,2304]{1,0:T(1,128)S(1)}, f32[128,2304]{1,0:T(8,128)S(1)}, bf16[512,2304]{1,0:T(8,128)(2,1)S(1)}) custom-call(bf16[512,2304]{1,0:T(8,128)(2,1)S(1)} %copy-done.34, f32[128,2304]{1,0:T(8,128)S(1)} %copy-done.13, f32[128,2304]{1,0:T(8,128)S(1)} %dynamic-slice_convert_fusion.refs_2_, f32[1,2304]{1,0:T(1,128)S(1)} %get-tuple-element.176.refs_6_.refs_3_), custom_call_target="tpu_custom_call" | custom-call | flops 1000000000 | bytes 100000000 | tf_op jit(solution)/shard_map/backward_line/pallas_call | solution.py:962
  472.8 15.1 %attend_back.2 = (bf16[512,2304]{1,0:T(8,128)(2,1)}, bf16[512,1024]{1,0:T(8,128)(2,1)S(1)}) custom-call(bf16[512,2304]{1,0:T(8,128)(2,1)} %copy-done.39, bf16[2304,1280]{1,0:T(8,128)(2,1)} %bitcast.56, bf16[512,1024]{1,0:T(8,128)(2,1)S(1)} %copy-done.90, f32[512,128]{1,0:T(8,128)S(1)} %copy-done.96, f32[512,128]{1,0:T(8,128)S(1)} %copy-done.26, ...), custom_call_target="tpu_custom_call" | custom-call | flops 6039797760 | bytes 20000000 | tf_op jit(solution)/shard_map/attend_back/pallas_call | solution.py:1216
  488.0 6.5 outer_sums.5
  494.5 2.5 copy-done.2
  501.5 40.7 %backward_line.4 = (f32[1,2304]{1,0:T(1,128)S(1)}, f32[128,2304]{1,0:T(8,128)S(1)}, bf16[512,2304]{1,0:T(8,128)(2,1)S(1)}) custom-call(bf16[512,2304]{1,0:T(8,128)(2,1)S(1)} %copy-done.33, f32[128,2304]{1,0:T(8,128)S(1)} %copy-done.11, f32[128,2304]{1,0:T(8,128)S(1)} %copy-done.52, f32[1,2304]{1,0:T(1,128)S(1)} %get-tuple-element.177.refs_5_.refs_3_), custom_call_target="tpu_custom_call" | custom-call | flops 1000000000 | bytes 100000000 | tf_op jit(solution)/shard_map/backward_line/pallas_call | solution.py:962
  542.3 4.7 multiply_convert_fusion.1
  547.1 4.2 fusion.22
  551.3 9.6 %outer_sums.6 = bf16[2304,2304]{1,0:T(8,128)(2,1)} custom-call(bf16[512,2304]{1,0:T(8,128)(2,1)S(1)} %copy-done.36, bf16[512,768]{1,0:T(8,128)(2,1)S(1)} %get-tuple-element.170.refs_1_, bf16[512,2304]{1,0:T(8,128)(2,1)S(1)} %copy-done.36, bf16[512,768]{1,0:T(8,128)(2,1)S(1)} %get-tuple-element.169.refs_3_, bf16[512,2304]{1,0:T(8,128)(2,1)S(1)} %get-tuple-element.129.refs_4_, ...), custom_call_target="tpu_custom_call" | custom-call | flops 5435817984 | bytes 12976128 | tf_op jit(solution)/shard_map/outer_sums/pallas_call | solution.py:1247
  560.9 7.2 fusion.4.refs_0_
  573.0 91.4 %backward_line.5 = (f32[1,2304]{1,0:T(1,128)S(1)}, f32[128,2304]{1,0:T(8,128)S(1)}, bf16[512,2304]{1,0:T(8,128)(2,1)S(1)}, bf16[4,144,2304]{2,1,0:T(8,128)(2,1)S(1)}) custom-call(bf16[512,2304]{1,0:T(8,128)(2,1)S(1)} %copy-done.31, f32[128,2304]{1,0:T(8,128)S(1)} %get-tuple-element.104.refs_4_.refs_1_, f32[128,2304]{1,0:T(8,128)S(1)} %copy-done.50, ...), custom_call_target="tpu_custom_call" | custom-call | flops 1000000000 | bytes 100000000 | tf_op jit(solution)/shard_map/backward_line/pallas_call | solution.py:962
  669.7 14.8 %attend_back.3 = (bf16[512,2304]{1,0:T(8,128)(2,1)}, bf16[512,1024]{1,0:T(8,128)(2,1)S(1)}) custom-call(bf16[512,2304]{1,0:T(8,128)(2,1)} %copy-done.37, bf16[2304,1280]{1,0:T(8,128)(2,1)} %bitcast.54, bf16[512,1024]{1,0:T(8,128)(2,1)S(1)} %copy-done.88, f32[512,128]{1,0:T(8,128)S(1)} %copy-done.94, f32[512,128]{1,0:T(8,128)S(1)} %copy-done.27, ...), custom_call_target="tpu_custom_call" | custom-call | flops 6039797760 | bytes 20000000 | tf_op jit(solution)/shard_map/attend_back/pallas_call | solution.py:1216
  684.6 6.5 outer_sums.7
  691.1 2.5 copy-done.3
  693.6 4.3 convolution_convert_fusion.refs_0_
  703.7 60.5 %backward_last_line.1 = (f32[1,2304]{1,0:T(1,128)}, bf16[128,2304]{1,0:T(8,128)(2,1)S(1)}, bf16[4,144,1280]{2,1,0:T(8,128)(2,1)S(1)}, f32[16,8,256]{2,1,0:T(8,128)S(1)}) custom-call(bf16[512,2304]{1,0:T(8,128)(2,1)S(1)} %copy-done.32, f32[128,2304]{1,0:T(8,128)S(1)} %dynamic-slice_convert_fusion.1.refs_5_.refs_1_, f32[128,2304]{1,0:T(8,128)S(1)} %copy-done.48, ...), custom_call_target="tpu_custom_call" | custom-call | flops 1000000000 | bytes 100000000 | tf_op jit(solution)/shard_map/backward_last_line/pallas_call | solution.py:962
  767.8 2.2 convert_element_type.133
  770.0 4.5 psum.7
  776.2 82.2 %last_line.1 = (bf16[128,2304]{1,0:T(8,128)(2,1)S(1)}, bf16[4,144,2304]{2,1,0:T(8,128)(2,1)S(1)}) custom-call(bf16[512,2304]{1,0:T(8,128)(2,1)S(1)} %convolution_convert_fusion.refs_0_, f32[128,2304]{1,0:T(8,128)S(1)} %copy-done.14, bf16[4,144,2304]{2,1,0:T(8,128)(2,1)S(1)} %bitcast.45), custom_call_target="tpu_custom_call" | custom-call | flops 1000000000 | bytes 100000000 | tf_op jit(solution)/shard_map/last_line/pallas_call | solution.py:962
  862.9 43.9 %moves.3.refs_0_ = bf16[4,144,1280]{2,1,0:T(8,128)(2,1)S(1)} custom-call(bf16[4,144,1280]{2,1,0:T(8,128)(2,1)S(1)} %bitcast.52), custom_call_target="tpu_custom_call" | custom-call | flops 1000000000 | bytes 100000000 | tf_op jit(solution)/shard_map/moves/pallas_call | solution.py:634
  908.2 8.9 join_layers.1
  (253 shorter events, 76.8 us)
Async XLA Ops:
  7.2 17.3 %copy-start = (s32[4,8]{1,0:T(4,128)S(1)}, s32[4,8]{1,0:T(4,128)}, u32[]{:S(2)}) copy-start(s32[4,8]{1,0:T(4,128)} %param.18) | copy-start | bytes 388
  7.2 561.0 %reduce-scatter.5.cloned.1.call-start = ((), (), s32[]{:S(2)}) async-start(), calls=%async_computation.4 | async-start | bytes 13271040 | tf_op jit(solution)/shard_map/reduce_scatter | solution.py:206
  152.9 179.5 %copy-start.25 = (f32[512,128]{1,0:T(8,128)}, f32[512,128]{1,0:T(8,128)S(1)}, u32[]{:S(2)}) copy-start(f32[512,128]{1,0:T(8,128)S(1)} %get-tuple-element.186.refs_2_.cosine_ref) | copy-start | bytes 786436
  153.0 179.5 %copy-start.28 = (f32[512,128]{1,0:T(8,128)}, f32[512,128]{1,0:T(8,128)S(1)}, u32[]{:S(2)}) copy-start(f32[512,128]{1,0:T(8,128)S(1)} %get-tuple-element.187.refs_3_.sine_ref) | copy-start | bytes 786436
  153.0 90.9 %copy-start.56 = (bf16[4,144,768]{2,1,0:T(8,128)(2,1)S(1)}, bf16[4,144,768]{2,1,0:T(8,128)(2,1)}, u32[]{:S(2)}) copy-start(bf16[4,144,768]{2,1,0:T(8,128)(2,1)} %copy-done.55) | copy-start | bytes 2654212
  153.0 90.9 %copy-start.58 = (bf16[4,144,768]{2,1,0:T(8,128)(2,1)S(1)}, bf16[4,144,768]{2,1,0:T(8,128)(2,1)}, u32[]{:S(2)}) copy-start(bf16[4,144,768]{2,1,0:T(8,128)(2,1)} %copy-done.57) | copy-start | bytes 2654212
  243.9 88.5 %copy-start.66 = (bf16[128,2304]{1,0:T(8,128)(2,1)S(1)}, bf16[128,2304]{1,0:T(8,128)(2,1)}, u32[]{:S(2)}) copy-start(bf16[128,2304]{1,0:T(8,128)(2,1)} %refs_9_.1) | copy-start | bytes 1769476
  332.4 66.7 %copy-start.10 = (f32[128,2304]{1,0:T(8,128)}, f32[128,2304]{1,0:T(8,128)S(1)}, u32[]{:S(2)}) copy-start(f32[128,2304]{1,0:T(8,128)S(1)} %get-tuple-element.111.refs_5_.refs_1_) | copy-start | bytes 3538948
  332.4 66.7 %copy-start.84 = (f32[512,768]{1,0:T(8,128)}, f32[512,768]{1,0:T(8,128)S(1)}, u32[]{:S(2)}) copy-start(f32[512,768]{1,0:T(8,128)S(1)} %get-tuple-element.130) | copy-start | bytes 4718596
  332.4 66.7 %copy-start.91 = (bf16[512,768]{1,0:T(8,128)(2,1)}, bf16[512,768]{1,0:T(8,128)(2,1)S(1)}, u32[]{:S(2)}) copy-start(bf16[512,768]{1,0:T(8,128)(2,1)S(1)} %get-tuple-element.132.refs_5_) | copy-start | bytes 2359300
  426.0 272.7 %reduce-scatter.9.cloned.1.call-start = ((), (), s32[]{:S(2)}) async-start(), calls=%async_computation.6 | async-start | bytes 7372800 | tf_op jit(solution)/shard_map/reduce_scatter | solution.py:206
  429.1 42.5 %copy-start.26 = (f32[512,128]{1,0:T(8,128)S(1)}, f32[512,128]{1,0:T(8,128)}, u32[]{:S(2)}) copy-start(f32[512,128]{1,0:T(8,128)} %copy-done.25) | copy-start | bytes 786436
  429.1 42.5 %copy-start.29 = (f32[512,128]{1,0:T(8,128)S(1)}, f32[512,128]{1,0:T(8,128)}, u32[]{:S(2)}) copy-start(f32[512,128]{1,0:T(8,128)} %copy-done.28) | copy-start | bytes 786436
  429.1 42.5 %copy-start.96 = (f32[512,128]{1,0:T(8,128)S(1)}, f32[512,128]{1,0:T(8,128)}, u32[]{:S(2)}) copy-start(f32[512,128]{1,0:T(8,128)} %copy-done.95) | copy-start | bytes 786436
  471.6 16.4 %copy-start.76 = (f32[1,2304]{1,0:T(1,128)}, f32[1,2304]{1,0:T(1,128)S(1)}, u32[]{:S(2)}) copy-start(f32[1,2304]{1,0:T(1,128)S(1)} %get-tuple-element.148) | copy-start | bytes 27652
  472.8 15.2 %copy-start.6 = (bf16[512,2304]{1,0:T(8,128)(2,1)S(1)}, bf16[512,2304]{1,0:T(8,128)(2,1)}, u32[]{:S(2)}) copy-start(bf16[512,2304]{1,0:T(8,128)(2,1)} %copy-done.5) | copy-start | bytes 7077892
  472.8 15.2 %copy-start.40 = (bf16[512,2304]{1,0:T(8,128)(2,1)S(1)}, bf16[512,2304]{1,0:T(8,128)(2,1)}, u32[]{:S(2)}) copy-start(bf16[512,2304]{1,0:T(8,128)(2,1)} %copy-done.39) | copy-start | bytes 7077892
  472.8 15.2 %copy-start.73 = (bf16[512,320]{1,0:T(8,128)(2,1)S(1)}, bf16[512,320]{1,0:T(8,128)(2,1)}, u32[]{:S(2)}) copy-start(bf16[512,320]{1,0:T(8,128)(2,1)} %copy-done.72) | copy-start | bytes 983044
  497.0 277.5 %reduce-scatter.11.cloned.1.call-start = ((), (), s32[]{:S(2)}) async-start(), calls=%async_computation.7 | async-start | bytes 13271040 | tf_op jit(solution)/shard_map/reduce_scatter | solution.py:206
  501.5 40.7 %copy-start.83 = (f32[512,768]{1,0:T(8,128)S(1)}, f32[512,768]{1,0:T(8,128)}, u32[]{:S(2)}) copy-start(f32[512,768]{1,0:T(8,128)} %copy-done.82) | copy-start | bytes 4718596
  501.5 40.7 %copy-start.85 = (f32[512,768]{1,0:T(8,128)S(1)}, f32[512,768]{1,0:T(8,128)}, u32[]{:S(2)}) copy-start(f32[512,768]{1,0:T(8,128)} %copy-done.84) | copy-start | bytes 4718596
  568.2 293.2 %reduce-scatter.7.cloned.1.call-start = ((), (), s32[]{:S(2)}) async-start(), calls=%async_computation.5 | async-start | bytes 7372800 | tf_op jit(solution)/shard_map/reduce_scatter | solution.py:206
  573.0 95.4 %copy-start.27 = (f32[512,128]{1,0:T(8,128)S(1)}, f32[512,128]{1,0:T(8,128)}, u32[]{:S(2)}) copy-start(f32[512,128]{1,0:T(8,128)} %copy-done.25) | copy-start | bytes 786436
  573.0 95.4 %copy-start.30 = (f32[512,128]{1,0:T(8,128)S(1)}, f32[512,128]{1,0:T(8,128)}, u32[]{:S(2)}) copy-start(f32[512,128]{1,0:T(8,128)} %copy-done.28) | copy-start | bytes 786436
  573.0 95.4 %copy-start.94 = (f32[512,128]{1,0:T(8,128)S(1)}, f32[512,128]{1,0:T(8,128)}, u32[]{:S(2)}) copy-start(f32[512,128]{1,0:T(8,128)} %copy-done.93) | copy-start | bytes 786436
  668.4 16.1 %copy-start.80 = (f32[1,2304]{1,0:T(1,128)}, f32[1,2304]{1,0:T(1,128)S(1)}, u32[]{:S(2)}) copy-start(f32[1,2304]{1,0:T(1,128)S(1)} %get-tuple-element.147) | copy-start | bytes 27652
  669.7 14.8 %copy-start.4 = (bf16[512,2304]{1,0:T(8,128)(2,1)S(1)}, bf16[512,2304]{1,0:T(8,128)(2,1)}, u32[]{:S(2)}) copy-start(bf16[512,2304]{1,0:T(8,128)(2,1)} %fusion.2.refs_0_) | copy-start | bytes 7077892
  669.7 14.8 %copy-start.38 = (bf16[512,2304]{1,0:T(8,128)(2,1)S(1)}, bf16[512,2304]{1,0:T(8,128)(2,1)}, u32[]{:S(2)}) copy-start(bf16[512,2304]{1,0:T(8,128)(2,1)} %copy-done.37) | copy-start | bytes 7077892
  669.7 14.8 %copy-start.71 = (bf16[512,320]{1,0:T(8,128)(2,1)S(1)}, bf16[512,320]{1,0:T(8,128)(2,1)}, u32[]{:S(2)}) copy-start(bf16[512,320]{1,0:T(8,128)(2,1)} %copy-done.70) | copy-start | bytes 983044
  861.4 45.4 %copy-start.20 = (bf16[4,144,2304]{2,1,0:T(8,128)(2,1)S(1)}, bf16[4,144,2304]{2,1,0:T(8,128)(2,1)}, u32[]{:S(2)}) copy-start(bf16[4,144,2304]{2,1,0:T(8,128)(2,1)} %copy-done.19) | copy-start | bytes 7962628
  908.2 8.9 copy-start.69
  908.2 9.7 %copy-start.1 = (s32[4,8]{1,0:T(4,128)S(1)}, s32[4,8]{1,0:T(4,128)}, u32[]{:S(2)}) copy-start(s32[4,8]{1,0:T(4,128)} %param.18) | copy-start | bytes 388
  (79 other events, 173.7 us)
Sparse Core Ops, SparseCore 0:
  426.1 103.3 reduce-scatter.4
  532.5 66.8 reduce-scatter.8
  602.5 104.5 reduce-scatter.10
  710.0 67.3 reduce-scatter.6

commit v3 on v2

--- a/solution.py
+++ b/solution.py
@@ -135,68 +135,131 @@
     )
 
 
-def cut_kernel(plan, *refs):
-    attention, feed, outs = refs[:4], refs[4:7], refs[7:]
-    for i, ref in enumerate(attention):
+def cut_attention(plan, sources, out):
+    for i, ref in enumerate(sources):
         for j, (first, last) in enumerate(zip(plan.head_cuts, plan.head_cuts[1:])):
             start, count = i * plan.head_width, (last - first) * HEAD_DIM
-            outs[0][j, :, start : start + count] = ref[0, :, first * HEAD_DIM : last * HEAD_DIM]
+            out[j, :, start : start + count] = ref[:, first * HEAD_DIM : last * HEAD_DIM]
             if count < plan.head_width:
-                outs[0][j, :, start + count : start + plan.head_width] = jnp.zeros(
-                    (ref.shape[1], plan.head_width - count), ref.dtype
+                out[j, :, start + count : start + plan.head_width] = jnp.zeros(
+                    (ref.shape[0], plan.head_width - count), ref.dtype
                 )
-    for ref, out in zip(feed, outs[1:]):
-        for j, (first, last) in enumerate(zip(plan.unit_cuts, plan.unit_cuts[1:])):
-            out[j, :, : last - first] = ref[0, :, first:last]
-            out[j, :, last - first :] = jnp.zeros((ref.shape[1], plan.unit_width - (last - first)), ref.dtype)
-
-
-def cut_layer(plan, layer, attention, feed):
-    specs = [
-        pl.BlockSpec((1,) + weight.shape[1:], lambda i, layer=layer: (layer, 0, 0)) for weight in attention + feed
-    ]
-    rows = attention[0].shape[1]
-    outs = [
-        jax.ShapeDtypeStruct((plan.n_ctx, rows, width), jnp.bfloat16)
-        for width in [4 * plan.head_width] + [plan.unit_width] * 3
-    ]
-    return pl.pallas_call(
-        functools.partial(cut_kernel, plan),
-        name="cut_layer",
-        grid=(1,),
-        out_shape=tuple(outs),
-        in_specs=specs,
-        out_specs=tuple(pl.BlockSpec(out.shape, lambda i: (0, 0, 0)) for out in outs),
-        compiler_params=pltpu.CompilerParams(vmem_limit_bytes=40 * 2**20),
-        cost_estimate=pl.CostEstimate(flops=0, bytes_accessed=8 * 10**6, transcendentals=0),
-    )(*attention, *feed)
+
+
+def cut_feed(plan, ref, out):
+    for j, (first, last) in enumerate(zip(plan.unit_cuts, plan.unit_cuts[1:])):
+        out[j, :, : last - first] = ref[:, first:last]
+        out[j, :, last - first :] = jnp.zeros((ref.shape[0], plan.unit_width - (last - first)), ref.dtype)
+
+
+def start_kernel(plan, *refs):
+    weights, refs = take(refs, 7)
+    (front_ref, behind_ref, inputs_ref), refs = take(refs, 3)
+    cuts, refs = take(refs, 4 * (LAYERS - 1))
+    results, refs = take(refs, 6)
+    raw, refs = take(refs, 7 * LAYERS)
+    (load_sems,), refs = take(refs, 1)
+    own_cuts, refs = take(refs, 4)
+    (gain_blocks,), refs = take(refs, 1)
+    loads = start_loads([ref.at[layer] for layer in range(LAYERS) for ref in weights], raw, load_sems)
+    greet(*place())
+    kinds = (Collect, Fetch, Fetch, Fetch, Exchange, Exchange)
+    sources = [inputs_ref, own_cuts[0], gain_blocks, *own_cuts[1:]]
+    jobs = make_jobs(kinds, [0] * 6, sources, results, refs)
+    jobs[0].start()
+    for copy in loads[:4]:
+        copy.wait()
+    cut_attention(plan, raw[:4], own_cuts[0])
+    jobs[1].start()
+    gain_blocks[...] = jnp.zeros(gain_blocks.shape, gain_blocks.dtype)
+    for j in range(gain_blocks.shape[0]):
+        gain_blocks[j, 0:LAYERS, : front_ref.shape[1]] = front_ref[...]
+        gain_blocks[j, LAYERS : 2 * LAYERS, : front_ref.shape[1]] = behind_ref[...]
+    jobs[2].start()
+    for i in range(3):
+        loads[4 + i].wait()
+        cut_feed(plan, raw[4 + i], own_cuts[1 + i])
+    steps = [job.steps() for job in jobs]
+    for i in range(3):
+        steps[0][i]()
+        steps[1][i]()
+    for i in range(3):
+        steps[2][i]()
+    jobs[3].start()
+    for act in steps[3][:3]:
+        act()
+    jobs[4].start()
+    jobs[5].start()
+    for act in steps[1][3:] + steps[2][3:]:
+        act()
+    for layer in range(1, LAYERS):
+        for copy in loads[7 * layer : 7 * layer + 7]:
+            copy.wait()
+        layer_raw, layer_cuts = raw[7 * layer : 7 * layer + 7], cuts[4 * (layer - 1) : 4 * layer]
+        cut_attention(plan, layer_raw[:4], layer_cuts[0])
+        for i in range(3):
+            cut_feed(plan, layer_raw[4 + i], layer_cuts[1 + i])
+    for act in steps[3][3:]:
+        act()
+    for job in jobs:
+        job.finish()
+
+
+def start_call(plan, number, weights, front, behind, inputs):
+    vmem, hbm = pl.BlockSpec(memory_space=pltpu.VMEM), pl.BlockSpec(memory_space=pltpu.HBM)
+    rows = weights[0].shape[1]
+    sized = jax.ShapeDtypeStruct
+    windows = [(plan.n_ctx, rows, width) for width in [4 * plan.head_width] + [plan.unit_width] * 3]
+    gain_shape = (plan.n_ctx, 16, (rows + LANES - 1) // LANES * LANES)
+    own = [sized(shape, jnp.bfloat16) for shape in windows]
+    gain_source = sized(gain_shape, jnp.bfloat16)
+    kinds = (Collect, Fetch, Fetch, Fetch, Exchange, Exchange)
+    sources = (inputs, own[0], gain_source, *own[1:])
+    results = [kind.result(source) for kind, source in zip(kinds, sources)]
+    dma = pltpu.SemaphoreType.DMA
+    outs = pl.pallas_call(
+        functools.partial(start_kernel, plan),
+        name="start",
+        out_shape=tuple(own * (LAYERS - 1) + results),
+        in_specs=[hbm] * 7 + [vmem] * 2 + [hbm],
+        out_specs=tuple([vmem] * 4 * (LAYERS - 1) + [hbm] * 6),
+        scratch_shapes=[pltpu.VMEM(weight.shape[1:], weight.dtype) for _ in range(LAYERS) for weight in weights]
+        + [dma((7 * LAYERS,))]
+        + [pltpu.VMEM(shape, jnp.bfloat16) for shape in windows + [gain_shape]]
+        + [dma((kind.semaphores,)) for kind in kinds],
+        compiler_params=pltpu.CompilerParams(
+            collective_id=number, has_side_effects=True, vmem_limit_bytes=START_MIB * 2**20
+        ),
+        cost_estimate=pl.CostEstimate(flops=10**9, bytes_accessed=100 * 10**6, transcendentals=0),
+    )(*weights, front, behind, inputs)
+    cuts, results = take(outs, 4 * (LAYERS - 1))
+    return [cuts[4 * i : 4 * i + 4] for i in range(LAYERS - 1)], results
 
 
 def join_kernel(plan, places, count, *refs):
     sources, outs = refs[:count], refs[count:]
-    for layer in range(LAYERS):
-        for i, out in enumerate(outs):
+    for source, (layer, top, weights) in zip(sources, places):
+        rows, start = source.shape[1], 0
+        for i in weights:
             cuts = [cut * HEAD_DIM for cut in plan.head_cuts] if i < 4 else plan.unit_cuts
-            which, start = places[layer][i]
             for j, (first, last) in enumerate(zip(cuts, cuts[1:])):
-                out[layer, :, first:last] = sources[which][j, :, start : start + last - first].astype(jnp.float32)
-
-
-def join_layers(plan, parts):
-    widths = [plan.head_width] * 4 + [plan.unit_width] * 3
+                outs[i][layer, top : top + rows, first:last] = source[j, :, start : start + last - first].astype(
+                    jnp.float32
+                )
+            start += plan.head_width if i < 4 else plan.unit_width
+
+
+def join_layers(plan, attention_parts, feed_parts):
     sources, places = [], []
-    for arrays in parts:
-        spots, queue = [], list(widths)
-        for array in arrays:
-            start = 0
-            while start < array.shape[2]:
-                spots.append((len(sources), start))
-                start += queue.pop(0)
-            sources.append(array)
-        places.append(spots)
-    rows = sources[0].shape[1]
+    for parts_of, weights in ((attention_parts, (0, 1, 2, 3)), (feed_parts, (4, 5, 6))):
+        for layer, parts in enumerate(parts_of):
+            top = 0
+            for part in parts:
+                sources.append(part)
+                places.append((layer, top, weights))
+                top += part.shape[1]
     outs = [
-        jax.ShapeDtypeStruct((LAYERS, rows, width), jnp.float32)
+        jax.ShapeDtypeStruct((LAYERS, top, width), jnp.float32)
         for width in [plan.head_cuts[-1] * HEAD_DIM] * 4 + [plan.unit_cuts[-1]] * 3
     ]
     return local_call(functools.partial(join_kernel, plan, places, len(sources)), "join_layers", sources, outs, [], 0)
@@ -218,6 +281,7 @@
 
 
 SLOT = 16
+START_MIB = 58
 PARTS = 1
 SKEW = 3
 
@@ -261,16 +325,25 @@
 
 class Exchange(Job):
     semaphores = 7
-
-    @staticmethod
-    def result(source):
-        return jax.ShapeDtypeStruct(source.shape, source.dtype)
+    span = None
+
+    @classmethod
+    def rows(cls, source):
+        return cls.span or (0, source.shape[1])
+
+    @classmethod
+    def result(cls, source):
+        first, last = cls.rows(source)
+        return jax.ShapeDtypeStruct((source.shape[0], last - first, source.shape[2]), source.dtype)
 
     def __init__(self, source, result, sems):
         d, c, t = place()
-        self.own = pltpu.make_async_copy(source.at[c], result.at[c], sems.at[6])
+        first, last = self.rows(source)
+        rows = pl.ds(first, last - first)
+        self.own = pltpu.make_async_copy(source.at[c, rows], result.at[c], sems.at[6])
         self.copies = [
-            send(source.at[c ^ k], result.at[c], sems.at[k - 1], sems.at[k + 2], (d, c ^ k, t)) for k in (3, 2, 1)
+            send(source.at[c ^ k, rows], result.at[c], sems.at[k - 1], sems.at[k + 2], (d, c ^ k, t))
+            for k in (3, 2, 1)
         ]
 
     def start(self):
@@ -282,6 +355,13 @@
         for copy in self.copies:
             copy.wait()
         self.own.wait()
+
+
+def exchange_rows(first, last):
+    class Some(Exchange):
+        span = (first, last)
+
+    return Some
 
 
 class Collect(Job):
@@ -361,7 +441,7 @@
 
 
 class GainScatter(Job):
-    semaphores = 31
+    semaphores = 33
     everyone = True
     near = True
     late = True
@@ -376,12 +456,13 @@
 
     @staticmethod
     def scratch(source):
-        return [pltpu.VMEM(GainScatter.blocks(source), source.dtype)]
-
-    def __init__(self, source, result, sems, cut):
+        return [pltpu.VMEM(GainScatter.blocks(source), source.dtype)] * 3
+
+    def __init__(self, source, result, sems, own, other, cut):
         d, c, t = place()
         mine = d * 4 + c
-        self.source, self.cut = source, cut
+        self.source, self.terms, self.cut = source, (own, other), cut
+        self.across = send(own, other, sems.at[31], sems.at[32], (d, c, 1 - t))
         self.own = pltpu.make_async_copy(cut.at[mine], result.at[mine], sems.at[0])
         self.copies = []
         for k in range(1, 16):
@@ -389,12 +470,16 @@
             self.copies.append(send(cut.at[g * 4 + i], result.at[mine], sems.at[k], sems.at[k + 15], (g, i, t)))
 
     def start(self, made):
-        self.cut[...] = jnp.zeros(self.cut.shape, self.cut.dtype)
+        own, other = self.terms
+        own[...] = jnp.zeros(own.shape, own.dtype)
         part = made.shape[1] // 16
         for i in range(16):
-            self.cut[i, 0:1, :part] = made[:, i * part : (i + 1) * part]
+            own[i, 0:1, :part] = made[:, i * part : (i + 1) * part]
             rows = self.source.shape[0]
-            self.cut[i, 1 : 1 + rows, :part] = self.source[:, i * part : (i + 1) * part]
+            own[i, 1 : 1 + rows, :part] = self.source[:, i * part : (i + 1) * part]
+        self.across.start()
+        self.across.wait()
+        self.cut[...] = own[...] + other[...]
         for copy in self.copies:
             copy.start()
         self.own.start()
@@ -593,7 +678,7 @@
 
 
 def job_specs(jobs):
-    vmem, hbm = pl.BlockSpec(memory_space=pltpu.VMEM), pl.BlockSpec(memory_space=pl.ANY)
+    vmem, hbm = pl.BlockSpec(memory_space=pltpu.VMEM), pl.BlockSpec(memory_space=pltpu.HBM)
     sources = [job[1] for job in jobs]
     in_specs = [vmem if job[0].near else hbm for job in jobs]
     out_shapes = [job[0].result(job[1]) for job in jobs]
@@ -888,6 +973,9 @@
     if prelude:
         made, refs = take(refs, 1)
         prelude_scratch, refs = take(refs, prelude[3])
+        held, refs = take(refs, prelude[1])
+        (load_sems,), refs = take(refs, 1)
+        loads = start_loads(prelude_in, held, load_sems)
     built = []
     for i, (settle, gather, _, _) in enumerate(lines):
         scratch, refs = take(refs, Line.scratch_count)
@@ -905,7 +993,9 @@
         if not job.late:
             job.start()
     if prelude:
-        prelude[0](*prelude_in, made[0], *prelude_out, *prelude_scratch)
+        for copy in loads:
+            copy.wait()
+        prelude[0](*held, made[0], *prelude_out, *prelude_scratch)
         built[0].begin()
 
     turns = max(line.turns for line in built)
@@ -943,13 +1033,14 @@
 
 
 def line_call(name, number, lines, jobs, prelude=None):
-    vmem = pl.BlockSpec(memory_space=pltpu.VMEM)
-    operands, shapes, scratch, facts = [], [], [], []
+    vmem, hbm = pl.BlockSpec(memory_space=pltpu.VMEM), pl.BlockSpec(memory_space=pltpu.HBM)
+    operands, shapes, scratch, facts, far = [], [], [], [], 0
     if prelude:
         kernel, prelude_in, prelude_out, prelude_scratch, made = prelude
+        far = len(prelude_in)
         operands += prelude_in
         shapes += prelude_out
-        scratch += [pltpu.VMEM(made, jnp.bfloat16)] + prelude_scratch
+        scratch += [pltpu.VMEM(made, jnp.bfloat16)] + prelude_scratch + load_scratch(prelude_in)
     for settle, gather, partial_sum, settle_in, settle_out in lines:
         rows, width = made if partial_sum is None else partial_sum.shape
         block = rows // 4
@@ -970,7 +1061,7 @@
         ),
         name=name,
         out_shape=tuple(shapes + out_shapes),
-        in_specs=[vmem] * len(operands) + in_specs,
+        in_specs=[hbm] * far + [vmem] * (len(operands) - far) + in_specs,
         out_specs=tuple([vmem] * len(shapes) + out_specs),
         scratch_shapes=scratch + job_scratch,
         compiler_params=pltpu.CompilerParams(
@@ -978,6 +1069,63 @@
         ),
         cost_estimate=pl.CostEstimate(flops=10**9, bytes_accessed=100 * 10**6, transcendentals=0),
     )(*operands, *sources)
+
+
+def load_scratch(operands):
+    return [pltpu.VMEM(operand.shape, operand.dtype) for operand in operands] + [
+        pltpu.SemaphoreType.DMA((len(operands),))
+    ]
+
+
+def start_loads(sources, held, sems):
+    copies = [pltpu.make_async_copy(source, ref, sems.at[i]) for i, (source, ref) in enumerate(zip(sources, held))]
+    for copy in copies:
+        copy.start()
+    return copies
+
+
+def work_kernel(kernel, n_in, n_out, n_scratch, kinds, counts, *refs):
+    far, refs = take(refs, n_in)
+    sources, refs = take(refs, len(kinds))
+    outs, refs = take(refs, n_out)
+    results, refs = take(refs, len(kinds))
+    scratch, refs = take(refs, n_scratch)
+    ins, refs = take(refs, n_in)
+    (load_sems,), refs = take(refs, 1)
+    loads = start_loads(far, ins, load_sems)
+    if kinds:
+        greet(*place())
+    jobs = make_jobs(kinds, counts, sources, results, refs)
+    for job in jobs:
+        job.start()
+    for copy in loads:
+        copy.wait()
+    kernel(*ins, *outs, *scratch)
+    for job in jobs:
+        for act in job.steps():
+            act()
+    for job in jobs:
+        job.finish()
+
+
+def work_call(kernel, name, number, operands, outs, scratch, jobs):
+    vmem, hbm = pl.BlockSpec(memory_space=pltpu.VMEM), pl.BlockSpec(memory_space=pltpu.HBM)
+    sources, in_specs, out_shapes, out_specs, job_scratch, counts = job_specs(jobs)
+    results = pl.pallas_call(
+        functools.partial(
+            work_kernel, kernel, len(operands), len(outs), len(scratch), [job[0] for job in jobs], counts
+        ),
+        name=name,
+        out_shape=tuple(list(outs) + out_shapes),
+        in_specs=[hbm] * len(operands) + in_specs,
+        out_specs=tuple([vmem] * len(outs) + out_specs),
+        scratch_shapes=list(scratch) + load_scratch(operands) + job_scratch,
+        compiler_params=pltpu.CompilerParams(
+            collective_id=number if jobs else None, has_side_effects=bool(jobs), vmem_limit_bytes=48 * 2**20
+        ),
+        cost_estimate=pl.CostEstimate(flops=10**10, bytes_accessed=50 * 10**6, transcendentals=0),
+    )(*operands, *sources)
+    return take(results, len(outs))
 
 
 def settle_forward(total, rows, ins, outs):
@@ -1053,7 +1201,7 @@
         )
         return output, moved
 
-    def backward(self, partial_sum, values, grad_rows, gain, jobs):
+    def backward(self, partial_sum, values, grad_rows, gain, jobs, last=None):
         lines = [
             (
                 settle_backward,
@@ -1063,8 +1211,12 @@
                 [jax.ShapeDtypeStruct(gain.shape, jnp.float32), jax.ShapeDtypeStruct(values.shape, jnp.float32)],
             )
         ]
+        if last:
+            lines.append((settle_last, False, last[0], [last[1]], []))
         gain_grad, grad, gathered, *moved = line_call("backward_line", self.next_number(), lines, jobs)
-        return grad, gain_grad, gathered, moved
+        if last:
+            return grad, gain_grad, gathered, moved[1:], moved[0]
+        return grad, gain_grad, gathered, moved, None
 
     def backward_last(self, partial_sum, values, grad_rows, gain, jobs, gain_grads):
         gain_grad, own, *moved, gain_blocks = line_call(
@@ -1098,8 +1250,12 @@
                 source = reduce_grads(source, lax.axis_size("ctx"))
                 moved.append(lax.all_to_all(source, "ctx", 0, 0, tiled=False))
                 continue
+            some = issubclass(kind, Exchange)
+            if some:
+                first, last = kind.rows(source)
+                source = source[:, first:last]
             blocks = source if kind is Spread else lax.all_to_all(source, "ctx", 0, 0, tiled=False)
-            moved.append(blocks if kind is Exchange else lax.all_gather(blocks, "dp", axis=0, tiled=True))
+            moved.append(blocks if some else lax.all_gather(blocks, "dp", axis=0, tiled=True))
         return tuple(moved)
 
     def own_rows(self, whole):
@@ -1117,16 +1273,17 @@
     def last(self, partial_sum, residual, jobs):
         return self.deliver(residual + depth_scale * scatter_rows(partial_sum)), self.moves(*jobs)
 
-    def backward(self, partial_sum, values, grad_rows, gain, jobs):
+    def backward(self, partial_sum, values, grad_rows, gain, jobs, last=None):
         gain_grad, from_norm = norm_backward(values, gain, scatter_rows(partial_sum))
         grad = grad_rows + from_norm
         gathered = gather_rows((depth_scale * grad).astype(jnp.bfloat16))
-        return grad, gain_grad, gathered, self.moves(*jobs)
+        output = self.last(*last, [])[0] if last else None
+        return grad, gain_grad, gathered, self.moves(*jobs), output
 
     def backward_last(self, partial_sum, values, grad_rows, gain, jobs, gain_grads):
         gain_grad, from_norm = norm_backward(values, gain, scatter_rows(partial_sum))
         sums = jnp.concatenate([gain_grad, gain_grads], axis=0)
-        sums = lax.psum_scatter(sums, ("dp", "ctx"), scatter_dimension=1, tiled=True)
+        sums = lax.psum(lax.psum_scatter(sums, ("dp", "ctx"), scatter_dimension=1, tiled=True), "tensor")
         return self.deliver(grad_rows + from_norm), sums, self.moves(*jobs)
 
     def return_grads(self, full):
@@ -1179,7 +1336,21 @@
         ).astype(jnp.bfloat16)
 
 
-def attend_back_kernel(heads, grad_ref, weight_ref, mixed_ref, total_ref, cosine_ref, sine_ref, bias_ref, partial_ref, all_ref, wide, turned):
+def norm_attend_kernel(
+    heads, inputs_ref, gain_ref, weight_ref, cosine_ref, sine_ref, bias_ref, partial_ref, mixed_ref, attended_ref, total_ref, normed_ref, wide
+):
+    rows = 128
+    for first in range(0, inputs_ref.shape[0], rows):
+        values = inputs_ref[first : first + rows].astype(jnp.float32)
+        normed_ref[first : first + rows] = (rms_parts(values)[0] * gain_ref[...]).astype(jnp.bfloat16)
+    attend_kernel(
+        heads, normed_ref, weight_ref, cosine_ref, sine_ref, bias_ref, partial_ref, mixed_ref, attended_ref, total_ref, wide
+    )
+
+
+def attend_back_kernel(
+    heads, grad_ref, weight_ref, mixed_ref, total_ref, cosine_ref, sine_ref, bias_ref, normed_ref, attended_ref, partial_ref, sums_ref, wide, turned, all_ref
+):
     width = heads * HEAD_DIM
     lead = wide.shape[1] - width
     wide[...] = times(grad_ref[...], weight_ref[:, 3 * width - lead :]).astype(jnp.bfloat16)
@@ -1209,6 +1380,10 @@
         partial_ref[:, first : first + 3 * LANES] = times_transposed(
             grad_all, weight_ref[first : first + 3 * LANES, : grad_all.shape[1]]
         ).astype(jnp.bfloat16)
+    for first in range(0, sums_ref.shape[0], 2 * LANES):
+        tile = slice(first, first + 2 * LANES)
+        sums_ref[tile, : 3 * width] = outer_rows(normed_ref[:, tile], all_ref[:, : 3 * width]).astype(jnp.bfloat16)
+        sums_ref[tile, 3 * width :] = outer_rows(grad_ref[:, tile], attended_ref[...]).astype(jnp.bfloat16)
 
 
 def local_call(kernel, name, operands, outs, scratch, flops):
@@ -1290,21 +1465,23 @@
     )
 
 
-def forward_attention(normed, weight, plan, bias, tables, kernels):
+def forward_attention(normed, weight, plan, bias, tables, kernels, gain):
     width = plan.head_width
     rows = normed.shape[0]
     if kernels:
         columns = (3 * width + LANES - 1) // LANES * LANES
         wide = (width + LANES - 1) // LANES * LANES
         sized = jax.ShapeDtypeStruct
+        first = gain is not None
         return (
-            functools.partial(attend_kernel, plan.head_count),
-            [normed, weight, *lane_tables(tables), bias],
+            functools.partial(norm_attend_kernel if first else attend_kernel, plan.head_count),
+            [normed] + ([gain] if first else []) + [weight, *lane_tables(tables), bias],
             [
                 sized((rows, columns), jnp.bfloat16),
                 sized((rows, width), jnp.bfloat16),
                 sized((rows, LANES), jnp.float32),
-            ],
+            ]
+            + ([sized(normed.shape, jnp.bfloat16)] if first else []),
             [pltpu.VMEM((rows, wide), jnp.bfloat16)],
             (rows, weight.shape[0]),
         ), None
@@ -1349,6 +1526,47 @@
     return partial_sum, (normed, gating, upward, activated)
 
 
+def feed_back_kernel(
+    grad_ref, normed_ref, gate_ref, up_ref, down_ref, gating_ref, upward_ref, activated_ref, partial_ref, sums_ref, gate_grad, up_grad
+):
+    units = gating_ref.shape[1]
+    grad = grad_ref[...]
+    for first in range(0, units, 2 * LANES):
+        tile = slice(first, first + 2 * LANES)
+        grad_act = times(grad, down_ref[:, tile])
+        gating, upward = gating_ref[:, tile], upward_ref[:, tile]
+        sigmoid_gate = jax.nn.sigmoid(gating)
+        gate_grad[:, tile] = (grad_act * upward * sigmoid_gate * (1.0 + gating * (1.0 - sigmoid_gate))).astype(
+            jnp.bfloat16
+        )
+        up_grad[:, tile] = (grad_act * gating * sigmoid_gate).astype(jnp.bfloat16)
+    for first in range(0, partial_ref.shape[1], 2 * LANES):
+        tile = slice(first, first + 2 * LANES)
+        partial_ref[:, tile] = (
+            times_transposed(gate_grad[...], gate_ref[tile, :]) + times_transposed(up_grad[...], up_ref[tile, :])
+        ).astype(jnp.bfloat16)
+        normed = normed_ref[:, tile]
+        sums_ref[tile, :units] = outer_rows(normed, gate_grad[...]).astype(jnp.bfloat16)
+        sums_ref[tile, units : 2 * units] = outer_rows(normed, up_grad[...]).astype(jnp.bfloat16)
+        sums_ref[tile, 2 * units :] = outer_rows(grad_ref[:, tile], activated_ref[...]).astype(jnp.bfloat16)
+
+
+def backward_feed_beside(down_grad, weights, record, number, jobs):
+    normed, gating, upward, activated = record
+    rows, width = down_grad.shape
+    units = gating.shape[1]
+    sized = jax.ShapeDtypeStruct
+    return work_call(
+        feed_back_kernel,
+        "feed_back",
+        number,
+        [down_grad, normed, *weights, gating, upward, activated],
+        [sized((rows, width), jnp.bfloat16), sized((width, 3 * units), jnp.bfloat16)],
+        [pltpu.VMEM((rows, units), jnp.bfloat16)] * 2,
+        jobs,
+    )
+
+
 def backward_feed(down_grad, weights, record):
     gate_weight, up_weight, down_weight = weights
     normed, gating, upward, activated = record
@@ -1362,22 +1580,27 @@
     return partial_sum, ((normed, grad_gating), (normed, grad_upward), (down_grad, activated))
 
 
-def backward_attention(branch_grad, weight, record, plan, bias, tables, kernels):
+def backward_attention(branch_grad, weight, record, plan, bias, tables, kernels, jobs):
     width = plan.head_width
     rows = branch_grad.shape[0]
     if kernels:
         normed, mixed, attended, total = record
         wide = (width + LANES - 1) // LANES * LANES
         sized = jax.ShapeDtypeStruct
-        partial_sum, grad_all = local_call(
+        (partial_sum, sums), moved = work_call(
             functools.partial(attend_back_kernel, plan.head_count),
             "attend_back",
-            [branch_grad, weight, mixed, total, *lane_tables(tables), bias],
-            [sized((rows, weight.shape[0]), jnp.bfloat16), sized(mixed.shape, jnp.bfloat16)],
-            [pltpu.VMEM((rows, wide), jnp.bfloat16), pltpu.VMEM((rows, 2 * width), jnp.float32)],
-            4 * rows * weight.shape[0] * weight.shape[1],
+            kernels.next_number() if jobs else None,
+            [branch_grad, weight, mixed, total, *lane_tables(tables), bias, normed, attended],
+            [sized((rows, weight.shape[0]), jnp.bfloat16), sized((weight.shape[0], 4 * width), jnp.bfloat16)],
+            [
+                pltpu.VMEM((rows, wide), jnp.bfloat16),
+                pltpu.VMEM((rows, 2 * width), jnp.float32),
+                pltpu.VMEM(mixed.shape, jnp.bfloat16),
+            ],
+            jobs,
         )
-        return partial_sum, ((normed, grad_all[:, : 3 * width]), (branch_grad, attended))
+        return partial_sum, sums, moved
     normed, query, key, value, probs, attended = record
     grad_mixed = times(branch_grad, weight[:, 3 * width :]).astype(jnp.bfloat16)
     grad_query, grad_key, grad_value = attention_backward(
@@ -1392,7 +1615,7 @@
         axis=1,
     ).astype(jnp.bfloat16)
     partial_sum = times_transposed(grad_all, weight[:, : 3 * width]).astype(jnp.bfloat16)
-    return partial_sum, ((normed, grad_all), (branch_grad, attended))
+    return partial_sum, outer_sums((normed, grad_all), (branch_grad, attended)), None
 
 
 def body(
@@ -1433,8 +1656,6 @@
     feed_stack = [gating_weight, upward_weight, downward_weight.transpose(0, 2, 1)]
 
     def windows(layer):
-        if kernels:
-            return cut_layer(plan, layer, attention_stack, feed_stack)
         attention = [cut_windows(weight[layer], head_cuts, plan.head_width) for weight in attention_stack]
         feed = [cut_windows(weight[layer], plan.unit_cuts, plan.unit_width) for weight in feed_stack]
         return [jnp.concatenate(attention, axis=2)] + feed
@@ -1442,21 +1663,22 @@
     def joined(blocks):
         return blocks.reshape(-1, blocks.shape[-1])
 
-    own_gains = jnp.pad(
-        jnp.concatenate([prenorm_gain, postnorm_gain], axis=0).T, ((0, 0), (0, LANES - 2 * LAYERS))
-    )
-    own_gains = jnp.broadcast_to(own_gains[None], (n_ctx,) + own_gains.shape)
-    attention_windows, gate, up, down = windows(0)
-    attention_blocks, gain_blocks, inputs_whole, gate, up, down = comm.moves(
-        (Fetch, attention_windows),
-        (Fetch, own_gains),
-        (Collect, inputs),
-        (Fetch, gate),
-        (Exchange, up),
-        (Exchange, down),
-        urgent=3,
-    )
-    gains = gain_blocks.reshape(-1, LANES)[:, : 2 * LAYERS].T.astype(jnp.float32)
+    if kernels:
+        later_windows, moved = start_call(
+            plan, comm.next_number(), attention_stack + feed_stack, prenorm_gain, postnorm_gain, inputs
+        )
+        inputs_whole, attention_blocks, gain_blocks, gate, up, down = moved
+        gains = gain_blocks[:, : 2 * LAYERS, : prenorm_gain.shape[1]].transpose(1, 0, 2).reshape(2 * LAYERS, -1)
+    else:
+        attention_windows, gate, up, down = windows(0)
+        later_windows = [windows(layer) for layer in range(1, LAYERS)]
+        attention_blocks, inputs_whole, gate, up, down = comm.moves(
+            (Fetch, attention_windows), (Collect, inputs), (Fetch, gate), (Exchange, up), (Exchange, down)
+        )
+        gains = lax.all_gather(
+            jnp.concatenate([prenorm_gain, postnorm_gain], axis=0), ("dp", "ctx"), axis=1, tiled=True
+        )
+    gains = gains.astype(jnp.float32)
     front = [gains[layer : layer + 1] for layer in range(LAYERS)]
     behind = [gains[LAYERS + layer : LAYERS + layer + 1] for layer in range(LAYERS)]
     attention_weights, feed_weights = [None] * LAYERS, [None] * LAYERS
@@ -1465,17 +1687,19 @@
 
     attention_weights[0] = joined(attention_blocks)
     residual = comm.own_rows(inputs_whole).astype(jnp.float32)
-    normed = (rms_parts(inputs_whole.astype(jnp.float32))[0] * front[0]).astype(jnp.bfloat16)
+    normed = inputs_whole
+    if not kernels:
+        normed = (rms_parts(inputs_whole.astype(jnp.float32))[0] * front[0]).astype(jnp.bfloat16)
     for layer in range(LAYERS):
         starts_of[layer] = residual
         more = layer + 1 < LAYERS
         partial_sum, attention_records[layer] = forward_attention(
-            normed, attention_weights[layer], plan, bias, tables, kernels
+            normed, attention_weights[layer], plan, bias, tables, kernels, None if layer else front[0]
         )
         prelude = partial_sum if kernels else None
         jobs = [(Spread, up, 6, 2), (Spread, down, 14, 2)]
         if more:
-            next_windows = windows(layer + 1)
+            next_windows = later_windows[layer]
             jobs += [(Exchange, next_windows[0]), (Exchange, next_windows[1])]
         else:
             jobs += [(Collect, cotangent, 5, 4)]
@@ -1483,7 +1707,7 @@
             None if kernels else partial_sum, residual, behind[layer], jobs, prelude
         )
         if kernels:
-            attention_records[layer] = (normed, *made)
+            attention_records[layer] = (made[3] if layer == 0 else normed, *made[:3])
         normed = normed_two
         feed_weights[layer] = [joined(blocks) for blocks in (gate, up, down)]
         middles[layer] = hidden
@@ -1514,48 +1738,87 @@
     gain_fronts, gain_backs, attention_parts, feed_parts = [[None] * LAYERS for _ in range(4)]
     for layer in reversed(range(LAYERS)):
         more, last_layer = layer > 0, layer + 1 == LAYERS
-        partial_sum, pairs = backward_feed(down_grad, feed_weights[layer], feed_records[layer])
-        sums = outer_sums(*pairs)
+        own_width = query_weight.shape[1]
+        cut_feed, cut_attention = own_width * 5 // 9 // 16 * 16, own_width // 2 // 16 * 16
+        cut_last = own_width // 3 // 16 * 16
+
+        def two(whole, cut):
+            if last_layer:
+                return [], []
+            return [(exchange_rows(0, cut), whole)], [(exchange_rows(cut, own_width), whole)]
+
+        beside, in_line = two(feed_parts[layer + 1] if not last_layer else None, cut_feed)
+        if kernels and beside:
+            (partial_sum, sums), upper = backward_feed_beside(
+                down_grad, feed_weights[layer], feed_records[layer], comm.next_number(), beside
+            )
+        else:
+            partial_sum, pairs = backward_feed(down_grad, feed_weights[layer], feed_records[layer])
+            sums = outer_sums(*pairs)
+            upper = comm.moves(*beside) if beside else ()
         partial_sum, sums = lax.optimization_barrier((partial_sum, sums))
-        feed_parts[layer] = reduce_grads(sums, n_ctx)
-        jobs = [] if last_layer else [(Exchange, feed_parts[layer + 1])]
-        grad_rows, gain_backs[layer], branch_grad, moved = comm.backward(
-            partial_sum, middles[layer], grad_rows, behind[layer], jobs
+        feed_sums = reduce_grads(sums, n_ctx)
+        grad_rows, gain_backs[layer], branch_grad, lower, last_output = comm.backward(
+            partial_sum,
+            middles[layer],
+            grad_rows,
+            behind[layer],
+            in_line,
+            None if more else (last_sum, middles[LAYERS - 1]),
         )
-        if not last_layer:
-            feed_parts[layer + 1] = moved[0]
-        partial_sum, pairs = backward_attention(
-            branch_grad, attention_weights[layer], attention_records[layer], plan, bias, tables, kernels
+        if beside:
+            feed_parts[layer + 1] = [upper[0], lower[0]]
+        if not more:
+            output = last_output
+        beside, in_line = two(attention_parts[layer + 1] if not last_layer else None, cut_attention)
+        partial_sum, sums, upper = backward_attention(
+            branch_grad,
+            attention_weights[layer],
+            attention_records[layer],
+            plan,
+            bias,
+            tables,
+            comm if kernels else None,
+            beside,
         )
-        sums = outer_sums(*pairs)
+        if beside and upper is None:
+            upper = comm.moves(*beside)
         partial_sum, sums = lax.optimization_barrier((partial_sum, sums))
-        attention_parts[layer] = reduce_grads(sums, n_ctx)
+        attention_sums = reduce_grads(sums, n_ctx)
         if more:
-            grad_rows, gain_fronts[layer], down_grad, _ = comm.backward(
-                partial_sum, starts_of[layer], grad_rows, front[layer], []
+            grad_rows, gain_fronts[layer], down_grad, lower, _ = comm.backward(
+                partial_sum, starts_of[layer], grad_rows, front[layer], in_line
             )
         else:
             others = jnp.concatenate(gain_fronts[1:] + gain_backs, axis=0)
-            jobs = [(Exchange, attention_parts[layer + 1])]
-            grad_inputs, gain_sums, moved = comm.backward_last(
-                partial_sum, starts_of[layer], grad_rows, front[layer], jobs, others
+            grad_inputs, gain_sums, (feed_moved, *lower) = comm.backward_last(
+                partial_sum,
+                starts_of[layer],
+                grad_rows,
+                front[layer],
+                [(exchange_rows(0, cut_last), feed_sums)] + in_line,
+                others,
             )
-            attention_parts[layer + 1] = moved[0]
-    last_sum, grad_inputs = lax.optimization_barrier((last_sum, grad_inputs))
-    output, moved = comm.last(last_sum, middles[LAYERS - 1], [(Exchange, feed_parts[0])])
-    feed_parts[0] = moved[0]
-    attention_parts[0], output = lax.optimization_barrier((attention_parts[0], output))
-    (attention_parts[0],) = comm.moves((Exchange, attention_parts[0]))
+        if beside:
+            attention_parts[layer + 1] = [upper[0], lower[0]]
+        feed_parts[layer], attention_parts[layer] = feed_sums, attention_sums
+    attention_parts[0], grad_inputs = lax.optimization_barrier((attention_parts[0], grad_inputs))
+    feed_rest, attention_moved = comm.moves(
+        (exchange_rows(cut_last, own_width), feed_parts[0]), (Exchange, attention_parts[0])
+    )
+    feed_parts[0], attention_parts[0] = [feed_moved, feed_rest], [attention_moved]
     grad_inputs = grad_inputs.astype(jnp.float32)
-    gain_sums = lax.psum(gain_sums, "tensor")
 
     if kernels:
-        joins = join_layers(plan, list(zip(attention_parts, feed_parts)))
+        joins = join_layers(plan, attention_parts, feed_parts)
     else:
 
         def spread(parts, index, width, cuts):
             return jnp.stack(
-                [join_windows(part[:, :, index * width : (index + 1) * width], cuts) for part in parts]
+                [
+                    join_windows(jnp.concatenate(part, axis=1)[:, :, index * width : (index + 1) * width], cuts)
+                    for part in parts
+                ]
             ).astype(jnp.float32)
 
         joins = [spread(attention_parts, i, plan.head_width, head_cuts) for i in range(4)]

time: 928 us -> 871 us (0.939)
  Pallas kernels: 785 us -> 763 us
  matrix products: 32.5 us -> 16.6 us
  local copies, waits for them, and re-layouts: 71.1 us -> 56.6 us
    pallas_call x2 -> x4, Pallas kernels: 2.03 us -> 212 us  [the longest x1 121 us: start_call(): pl.pallas_call(functools.partial(start_kernel, plan), name='start', out_s...]
    pallas_call x8 -> x7, Pallas kernels: 554 us -> 453 us  [line_call(): pl.pallas_call(functools.partial(line_kernel, (kernel, len(prelude_in), l...]
    pallas_call x2 -> x1, Pallas kernels: 157 us -> 79.6 us  [jobs_call(): pl.pallas_call(functools.partial(jobs_kernel, [job[0] for job in jobs], c...]
    pallas_call x3 -> x1, Pallas kernels: 38.8 us -> 9.02 us  [local_call(): pl.pallas_call(kernel, name=name, out_shape=tuple(outs), in_specs=[vmem]...]
    pallas_call x4 -> x1, Pallas kernels: 32.1 us -> 9.71 us  [outer_sums(): pl.pallas_call(outer_kernel, name='outer_sums', grid=(width // tile,), ou...]
    unnamed x217 -> x163, local copies, waits for them, and re-layouts: 69.8 us -> 54.2 us
    dot_general x5 -> x3, matrix products: 21.3 us -> 10.1 us  [times_transposed(): lax.dot_general(left, right, (((1,), (1,)), ((), ())), preferred_element_...]
  transfers between devices with their start and end apart: 4 -> 4, of which waited for: 0 -> 0; matrix products, arithmetic and copies ran while one was open for 3% -> 1% of each run, Pallas kernels for 40% -> 37%
where the time goes in v3:
time: 871 us; the launch traced here: 865 us
  Pallas kernels  763 us (88%)
  local copies, waits for them, and re-layouts  56.6 us (6%)
  matrix products  16.6 us (2%)
  between operations  14.9 us (2%)
  other arithmetic  12.9 us (1%)
    pallas_call x7, Pallas kernels, line_call(): pl.pallas_call(functools.partial(line_kernel, (kernel, len(prelude_in), l...  453 us
    pallas_call x1, Pallas kernels, start_call(): pl.pallas_call(functools.partial(start_kernel, plan), name='start', out_s...  121 us
    pallas_call x3, Pallas kernels, work_call(): pl.pallas_call(functools.partial(work_kernel, kernel, len(operands), len(...  90.9 us
    pallas_call x1, Pallas kernels, jobs_call(): pl.pallas_call(functools.partial(jobs_kernel, [job[0] for job in jobs], c...  79.6 us
    unnamed x163, local copies, waits for them, and re-layouts  54.2 us
  transfers between devices with their start and end apart: 4, of which 0 were waited for; matrix products, arithmetic and copies ran while one was open for 1% of the time, Pallas kernels for 37%

profile of v3, /device:TPU:0, one launch (start us, length us, event | category | flops | bytes accessed | tf_op | source)
XLA Modules:
  0.0 864.7 jit_solution(9302530628380491808)
XLA Ops:
  8.5 1.9 fusion.11
  11.2 121.2 %start.1 = (bf16[4,144,1280]{2,1,0:T(8,128)(2,1)}, bf16[4,144,768]{2,1,0:T(8,128)(2,1)}, bf16[4,144,768]{2,1,0:T(8,128)(2,1)}, bf16[4,144,768]{2,1,0:T(8,128)(2,...) custom-call(bf16[2,144,1152]{2,1,0:T(8,128)(2,1)} %refs_0_.1, ...), custom_call_target="tpu_custom_call" | custom-call | flops 1000000000 | bytes 100000000 | tf_op jit(solution)/shard_map/start/pallas_call | solution.py:220
  137.0 83.5 %forward_line.3 = (bf16[512,1024]{1,0:T(8,128)(2,1)S(1)}, bf16[512,320]{1,0:T(8,128)(2,1)S(1)}, f32[512,128]{1,0:T(8,128)S(1)}, bf16[512,2304]{1,0:T(8,128)(2,1)...) custom-call(bf16[512,2304]{1,0:T(8,128)(2,1)} %get-tuple-element.88., ...), custom_call_target="tpu_custom_call" | custom-call | flops 1000000000 | bytes 100000000 | tf_op jit(solution)/shard_map/forward_line/pallas_call | solution.py:1053
  220.5 1.4 copy-done.55
  224.4 82.2 %forward_line.4 = (f32[512,768]{1,0:T(8,128)S(1)}, f32[512,768]{1,0:T(8,128)S(1)}, bf16[512,768]{1,0:T(8,128)(2,1)S(1)}, f32[128,2304]{1,0:T(8,128)S(1)}, bf16[5...) custom-call(bf16[512,2304]{1,0:T(8,128)(2,1)} %get-tuple-element.95., ...), custom_call_target="tpu_custom_call" | custom-call | flops 1000000000 | bytes 100000000 | tf_op jit(solution)/shard_map/forward_line/pallas_call | solution.py:1053
  309.2 62.2 %forward_line.5 = (bf16[512,1024]{1,0:T(8,128)(2,1)S(1)}, bf16[512,320]{1,0:T(8,128)(2,1)S(1)}, f32[512,128]{1,0:T(8,128)S(1)}, f32[128,2304]{1,0:T(8,128)S(1)},...) custom-call(bf16[512,2304]{1,0:T(8,128)(2,1)} %copy-done.20, ...), custom_call_target="tpu_custom_call" | custom-call | flops 1000000000 | bytes 100000000 | tf_op jit(solution)/shard_map/forward_line/pallas_call | solution.py:1053
  376.5 2.0 fusion.12
  378.6 2.0 fusion.15
  380.6 2.5 multiply_convert_fusion.1
  383.1 2.0 fusion.16
  385.1 3.5 fusion.refs_0_
  388.7 9.7 %outer_sums.1 = bf16[2304,2304]{1,0:T(8,128)(2,1)} custom-call(bf16[512,2304]{1,0:T(8,128)(2,1)S(1)} %get-tuple-element.111.refs_0_.refs_2_, bf16[512,768]{1,0:T(8,128)(2,1)S(1)} %get-tuple-element.172.refs_1_, bf16[512,2304]{1,0:T(8,128)(2,1)S(1)} %get-tuple-element.111.refs_0_.refs_2_, bf16[512,768]{1,0:T(8,128)(2,1)S(1)} %get-tuple-element.173.refs_3_, ...), custom_call_target="tpu_custom_call" | custom-call | flops 5435817984 | bytes 12976128 | tf_op jit(solution)/shard_map/outer_sums/pallas_call | solution.py:1422
  399.9 1.7 copy-done.17
  401.6 42.1 %backward_line.3 = (f32[1,2304]{1,0:T(1,128)S(1)}, f32[128,2304]{1,0:T(8,128)S(1)}, bf16[512,2304]{1,0:T(8,128)(2,1)S(1)}) custom-call(bf16[512,2304]{1,0:T(8,128)(2,1)S(1)} %copy-done.17, f32[128,2304]{1,0:T(8,128)S(1)} %copy-done.4, f32[128,2304]{1,0:T(8,128)S(1)} %dynamic-slice_convert_fusion.refs_2_, f32[1,2304]{1,0:T(1,128)S(1)} %slice.44.refs_6_.refs_3_), custom_call_target="tpu_custom_call" | custom-call | flops 1000000000 | bytes 100000000 | tf_op jit(solution)/shard_map/backward_line/pallas_call | solution.py:1053
  446.7 20.9 %attend_back.2 = (bf16[512,2304]{1,0:T(8,128)(2,1)S(1)}, bf16[2304,1280]{1,0:T(8,128)(2,1)}) custom-call(bf16[512,2304]{1,0:T(8,128)(2,1)} %copy-done.58, bf16[2304,1280]{1,0:T(8,128)(2,1)} %bitcast.40, bf16[512,1024]{1,0:T(8,128)(2,1)S(1)} %copy-done.66, f32[512,128]{1,0:T(8,128)S(1)} %copy-done.76, f32[512,128]{1,0:T(8,128)S(1)} %copy-done.10, ...), custom_call_target="tpu_custom_call" | custom-call | flops 10000000000 | bytes 50000000 | tf_op jit(solution)/shard_map/attend_back/pallas_call | solution.py:1114
  470.9 1.8 copy-done.19
  474.0 40.0 %backward_line.4 = (f32[1,2304]{1,0:T(1,128)S(1)}, f32[128,2304]{1,0:T(8,128)S(1)}, bf16[512,2304]{1,0:T(8,128)(2,1)S(1)}) custom-call(bf16[512,2304]{1,0:T(8,128)(2,1)S(1)} %copy-done.19, f32[128,2304]{1,0:T(8,128)S(1)} %copy-done.7, f32[128,2304]{1,0:T(8,128)S(1)} %copy-done.34, f32[1,2304]{1,0:T(1,128)S(1)} %slice.42.refs_5_.refs_3_), custom_call_target="tpu_custom_call" | custom-call | flops 1000000000 | bytes 100000000 | tf_op jit(solution)/shard_map/backward_line/pallas_call | solution.py:1053
  515.6 1.4 copy-done.57
  517.0 1.4 copy-done.60
  518.4 1.4 copy-done.62
  521.1 40.8 %feed_back.1 = (bf16[512,2304]{1,0:T(8,128)(2,1)}, bf16[2304,2304]{1,0:T(8,128)(2,1)}, bf16[4,80,2304]{2,1,0:T(8,128)(2,1)S(1)}) custom-call(bf16[512,2304]{1,0:T(8,128)(2,1)} %copy-done.57, bf16[512,2304]{1,0:T(8,128)(2,1)} %get-tuple-element.95.refs_0_.refs_1_, bf16[2304,768]{1,0:T(8,128)(2,1)} %bitcast.42, bf16[2304,768]{1,0:T(8,128)(2,1)} %bitcast.44, ...), custom_call_target="tpu_custom_call" | custom-call | flops 10000000000 | bytes 50000000 | tf_op jit(solution)/shard_map/feed_back/pallas_call | solution.py:1114
  563.2 4.5 convolution_convert_fusion.refs_4_
  567.7 77.1 %backward_line.5 = (f32[1,2304]{1,0:T(1,128)S(1)}, f32[128,2304]{1,0:T(8,128)S(1)}, bf16[512,2304]{1,0:T(8,128)(2,1)S(1)}, bf16[128,2304]{1,0:T(8,128)(2,1)S(1)}, bf16[4,64,2304]{2,1,0:T(8,128)(2,1)S(1)}) custom-call(bf16[512,2304]{1,0:T(8,128)(2,1)S(1)} %copy-done.16, f32[128,2304]{1,0:T(8,128)S(1)} %get-tuple-element.99.refs_4_.refs_1_, ...), custom_call_target="tpu_custom_call" | custom-call | flops 1000000000 | bytes 100000000 | tf_op jit(solution)/shard_map/backward_line/pallas_call | solution.py:1053
  647.7 1.6 copy-done.56
  655.7 29.2 %attend_back.3 = (bf16[512,2304]{1,0:T(8,128)(2,1)}, bf16[2304,1280]{1,0:T(8,128)(2,1)}, bf16[4,64,1280]{2,1,0:T(8,128)(2,1)S(1)}) custom-call(bf16[512,2304]{1,0:T(8,128)(2,1)} %copy-done.56, bf16[2304,1280]{1,0:T(8,128)(2,1)} %bitcast.38, bf16[512,1024]{1,0:T(8,128)(2,1)S(1)} %copy-done.64, f32[512,128]{1,0:T(8,128)S(1)} %copy-done.74, ...), custom_call_target="tpu_custom_call" | custom-call | flops 10000000000 | bytes 50000000 | tf_op jit(solution)/shard_map/attend_back/pallas_call | solution.py:1114
  685.8 1.5 pad_maximum_fusion.2.refs_6_
  687.5 1.7 copy-done.2
  690.6 1.6 copy-done.28
  693.2 65.7 %backward_last_line.1 = (f32[1,2304]{1,0:T(1,128)}, bf16[128,2304]{1,0:T(8,128)(2,1)S(1)}, bf16[4,48,2304]{2,1,0:T(8,128)(2,1)S(1)}, bf16[4,80,1280]{2,1,0:T(8,128)(2,1)S(1)}, f32[16,8,256]{2,1,0:T(8,128)S(1)}) custom-call(bf16[512,2304]{1,0:T(8,128)(2,1)S(1)} %copy-done.15, f32[128,2304]{1,0:T(8,128)S(1)} %dynamic-slice_convert_fusion.1.refs_6_.refs_1_, ...), custom_call_target="tpu_custom_call" | custom-call | flops 1000000000 | bytes 100000000 | tf_op jit(solution)/shard_map/backward_last_line/pallas_call | solution.py:1053
  763.7 2.2 convert_element_type.112
  767.3 79.6 %moves.1 = (bf16[4,96,2304]{2,1,0:T(8,128)(2,1)S(1)}, bf16[4,144,1280]{2,1,0:T(8,128)(2,1)S(1)}) custom-call(bf16[4,144,2304]{2,1,0:T(8,128)(2,1)} %bitcast.32, bf16[4,144,1280]{2,1,0:T(8,128)(2,1)S(1)} %bitcast.36), custom_call_target="tpu_custom_call" | custom-call | flops 1000000000 | bytes 100000000 | tf_op jit(solution)/shard_map/moves/pallas_call | solution.py:719
  848.1 9.0 %join_layers.1 = (f32[2,144,1152]{2,1,0:T(8,128)}, f32[2,144,1152]{2,1,0:T(8,128)}, f32[2,144,1152]{2,1,0:T(8,128)}, f32[2,144,1152]{2,1,0:T(8,128)}, f32[2,144,...) custom-call(bf16[4,144,1280]{2,1,0:T(8,128)(2,1)S(1)} %get-tuple-element.151.refs_0_, ...), custom_call_target="tpu_custom_call" | custom-call | bytes 20000000 | tf_op jit(solution)/shard_map/join_layers/pallas_call | solution.py:1391
  (187 shorter events, 50.4 us)
Async XLA Ops:
  7.2 509.8 %reduce-scatter.5.cloned.1.call-start = ((), (), s32[]{:S(2)}) async-start(), calls=%async_computation.4 | async-start | bytes 13271040 | tf_op jit(solution)/shard_map/reduce_scatter | solution.py:269
  133.8 3.1 copy-start.25
  133.8 3.1 copy-start.37
  133.8 3.1 copy-start.38
  136.9 172.2 %copy-start.9 = (f32[512,128]{1,0:T(8,128)}, f32[512,128]{1,0:T(8,128)S(1)}, u32[]{:S(2)}) copy-start(f32[512,128]{1,0:T(8,128)S(1)} %get-tuple-element.181.refs_3_.refs_2_.refs_4_) | copy-start | bytes 786436
  137.0 172.2 %copy-start.12 = (f32[512,128]{1,0:T(8,128)}, f32[512,128]{1,0:T(8,128)S(1)}, u32[]{:S(2)}) copy-start(f32[512,128]{1,0:T(8,128)S(1)} %get-tuple-element.182.refs_4_.refs_3_.refs_5_) | copy-start | bytes 786436
  137.0 87.4 %copy-start.35 = (bf16[4,144,768]{2,1,0:T(8,128)(2,1)S(1)}, bf16[4,144,768]{2,1,0:T(8,128)(2,1)}, u32[]{:S(2)}) copy-start(bf16[4,144,768]{2,1,0:T(8,128)(2,1)} %get-tuple-element.102.refs_8_) | copy-start | bytes 2654212
  137.0 87.4 %copy-start.36 = (bf16[4,144,768]{2,1,0:T(8,128)(2,1)S(1)}, bf16[4,144,768]{2,1,0:T(8,128)(2,1)}, u32[]{:S(2)}) copy-start(bf16[4,144,768]{2,1,0:T(8,128)(2,1)} %get-tuple-element.103.refs_9_) | copy-start | bytes 2654212
  224.4 84.8 %copy-start.46 = (bf16[128,2304]{1,0:T(8,128)(2,1)S(1)}, bf16[128,2304]{1,0:T(8,128)(2,1)}, u32[]{:S(2)}) copy-start(bf16[128,2304]{1,0:T(8,128)(2,1)} %refs_9_.3) | copy-start | bytes 1769476
  309.2 62.2 %copy-start.6 = (f32[128,2304]{1,0:T(8,128)}, f32[128,2304]{1,0:T(8,128)S(1)}, u32[]{:S(2)}) copy-start(f32[128,2304]{1,0:T(8,128)S(1)} %get-tuple-element.106.refs_5_.refs_1_) | copy-start | bytes 3538948
  309.2 62.2 %copy-start.61 = (f32[512,768]{1,0:T(8,128)}, f32[512,768]{1,0:T(8,128)S(1)}, u32[]{:S(2)}) copy-start(f32[512,768]{1,0:T(8,128)S(1)} %get-tuple-element.124.refs_6_) | copy-start | bytes 4718596
  309.2 62.3 %copy-start.67 = (bf16[512,768]{1,0:T(8,128)(2,1)}, bf16[512,768]{1,0:T(8,128)(2,1)S(1)}, u32[]{:S(2)}) copy-start(bf16[512,768]{1,0:T(8,128)(2,1)S(1)} %get-tuple-element.125.refs_7_) | copy-start | bytes 2359300
  372.9 3.7 copy-start.78
  383.1 5.6 copy-start.77
  398.4 250.8 %reduce-scatter.7.cloned.1.call-start = ((), (), s32[]{:S(2)}) async-start(), calls=%async_computation.5 | async-start | bytes 7372800 | tf_op jit(solution)/shard_map/reduce_scatter | solution.py:269
  401.6 45.2 %copy-start.10 = (f32[512,128]{1,0:T(8,128)S(1)}, f32[512,128]{1,0:T(8,128)}, u32[]{:S(2)}) copy-start(f32[512,128]{1,0:T(8,128)} %copy-done.9) | copy-start | bytes 786436
  401.6 45.2 %copy-start.13 = (f32[512,128]{1,0:T(8,128)S(1)}, f32[512,128]{1,0:T(8,128)}, u32[]{:S(2)}) copy-start(f32[512,128]{1,0:T(8,128)} %copy-done.12) | copy-start | bytes 786436
  401.6 45.2 %copy-start.66 = (bf16[512,1024]{1,0:T(8,128)(2,1)S(1)}, bf16[512,1024]{1,0:T(8,128)(2,1)}, u32[]{:S(2)}) copy-start(bf16[512,1024]{1,0:T(8,128)(2,1)} %copy-done.65) | copy-start | bytes 3145732
  401.6 45.2 %copy-start.72 = (bf16[512,320]{1,0:T(8,128)(2,1)S(1)}, bf16[512,320]{1,0:T(8,128)(2,1)}, u32[]{:S(2)}) copy-start(bf16[512,320]{1,0:T(8,128)(2,1)} %copy-done.71) | copy-start | bytes 983044
  401.6 45.2 %copy-start.76 = (f32[512,128]{1,0:T(8,128)S(1)}, f32[512,128]{1,0:T(8,128)}, u32[]{:S(2)}) copy-start(f32[512,128]{1,0:T(8,128)} %copy-done.75) | copy-start | bytes 786436
  469.1 218.3 %reduce-scatter.11.cloned.1.call-start = ((), (), s32[]{:S(2)}) async-start(), calls=%async_computation.7 | async-start | bytes 13271040 | tf_op jit(solution)/shard_map/reduce_scatter | solution.py:269
  563.1 199.1 %reduce-scatter.9.cloned.1.call-start = ((), (), s32[]{:S(2)}) async-start(), calls=%async_computation.6 | async-start | bytes 7372800 | tf_op jit(solution)/shard_map/reduce_scatter | solution.py:269
  563.1 4.5 copy-start.5
  563.1 4.5 copy-start.16
  563.2 4.5 copy-start.30
  649.2 35.7 %copy-start.54 = (f32[1,2304]{1,0:T(1,128)}, f32[1,2304]{1,0:T(1,128)S(1)}, u32[]{:S(2)}) copy-start(f32[1,2304]{1,0:T(1,128)S(1)} %get-tuple-element.145) | copy-start | bytes 27652
  767.2 80.8 %copy-start.32 = (bf16[4,64,2304]{2,1,0:T(8,128)(2,1)S(1)}, bf16[4,64,2304]{2,1,0:T(8,128)(2,1)}, u32[]{:S(2)}) copy-start(bf16[4,64,2304]{2,1,0:T(8,128)(2,1)} %copy-done.31) | copy-start | bytes 3538948
  767.3 80.8 %copy-start.41 = (bf16[4,48,2304]{2,1,0:T(8,128)(2,1)S(1)}, bf16[4,48,2304]{2,1,0:T(8,128)(2,1)}, u32[]{:S(2)}) copy-start(bf16[4,48,2304]{2,1,0:T(8,128)(2,1)} %copy-done.40) | copy-start | bytes 2654212
  767.3 80.8 %copy-start.43 = (bf16[4,80,1280]{2,1,0:T(8,128)(2,1)S(1)}, bf16[4,80,1280]{2,1,0:T(8,128)(2,1)}, u32[]{:S(2)}) copy-start(bf16[4,80,1280]{2,1,0:T(8,128)(2,1)} %copy-done.42) | copy-start | bytes 2457604
  767.3 80.8 %copy-start.45 = (bf16[4,64,1280]{2,1,0:T(8,128)(2,1)S(1)}, bf16[4,64,1280]{2,1,0:T(8,128)(2,1)}, u32[]{:S(2)}) copy-start(bf16[4,64,1280]{2,1,0:T(8,128)(2,1)} %copy-done.44) | copy-start | bytes 1966084
  848.1 9.0 %copy-start.49 = (bf16[128,2304]{1,0:T(8,128)(2,1)S(1)}, bf16[128,2304]{1,0:T(8,128)(2,1)}, u32[]{:S(2)}) copy-start(bf16[128,2304]{1,0:T(8,128)(2,1)} %copy-done.48) | copy-start | bytes 1769476
  848.1 9.8 %copy-start.1 = (s32[4,8]{1,0:T(4,128)S(1)}, s32[4,8]{1,0:T(4,128)}, u32[]{:S(2)}) copy-start(s32[4,8]{1,0:T(4,128)} %param.18) | copy-start | bytes 388
  (53 other events, 66.1 us)
Sparse Core Ops, SparseCore 0:
  398.5 104.4 reduce-scatter.4
  506.1 66.8 reduce-scatter.6
  576.1 104.5 reduce-scatter.10
  685.9 65.6 reduce-scatter.8

commit v4 on v3

--- a/solution.py
+++ b/solution.py
@@ -281,7 +281,7 @@
 
 
 SLOT = 16
-START_MIB = 58
+START_MIB = 60
 PARTS = 1
 SKEW = 3
 
@@ -313,7 +313,6 @@
 class Job:
     everyone = False
     near = False
-    late = False
 
     @staticmethod
     def scratch(source):
@@ -444,7 +443,6 @@
     semaphores = 33
     everyone = True
     near = True
-    late = True
 
     @staticmethod
     def blocks(source):
@@ -469,14 +467,12 @@
             g, i = d ^ (k // 4), c ^ (k % 4)
             self.copies.append(send(cut.at[g * 4 + i], result.at[mine], sems.at[k], sems.at[k + 15], (g, i, t)))
 
-    def start(self, made):
+    def start(self):
         own, other = self.terms
         own[...] = jnp.zeros(own.shape, own.dtype)
-        part = made.shape[1] // 16
+        part = self.source.shape[1] // 16
         for i in range(16):
-            own[i, 0:1, :part] = made[:, i * part : (i + 1) * part]
-            rows = self.source.shape[0]
-            own[i, 1 : 1 + rows, :part] = self.source[:, i * part : (i + 1) * part]
+            own[i, : self.source.shape[0], :part] = self.source[:, i * part : (i + 1) * part]
         self.across.start()
         self.across.wait()
         self.cut[...] = own[...] + other[...]
@@ -724,7 +720,7 @@
         out_specs=tuple(out_specs),
         scratch_shapes=scratch,
         compiler_params=pltpu.CompilerParams(
-            collective_id=number, has_side_effects=True, vmem_limit_bytes=48 * 2**20
+            collective_id=number, has_side_effects=True, vmem_limit_bytes=60 * 2**20
         ),
         cost_estimate=pl.CostEstimate(flops=10**9, bytes_accessed=100 * 10**6, transcendentals=0),
     )(*sources)
@@ -990,8 +986,7 @@
     for line in built[1:]:
         line.begin()
     for job in jobs:
-        if not job.late:
-            job.start()
+        job.start()
     if prelude:
         for copy in loads:
             copy.wait()
@@ -1021,9 +1016,6 @@
         return carry
 
     lax.fori_loop(0, turns, step, 0)
-    for job in jobs:
-        if job.late:
-            job.start(built[0].settle_out[0])
     for act in rest:
         act()
     for line in built:
@@ -1065,7 +1057,7 @@
         out_specs=tuple([vmem] * len(shapes) + out_specs),
         scratch_shapes=scratch + job_scratch,
         compiler_params=pltpu.CompilerParams(
-            collective_id=number, has_side_effects=True, vmem_limit_bytes=(58 if any(job[0] is Return for job in jobs) else 40) * 2**20
+            collective_id=number, has_side_effects=True, vmem_limit_bytes=(40 if jobs else 60) * 2**20
         ),
         cost_estimate=pl.CostEstimate(flops=10**9, bytes_accessed=100 * 10**6, transcendentals=0),
     )(*operands, *sources)
@@ -1121,7 +1113,7 @@
         out_specs=tuple([vmem] * len(outs) + out_specs),
         scratch_shapes=list(scratch) + load_scratch(operands) + job_scratch,
         compiler_params=pltpu.CompilerParams(
-            collective_id=number if jobs else None, has_side_effects=bool(jobs), vmem_limit_bytes=48 * 2**20
+            collective_id=number if jobs else None, has_side_effects=bool(jobs), vmem_limit_bytes=60 * 2**20
         ),
         cost_estimate=pl.CostEstimate(flops=10**10, bytes_accessed=50 * 10**6, transcendentals=0),
     )(*operands, *sources)
@@ -1218,8 +1210,8 @@
             return grad, gain_grad, gathered, moved[1:], moved[0]
         return grad, gain_grad, gathered, moved, None
 
-    def backward_last(self, partial_sum, values, grad_rows, gain, jobs, gain_grads):
-        gain_grad, own, *moved, gain_blocks = line_call(
+    def backward_last(self, partial_sum, values, grad_rows, gain, jobs):
+        gain_grad, own, *moved = line_call(
             "backward_last_line",
             self.next_number(),
             [
@@ -1231,9 +1223,13 @@
                     [jax.ShapeDtypeStruct(gain.shape, jnp.float32)],
                 )
             ],
-            jobs + [(GainScatter, gain_grads)],
+            jobs,
         )
-        return own, jnp.sum(gain_blocks, axis=0)[: 1 + gain_grads.shape[0], : gain.shape[1] // 16], moved
+        return own, gain_grad, moved
+
+    def sum_gains(self, gain_grads, jobs):
+        gain_blocks, *moved = self.moves((GainScatter, gain_grads), *jobs)
+        return jnp.sum(gain_blocks, axis=0)[: gain_grads.shape[0], : gain_grads.shape[1] // 16], moved
 
     def return_grads(self, full):
         return full.reshape(16, -1, full.shape[1])
@@ -1280,11 +1276,13 @@
         output = self.last(*last, [])[0] if last else None
         return grad, gain_grad, gathered, self.moves(*jobs), output
 
-    def backward_last(self, partial_sum, values, grad_rows, gain, jobs, gain_grads):
+    def backward_last(self, partial_sum, values, grad_rows, gain, jobs):
         gain_grad, from_norm = norm_backward(values, gain, scatter_rows(partial_sum))
-        sums = jnp.concatenate([gain_grad, gain_grads], axis=0)
-        sums = lax.psum(lax.psum_scatter(sums, ("dp", "ctx"), scatter_dimension=1, tiled=True), "tensor")
-        return self.deliver(grad_rows + from_norm), sums, self.moves(*jobs)
+        return self.deliver(grad_rows + from_norm), gain_grad, self.moves(*jobs)
+
+    def sum_gains(self, gain_grads, jobs):
+        sums = lax.psum_scatter(gain_grads, ("dp", "ctx"), scatter_dimension=1, tiled=True)
+        return lax.psum(sums, "tensor"), self.moves(*jobs)
 
     def return_grads(self, full):
         return full
@@ -1549,6 +1547,32 @@
         sums_ref[tile, :units] = outer_rows(normed, gate_grad[...]).astype(jnp.bfloat16)
         sums_ref[tile, units : 2 * units] = outer_rows(normed, up_grad[...]).astype(jnp.bfloat16)
         sums_ref[tile, 2 * units :] = outer_rows(grad_ref[:, tile], activated_ref[...]).astype(jnp.bfloat16)
+
+
+def feed_both_kernel(
+    normed_ref, gate_ref, up_ref, down_ref, grad_ref, last_ref, partial_ref, sums_ref, gating, upward, activated, gate_grad, up_grad
+):
+    feed_kernel(normed_ref, gate_ref, up_ref, down_ref, last_ref, gating, upward, activated)
+    feed_back_kernel(
+        grad_ref, normed_ref, gate_ref, up_ref, down_ref, gating, upward, activated, partial_ref, sums_ref, gate_grad, up_grad
+    )
+
+
+def feed_both(normed, weights, down_grad):
+    rows, width = normed.shape
+    units = weights[0].shape[1]
+    sized = jax.ShapeDtypeStruct
+    partial_sum = sized((rows, width), jnp.bfloat16)
+    outs, _ = work_call(
+        feed_both_kernel,
+        "feed_both",
+        None,
+        [normed, *weights, down_grad],
+        [partial_sum, partial_sum, sized((width, 3 * units), jnp.bfloat16)],
+        [pltpu.VMEM((rows, units), jnp.float32)] * 2 + [pltpu.VMEM((rows, units), jnp.bfloat16)] * 3,
+        [],
+    )
+    return outs
 
 
 def backward_feed_beside(down_grad, weights, record, number, jobs):
@@ -1730,7 +1754,10 @@
             attention_weights[layer + 1] = joined(moved[0])
             gate, up, down = moved[1:]
         else:
-            last_sum, feed_records[layer] = forward_feed(normed, feed_weights[layer])
+            if kernels:
+                feed_records[layer] = (normed,)
+            else:
+                last_sum, feed_records[layer] = forward_feed(normed, feed_weights[layer])
             cotangent_whole = moved[0]
 
     grad_rows = comm.own_rows(cotangent_whole).astype(jnp.float32)
@@ -1740,7 +1767,6 @@
         more, last_layer = layer > 0, layer + 1 == LAYERS
         own_width = query_weight.shape[1]
         cut_feed, cut_attention = own_width * 5 // 9 // 16 * 16, own_width // 2 // 16 * 16
-        cut_last = own_width // 3 // 16 * 16
 
         def two(whole, cut):
             if last_layer:
@@ -1748,7 +1774,9 @@
             return [(exchange_rows(0, cut), whole)], [(exchange_rows(cut, own_width), whole)]
 
         beside, in_line = two(feed_parts[layer + 1] if not last_layer else None, cut_feed)
-        if kernels and beside:
+        if kernels and last_layer:
+            last_sum, partial_sum, sums = feed_both(feed_records[layer][0], feed_weights[layer], down_grad)
+        elif kernels:
             (partial_sum, sums), upper = backward_feed_beside(
                 down_grad, feed_weights[layer], feed_records[layer], comm.next_number(), beside
             )
@@ -1790,23 +1818,18 @@
                 partial_sum, starts_of[layer], grad_rows, front[layer], in_line
             )
         else:
-            others = jnp.concatenate(gain_fronts[1:] + gain_backs, axis=0)
-            grad_inputs, gain_sums, (feed_moved, *lower) = comm.backward_last(
-                partial_sum,
-                starts_of[layer],
-                grad_rows,
-                front[layer],
-                [(exchange_rows(0, cut_last), feed_sums)] + in_line,
-                others,
+            grad_inputs, gain_fronts[layer], lower = comm.backward_last(
+                partial_sum, starts_of[layer], grad_rows, front[layer], in_line
             )
         if beside:
             attention_parts[layer + 1] = [upper[0], lower[0]]
         feed_parts[layer], attention_parts[layer] = feed_sums, attention_sums
-    attention_parts[0], grad_inputs = lax.optimization_barrier((attention_parts[0], grad_inputs))
-    feed_rest, attention_moved = comm.moves(
-        (exchange_rows(cut_last, own_width), feed_parts[0]), (Exchange, attention_parts[0])
-    )
-    feed_parts[0], attention_parts[0] = [feed_moved, feed_rest], [attention_moved]
+    feed_parts[0], grad_inputs = lax.optimization_barrier((feed_parts[0], grad_inputs))
+    feed_parts[0] = comm.moves((Exchange, feed_parts[0]))
+    attention_parts[0], feed_parts[0] = lax.optimization_barrier((attention_parts[0], feed_parts[0]))
+    gain_sums, attention_parts[0] = comm.sum_gains(
+        jnp.concatenate(gain_fronts + gain_backs, axis=0), [(Exchange, attention_parts[0])]
+    )
     grad_inputs = grad_inputs.astype(jnp.float32)
 
     if kernels:

time: 871 us -> 864 us (level)
  Pallas kernels: 763 us -> 799 us
  local copies, waits for them, and re-layouts: 56.6 us -> 30.9 us
  matrix products: 16.6 us -> 0 us
    pallas_call x1 -> x2, Pallas kernels: 79.6 us -> 111 us  [jobs_call(): pl.pallas_call(functools.partial(jobs_kernel, [job[0] for job in jobs], c...]
    pallas_call x3 -> x4, Pallas kernels: 90.9 us -> 121 us  [work_call(): pl.pallas_call(functools.partial(work_kernel, kernel, len(operands), len(...]
    unnamed x163 -> x107, local copies, waits for them, and re-layouts: 54.2 us -> 28.5 us
    dot_general x6 -> x0, matrix products: 16.6 us -> none  [the longest x3 10.1 us: times_transposed(): lax.dot_general(left, right, (((1,), (1,)), ((), ())), preferred_element_...]
    pallas_call x7, Pallas kernels: 453 us -> 437 us  [line_call(): pl.pallas_call(functools.partial(line_kernel, (kernel, len(prelude_in), l...]
    pallas_call x1 -> x0, Pallas kernels: 9.71 us -> none  [outer_sums(): pl.pallas_call(outer_kernel, name='outer_sums', grid=(width // tile,), ou...]
  transfers between devices with their start and end apart: 4 -> 4, of which waited for: 0 -> 0; matrix products, arithmetic and copies ran while one was open for 1% -> 0% of each run, Pallas kernels for 37% -> 43%
where the time goes in v4:
time: 864 us; the launch traced here: 859 us
  Pallas kernels  799 us (92%)
  local copies, waits for them, and re-layouts  30.9 us (4%)
  between operations  14.6 us (2%)
  other arithmetic  13.9 us (2%)
    pallas_call x7, Pallas kernels, line_call(): pl.pallas_call(functools.partial(line_kernel, (kernel, len(prelude_in), l...  437 us
    pallas_call x1, Pallas kernels, start_call(): pl.pallas_call(functools.partial(start_kernel, plan), name='start', out_s...  121 us
    pallas_call x4, Pallas kernels, work_call(): pl.pallas_call(functools.partial(work_kernel, kernel, len(operands), len(...  121 us
    pallas_call x2, Pallas kernels, jobs_call(): pl.pallas_call(functools.partial(jobs_kernel, [job[0] for job in jobs], c...  111 us
    unnamed x107, local copies, waits for them, and re-layouts  28.5 us
  transfers between devices with their start and end apart: 4, of which 0 were waited for; matrix products, arithmetic and copies ran while one was open for 0% of the time, Pallas kernels for 43%

profile of v4, /device:TPU:0, one launch (start us, length us, event | category | flops | bytes accessed | tf_op | source)
XLA Modules:
  0.0 858.5 jit_solution(14755635640060554192)
XLA Ops:
  7.3 1.2 dynamic_slice.14
  8.5 1.9 fusion.10
  11.2 121.1 %start.1 = (bf16[4,144,1280]{2,1,0:T(8,128)(2,1)}, bf16[4,144,768]{2,1,0:T(8,128)(2,1)}, bf16[4,144,768]{2,1,0:T(8,128)(2,1)}, bf16[4,144,768]{2,1,0:T(8,128)(2,...) custom-call(bf16[2,144,1152]{2,1,0:T(8,128)(2,1)} %refs_0_.1, ...), custom_call_target="tpu_custom_call" | custom-call | flops 1000000000 | bytes 100000000 | tf_op jit(solution)/shard_map/start/pallas_call | solution.py:220
  135.3 1.5 dynamic-slice_convert_fusion.1.refs_6_.refs_1_
  137.4 83.6 %forward_line.3 = (bf16[512,1024]{1,0:T(8,128)(2,1)S(1)}, bf16[512,320]{1,0:T(8,128)(2,1)S(1)}, f32[512,128]{1,0:T(8,128)S(1)}, bf16[512,2304]{1,0:T(8,128)(2,1)...) custom-call(bf16[512,2304]{1,0:T(8,128)(2,1)} %get-tuple-element.92., ...), custom_call_target="tpu_custom_call" | custom-call | flops 1000000000 | bytes 100000000 | tf_op jit(solution)/shard_map/forward_line/pallas_call | solution.py:1045
  221.0 1.4 copy-done.39
  224.1 82.2 %forward_line.4 = (f32[512,768]{1,0:T(8,128)S(1)}, f32[512,768]{1,0:T(8,128)S(1)}, bf16[512,768]{1,0:T(8,128)(2,1)S(1)}, f32[128,2304]{1,0:T(8,128)S(1)}, bf16[5...) custom-call(bf16[512,2304]{1,0:T(8,128)(2,1)} %get-tuple-element.99., ...), custom_call_target="tpu_custom_call" | custom-call | flops 1000000000 | bytes 100000000 | tf_op jit(solution)/shard_map/forward_line/pallas_call | solution.py:1045
  306.4 1.4 copy-done.12
  309.0 62.3 %forward_line.5 = (bf16[512,1024]{1,0:T(8,128)(2,1)S(1)}, bf16[512,320]{1,0:T(8,128)(2,1)S(1)}, f32[512,128]{1,0:T(8,128)S(1)}, f32[128,2304]{1,0:T(8,128)S(1)},...) custom-call(bf16[512,2304]{1,0:T(8,128)(2,1)} %copy-done.12, ...), custom_call_target="tpu_custom_call" | custom-call | flops 1000000000 | bytes 100000000 | tf_op jit(solution)/shard_map/forward_line/pallas_call | solution.py:1045
  371.3 1.4 copy-done.41
  374.2 2.1 multiply_convert_fusion.refs_4_
  377.0 28.0 %feed_both.1 = (bf16[512,2304]{1,0:T(8,128)(2,1)}, bf16[512,2304]{1,0:T(8,128)(2,1)}, bf16[2304,2304]{1,0:T(8,128)(2,1)}) custom-call(bf16[512,2304]{1,0:T(8,128)(2,1)} %copy-done.41, bf16[2304,768]{1,0:T(8,128)(2,1)} %bitcast.38, bf16[2304,768]{1,0:T(8,128)(2,1)} %bitcast.39, bf16[2304,768]{1,0:T(8,128)(2,1)} %bitcast.40, ...), custom_call_target="tpu_custom_call" | custom-call | flops 10000000000 | bytes 50000000 | tf_op jit(solution)/shard_map/feed_both/pallas_call | solution.py:1106
  405.1 2.2 dynamic-slice_convert_fusion.refs_2_
  407.3 46.1 %backward_line.3 = (f32[1,2304]{1,0:T(1,128)}, f32[128,2304]{1,0:T(8,128)}, bf16[512,2304]{1,0:T(8,128)(2,1)}) custom-call(bf16[512,2304]{1,0:T(8,128)(2,1)} %get-tuple-element.120.refs_0_, f32[128,2304]{1,0:T(8,128)} %copy-done.3, f32[128,2304]{1,0:T(8,128)} %dynamic-slice_convert_fusion.refs_2_, f32[1,2304]{1,0:T(1,128)} %copy-done.36), custom_call_target="tpu_custom_call" | custom-call | flops 1000000000 | bytes 100000000 | tf_op jit(solution)/shard_map/backward_line/pallas_call | solution.py:1045
  453.4 22.0 %attend_back.2 = (bf16[512,2304]{1,0:T(8,128)(2,1)}, bf16[2304,1280]{1,0:T(8,128)(2,1)}) custom-call(bf16[512,2304]{1,0:T(8,128)(2,1)} %get-tuple-element.122.refs_0_, bf16[2304,1280]{1,0:T(8,128)(2,1)} %bitcast.26, bf16[512,1024]{1,0:T(8,128)(2,1)} %copy-done.45, f32[512,128]{1,0:T(8,128)} %copy-done.50, f32[512,128]{1,0:T(8,128)} %copy-done.7, ...), custom_call_target="tpu_custom_call" | custom-call | flops 10000000000 | bytes 50000000 | tf_op jit(solution)/shard_map/attend_back/pallas_call | solution.py:1106
  475.6 44.1 %backward_line.4 = (f32[1,2304]{1,0:T(1,128)}, f32[128,2304]{1,0:T(8,128)}, bf16[512,2304]{1,0:T(8,128)(2,1)}) custom-call(bf16[512,2304]{1,0:T(8,128)(2,1)} %get-tuple-element.126.refs_0_, f32[128,2304]{1,0:T(8,128)} %copy-done.5, f32[128,2304]{1,0:T(8,128)} %get-tuple-element.127.refs_2_, f32[1,2304]{1,0:T(1,128)} %copy-done.35), custom_call_target="tpu_custom_call" | custom-call | flops 1000000000 | bytes 100000000 | tf_op jit(solution)/shard_map/backward_line/pallas_call | solution.py:1045
  519.7 41.9 %feed_back.1 = (bf16[512,2304]{1,0:T(8,128)(2,1)}, bf16[2304,2304]{1,0:T(8,128)(2,1)}, bf16[4,80,2304]{2,1,0:T(8,128)(2,1)}) custom-call(bf16[512,2304]{1,0:T(8,128)(2,1)} %get-tuple-element.128.refs_0_, bf16[512,2304]{1,0:T(8,128)(2,1)} %get-tuple-element.99.refs_0_.refs_1_, bf16[2304,768]{1,0:T(8,128)(2,1)} %bitcast.28, bf16[2304,768]{1,0:T(8,128)(2,1)} %bitcast.30, ...), custom_call_target="tpu_custom_call" | custom-call | flops 10000000000 | bytes 50000000 | tf_op jit(solution)/shard_map/feed_back/pallas_call | solution.py:1106
  561.7 1.2 copy-done.17
  562.9 1.3 copy-done.4
  564.1 1.7 copy-done.9
  565.8 1.7 copy-done.10
  567.5 77.6 %backward_line.5 = (f32[1,2304]{1,0:T(1,128)S(1)}, f32[128,2304]{1,0:T(8,128)S(1)}, bf16[512,2304]{1,0:T(8,128)(2,1)S(1)}, bf16[128,2304]{1,0:T(8,128)(2,1)S(1)}, bf16[4,64,2304]{2,1,0:T(8,128)(2,1)S(1)}) custom-call(bf16[512,2304]{1,0:T(8,128)(2,1)S(1)} %copy-done.10, f32[128,2304]{1,0:T(8,128)S(1)} %get-tuple-element.103.refs_4_.refs_1_, ...), custom_call_target="tpu_custom_call" | custom-call | flops 1000000000 | bytes 100000000 | tf_op jit(solution)/shard_map/backward_line/pallas_call | solution.py:1045
  648.5 1.4 copy-done.40
  649.9 29.2 %attend_back.3 = (bf16[512,2304]{1,0:T(8,128)(2,1)}, bf16[2304,1280]{1,0:T(8,128)(2,1)}, bf16[4,64,1280]{2,1,0:T(8,128)(2,1)}) custom-call(bf16[512,2304]{1,0:T(8,128)(2,1)} %copy-done.40, bf16[2304,1280]{1,0:T(8,128)(2,1)} %bitcast.24, bf16[512,1024]{1,0:T(8,128)(2,1)} %copy-done.44, f32[512,128]{1,0:T(8,128)} %copy-done.49, f32[512,128]{1,0:T(8,128)} %copy-done.7, ...), custom_call_target="tpu_custom_call" | custom-call | flops 10000000000 | bytes 50000000 | tf_op jit(solution)/shard_map/attend_back/pallas_call | solution.py:1106
  679.2 1.2 copy-done.19
  680.5 1.7 copy-done.11
  682.1 1.4 copy-done.13
  683.5 41.2 %backward_last_line.1 = (f32[1,2304]{1,0:T(1,128)S(1)}, bf16[128,2304]{1,0:T(8,128)(2,1)S(1)}, bf16[4,80,1280]{2,1,0:T(8,128)(2,1)S(1)}) custom-call(bf16[512,2304]{1,0:T(8,128)(2,1)S(1)} %copy-done.11, f32[128,2304]{1,0:T(8,128)S(1)} %dynamic-slice_convert_fusion.1.refs_6_.refs_1_, f32[128,2304]{1,0:T(8,128)S(1)} %copy-done.19, f32[1,2304]{1,0:T(1,128)S(1)} %copy-done.34, ...), custom_call_target="tpu_custom_call" | custom-call | flops 1000000000 | bytes 100000000 | tf_op jit(solution)/shard_map/backward_last_line/pallas_call | solution.py:1045
  727.3 68.8 %moves.2.refs_3_ = bf16[4,144,2304]{2,1,0:T(8,128)(2,1)} custom-call(bf16[4,144,2304]{2,1,0:T(8,128)(2,1)} %bitcast.33), custom_call_target="tpu_custom_call" | custom-call | flops 1000000000 | bytes 100000000 | tf_op jit(solution)/shard_map/moves/pallas_call | solution.py:715
  796.2 41.8 %moves.3 = (f32[16,8,256]{2,1,0:T(8,128)}, bf16[4,144,1280]{2,1,0:T(8,128)(2,1)}) custom-call(f32[4,2304]{1,0:T(4,128)} %pad_maximum_fusion.2.refs_0_, bf16[4,144,1280]{2,1,0:T(8,128)(2,1)} %bitcast.42), custom_call_target="tpu_custom_call" | custom-call | flops 1000000000 | bytes 100000000 | tf_op jit(solution)/shard_map/moves/pallas_call | solution.py:715
  839.6 1.4 copy-done.16
  842.0 8.9 %join_layers.1 = (f32[2,144,1152]{2,1,0:T(8,128)}, f32[2,144,1152]{2,1,0:T(8,128)}, f32[2,144,1152]{2,1,0:T(8,128)}, f32[2,144,1152]{2,1,0:T(8,128)}, f32[2,144,...) custom-call(bf16[4,144,1280]{2,1,0:T(8,128)(2,1)S(1)} %copy-done.16, ...), custom_call_target="tpu_custom_call" | custom-call | bytes 20000000 | tf_op jit(solution)/shard_map/join_layers/pallas_call | solution.py:1389
  (126 shorter events, 19.2 us)
Async XLA Ops:
  7.2 512.5 %reduce-scatter.5.cloned.1.call-start = ((), (), s32[]{:S(2)}) async-start(), calls=%async_computation.4 | async-start | bytes 13271040 | tf_op jit(solution)/shard_map/reduce_scatter | solution.py:269
  133.5 175.5 %copy-start.36 = (f32[1,2304]{1,0:T(1,128)}, f32[1,2304]{1,0:T(1,128)S(1)}, u32[]{:S(2)}) copy-start(f32[1,2304]{1,0:T(1,128)S(1)} %slice.44.refs_6_.refs_3_) | copy-start | bytes 27652
  133.6 90.5 %copy-start.35 = (f32[1,2304]{1,0:T(1,128)}, f32[1,2304]{1,0:T(1,128)S(1)}, u32[]{:S(2)}) copy-start(f32[1,2304]{1,0:T(1,128)S(1)} %slice.42.refs_5_.refs_3_) | copy-start | bytes 27652
  133.8 3.5 copy-start.33
  133.8 3.5 copy-start.15
  133.8 3.5 copy-start.24
  133.8 3.5 copy-start.25
  133.8 3.5 copy-start.26
  135.3 173.7 %copy-start.2 = (f32[512,512]{1,0:T(8,128)}, f32[512,512]{1,0:T(8,128)S(1)}, u32[]{:S(2)}) copy-start(f32[512,512]{1,0:T(8,128)S(1)} %or_select_fusion.refs_5_.refs_4_.refs_6_) | copy-start | bytes 3145732
  137.3 171.7 %copy-start.7 = (f32[512,128]{1,0:T(8,128)}, f32[512,128]{1,0:T(8,128)S(1)}, u32[]{:S(2)}) copy-start(f32[512,128]{1,0:T(8,128)S(1)} %get-tuple-element.186.refs_3_.refs_2_.refs_4_) | copy-start | bytes 786436
  137.3 171.7 %copy-start.8 = (f32[512,128]{1,0:T(8,128)}, f32[512,128]{1,0:T(8,128)S(1)}, u32[]{:S(2)}) copy-start(f32[512,128]{1,0:T(8,128)S(1)} %get-tuple-element.187.refs_4_.refs_3_.refs_5_) | copy-start | bytes 786436
  137.4 86.7 %copy-start.22 = (bf16[4,144,768]{2,1,0:T(8,128)(2,1)S(1)}, bf16[4,144,768]{2,1,0:T(8,128)(2,1)}, u32[]{:S(2)}) copy-start(bf16[4,144,768]{2,1,0:T(8,128)(2,1)} %get-tuple-element.106.refs_8_) | copy-start | bytes 2654212
  137.4 86.7 %copy-start.23 = (bf16[4,144,768]{2,1,0:T(8,128)(2,1)S(1)}, bf16[4,144,768]{2,1,0:T(8,128)(2,1)}, u32[]{:S(2)}) copy-start(bf16[4,144,768]{2,1,0:T(8,128)(2,1)} %get-tuple-element.107.refs_9_) | copy-start | bytes 2654212
  224.1 82.3 %copy-start.47 = (bf16[512,320]{1,0:T(8,128)(2,1)}, bf16[512,320]{1,0:T(8,128)(2,1)S(1)}, u32[]{:S(2)}) copy-start(bf16[512,320]{1,0:T(8,128)(2,1)S(1)} %get-tuple-element.144.refs_8_) | copy-start | bytes 983044
  224.1 84.9 %copy-start.30 = (bf16[128,2304]{1,0:T(8,128)(2,1)S(1)}, bf16[128,2304]{1,0:T(8,128)(2,1)}, u32[]{:S(2)}) copy-start(bf16[128,2304]{1,0:T(8,128)(2,1)} %refs_9_.3) | copy-start | bytes 1769476
  309.0 62.3 %copy-start.5 = (f32[128,2304]{1,0:T(8,128)}, f32[128,2304]{1,0:T(8,128)S(1)}, u32[]{:S(2)}) copy-start(f32[128,2304]{1,0:T(8,128)S(1)} %get-tuple-element.110.refs_5_.refs_1_) | copy-start | bytes 3538948
  309.0 62.3 %copy-start.43 = (f32[512,768]{1,0:T(8,128)}, f32[512,768]{1,0:T(8,128)S(1)}, u32[]{:S(2)}) copy-start(f32[512,768]{1,0:T(8,128)S(1)} %get-tuple-element.130.refs_6_) | copy-start | bytes 4718596
  309.0 62.3 %copy-start.46 = (bf16[512,768]{1,0:T(8,128)(2,1)}, bf16[512,768]{1,0:T(8,128)(2,1)S(1)}, u32[]{:S(2)}) copy-start(bf16[512,768]{1,0:T(8,128)(2,1)S(1)} %get-tuple-element.131.refs_7_) | copy-start | bytes 2359300
  374.2 2.1 copy-start.3
  374.2 2.5 copy-start.6
  374.2 2.8 copy-start.45
  405.1 244.8 %reduce-scatter.9.cloned.1.call-start = ((), (), s32[]{:S(2)}) async-start(), calls=%async_computation.6 | async-start | bytes 7372800 | tf_op jit(solution)/shard_map/reduce_scatter | solution.py:269
  475.4 250.9 %reduce-scatter.7.cloned.1.call-start = ((), (), s32[]{:S(2)}) async-start(), calls=%async_computation.5 | async-start | bytes 13271040 | tf_op jit(solution)/shard_map/reduce_scatter | solution.py:269
  561.6 234.6 %reduce-scatter.11.cloned.1.call-start = ((), (), s32[]{:S(2)}) async-start(), calls=%async_computation.7 | async-start | bytes 7372800 | tf_op jit(solution)/shard_map/reduce_scatter | solution.py:269
  683.5 42.1 %copy-start.38 = (f32[1,2304]{1,0:T(1,128)S(1)}, f32[1,2304]{1,0:T(1,128)}, u32[]{:S(2)}) copy-start(f32[1,2304]{1,0:T(1,128)} %copy-done.37) | copy-start | bytes 27652
  683.5 42.1 %copy-start.51 = (f32[1,2304]{1,0:T(1,128)S(1)}, f32[1,2304]{1,0:T(1,128)}, u32[]{:S(2)}) copy-start(f32[1,2304]{1,0:T(1,128)} %get-tuple-element.155) | copy-start | bytes 27652
  683.5 42.1 %copy-start.52 = (f32[1,2304]{1,0:T(1,128)S(1)}, f32[1,2304]{1,0:T(1,128)}, u32[]{:S(2)}) copy-start(f32[1,2304]{1,0:T(1,128)} %get-tuple-element.153) | copy-start | bytes 27652
  796.2 43.4 %copy-start.14 = (bf16[4,80,2304]{2,1,0:T(8,128)(2,1)S(1)}, bf16[4,80,2304]{2,1,0:T(8,128)(2,1)}, u32[]{:S(2)}) copy-start(bf16[4,80,2304]{2,1,0:T(8,128)(2,1)} %get-tuple-element.164.refs_4_) | copy-start | bytes 4423684
  796.2 43.4 %copy-start.21 = (bf16[4,64,2304]{2,1,0:T(8,128)(2,1)S(1)}, bf16[4,64,2304]{2,1,0:T(8,128)(2,1)}, u32[]{:S(2)}) copy-start(bf16[4,64,2304]{2,1,0:T(8,128)(2,1)} %copy-done.20) | copy-start | bytes 3538948
  796.2 43.4 %copy-start.28 = (bf16[4,80,1280]{2,1,0:T(8,128)(2,1)S(1)}, bf16[4,80,1280]{2,1,0:T(8,128)(2,1)}, u32[]{:S(2)}) copy-start(bf16[4,80,1280]{2,1,0:T(8,128)(2,1)} %copy-done.27) | copy-start | bytes 2457604
  842.0 8.9 %copy-start.32 = (bf16[128,2304]{1,0:T(8,128)(2,1)S(1)}, bf16[128,2304]{1,0:T(8,128)(2,1)}, u32[]{:S(2)}) copy-start(bf16[128,2304]{1,0:T(8,128)(2,1)} %copy-done.31) | copy-start | bytes 1769476
  842.0 9.7 %copy-start.1 = (s32[4,8]{1,0:T(4,128)S(1)}, s32[4,8]{1,0:T(4,128)}, u32[]{:S(2)}) copy-start(s32[4,8]{1,0:T(4,128)} %param.18) | copy-start | bytes 388
  (25 other events, 29.6 us)
Sparse Core Ops, SparseCore 0:
  405.2 104.3 reduce-scatter.4
  512.6 66.8 reduce-scatter.8
  582.7 104.5 reduce-scatter.6
  690.2 66.8 reduce-scatter.10
